TPU v7x, 128 devices: a whole 4x4x4 slice. The times are simulated.
128 devices in a mesh: pipe: 8 (over y_lo, z), expert: 16 (over x, y_hi, core).
Axes of the slice: x: 4, y: 4 (y_hi: 2, y_lo: 2; y = y_hi * 2 + y_lo), z: 4, core: 2. Of those that a mesh axis runs over, the one named last changes fastest.
Arguments:
- out_grad: bfloat16 [8, 2, 1024, 3584], P('pipe', None, 'expert'), may hold values from -6 to 6
- saved_input: bfloat16 [8, 2, 1024, 3584], P('pipe', None, 'expert'), may hold values from -6 to 6
- saved_hidden: bfloat16 [8, 2, 1024, 8, 1024], P('pipe', None, 'expert'), may hold values from -0.29882812 to 0.29882812
- expert_ids: int32 [8, 2, 1024, 8], P('pipe', None, 'expert'), may hold values from 0 to 15, all different within a row; in each aligned block of 64 rows (0 to 63, 64 to 127, ..., all dimensions but the last counted through in order) at most 56 rows name the same one
- down_weight: bfloat16 [8, 2, 16, 1024, 3584], P('pipe', None, 'expert'), may hold values from -0.1875 to 0.1875
- router_weight: bfloat16 [8, 2, 16, 3584], P('pipe'), may hold values from -0.09375 to 0.09375
Outputs:
- hidden_grad: bfloat16 [8, 2, 1024, 8, 1024], P('pipe', None, 'expert')
- router_grad: float32 [8, 2, 16, 3584], P('pipe')
Inputs may be any that keep to these rules, and one draw needn't show every extreme that they name: `expert_ids`: each token names 8 different experts. Among the 64 tokens of one device in one slot, no expert is named by more than 56, and in some of these blocks one is named by exactly 56.
All inputs are finite; a program needn't handle non-finite values.
Results may differ from a plain program's by a relative error of at most 0.005.
Values may be sent and summed in bfloat16 or wider, within the bound.
No kernel may reach another device: no remote copies, remote signals or barrier semaphores. Data moves between devices by JAX's collectives and lax.ppermute only.
A program may use at most 128 MiB of HBM per device.

v0:
```python
import jax
import jax.numpy as jnp
from jax import lax
from jax.sharding import PartitionSpec as P

CAP = 56


route_scale = 2.5


def partner(block, axis, bit):
    count = lax.axis_size(axis)
    route = []
    for low in range(count):
        high = low | 1 << bit
        if high != low and high < count:
            route += [(low, high), (high, low)]
    return lax.ppermute(block, axis, route)


def token_math(back, hidden, inputs, router, member):
    dgate = jnp.sum(hidden.astype(jnp.float32) * back.astype(jnp.float32), axis=2)
    logits = jnp.einsum("td,ed->te", inputs, router, preferred_element_type=jnp.float32)
    probs = jax.nn.sigmoid(logits)
    chosen = jnp.sum(jnp.where(member, probs[:, None, :], 0.0), axis=2)
    total = jnp.sum(chosen, axis=1, keepdims=True)
    weights = route_scale * chosen / total
    hidden_grad = (weights[:, :, None] * back.astype(jnp.float32)).astype(jnp.bfloat16)
    centred = dgate - jnp.sum(chosen / total * dgate, axis=1, keepdims=True)
    selected = route_scale / total * centred * chosen * (1.0 - chosen)
    logit_grad = jnp.sum(jnp.where(member, selected[:, :, None], 0.0), axis=1)
    partial_value = jnp.dot(
        logit_grad.T, inputs.astype(jnp.float32), precision=lax.Precision.HIGHEST
    )
    return (hidden_grad, partial_value)


def local(out_grad, saved_input, saved_hidden, expert_ids, down_weight, router_weight):
    peers = lax.axis_size("expert")
    tok_count = out_grad.shape[2]
    tok_iota = jnp.arange(tok_count, dtype=jnp.int32)
    earlier = (tok_iota[:, None] > tok_iota[None, :]).astype(jnp.float32)
    slot_iota = jnp.arange(CAP, dtype=jnp.float32)
    grads_list = []
    partial_list = []
    for slot_index in range(2):
        grads = out_grad[0, slot_index]
        routes = expert_ids[0, slot_index]
        weights_down = down_weight[0, slot_index, 0]
        member = routes[:, :, None] == jnp.arange(peers, dtype=jnp.int32)[None, None, :]
        onehot = jnp.any(member, axis=1).astype(jnp.float32)
        before = jnp.dot(earlier, onehot, precision=lax.Precision.HIGHEST)
        position = jnp.sum(jnp.where(member, before[:, None, :], 0.0), axis=2)
        pick = jnp.logical_and(
            member[:, :, :, None], position[:, :, None, None] == slot_iota[None, None, None, :]
        )
        place = jnp.any(pick, axis=1).astype(jnp.bfloat16)
        send = jnp.einsum("tec,td->ecd", place, grads, preferred_element_type=jnp.float32).astype(
            jnp.bfloat16
        )
        proj = jnp.einsum(
            "srd,hd->srh",
            lax.all_to_all(send, "expert", split_axis=0, concat_axis=0, tiled=True),
            weights_down,
            preferred_element_type=jnp.float32,
        ).astype(jnp.bfloat16)
        returned = lax.all_to_all(proj, "expert", split_axis=0, concat_axis=0, tiled=True)
        back = jnp.einsum(
            "tkec,ech->tkh", pick.astype(jnp.bfloat16), returned, preferred_element_type=jnp.float32
        ).astype(jnp.bfloat16)
        hidden_grad, partial_value = token_math(
            back,
            saved_hidden[0, slot_index],
            saved_input[0, slot_index],
            router_weight[0, slot_index],
            member,
        )
        grads_list.append(hidden_grad)
        partial_list.append(partial_value)
    stacked = jnp.stack(partial_list)
    summed = lax.psum(stacked, "expert")
    mirrored = summed
    for bit_number in range(lax.axis_size("pipe").bit_length() - 1):
        mirrored = partner(mirrored.astype(jnp.bfloat16), "pipe", bit_number).astype(mirrored.dtype)
    result = summed + mirrored[::-1]
    return (jnp.stack(grads_list)[None], result[None])


def solution(mesh):
    in_specs = (
        P("pipe", None, "expert", None),
        P("pipe", None, "expert", None),
        P("pipe", None, "expert", None, None),
        P("pipe", None, "expert", None),
        P("pipe", None, "expert", None, None),
        P("pipe", None, None, None),
    )
    out_specs = (P("pipe", None, "expert", None, None), P("pipe", None, None, None))
    return jax.shard_map(local, mesh=mesh, in_specs=in_specs, out_specs=out_specs, check_vma=False)
```

profile of v0, /device:TPU:1, one launch (start us, length us, event | category | flops | bytes accessed | tf_op | source)
XLA Modules:
  0.0 470.3 jit_solution(8704448471986983932)
XLA Ops:
  8.0 1.2 iota_compare_fusion
  9.3 1.3 fusion.36
  10.6 1.2 select_reduce_fusion
  12.0 1.7 and_reduce_fusion
  13.8 5.6 %convolution_convert_fusion = bf16[16,56,3584]{2,1,0:T(8,128)(2,1)} fusion(pred[64,16,56]{2,1,0:T(8,128)(4,1)S(1)} %and_reduce_fusion, bf16[1,2,64,3584]{3,2,1,0:T(8,128)(2,1)} %param.6), kind=kOutput, calls=%fused_computation.6 | convolution fusion | flops 414253056 | bytes 6938624 | tf_op jit(solution)/shard_map/tec,td->ecd/dot_general | solution.py:59
  19.4 8.6 %all-to-all-start.2 = ((bf16[16,56,3584]{2,1,0:T(8,128)(2,1)}), bf16[16,56,3584]{2,1,0:T(8,128)(2,1)}, u32[]{:S(2)}, u32[]{:S(2)}) async-start(bf16[16,56,3584]{2,1,0:T(8,128)(2,1)} %convolution_convert_fusion), calls=%async_computation.2 | async-start | bytes 12845056 | tf_op jit(solution)/shard_map/all_to_all | solution.py:64
  28.3 1.2 iota_compare_fusion.1
  29.7 1.2 select_reduce_fusion.2
  31.1 1.7 and_reduce_fusion.1
  32.8 4.5 convolution_convert_fusion.1
  37.3 84.7 %all-to-all-done.2 = bf16[16,56,3584]{2,1,0:T(8,128)(2,1)} async-done(((bf16[16,56,3584]{2,1,0:T(8,128)(2,1)}), bf16[16,56,3584]{2,1,0:T(8,128)(2,1)}, u32[]{:S(2)}, u32[]{:S(2)}) %all-to-all-start.2) | async-done | bytes 6422560 | tf_op jit(solution)/shard_map/all_to_all | solution.py:64
  122.0 12.4 %all-to-all-start = ((bf16[16,56,3584]{2,1,0:T(8,128)(2,1)}), bf16[16,56,3584]{2,1,0:T(8,128)(2,1)}, u32[]{:S(2)}, u32[]{:S(2)}) async-start(bf16[16,56,3584]{2,1,0:T(8,128)(2,1)} %convolution_convert_fusion.1), calls=%async_computation | async-start | bytes 12845056 | tf_op jit(solution)/shard_map/all_to_all | solution.py:64
  134.4 12.1 %fusion.23 = bf16[16,56,1024]{2,1,0:T(8,128)(2,1)} fusion(bf16[16,56,3584]{2,1,0:T(8,128)(2,1)} %all-to-all-done.2, bf16[1,2,1,1024,3584]{4,3,2,1,0:T(8,128)(2,1)} %param.10), kind=kOutput, calls=%fused_computation.34 | convolution fusion | flops 6577586176 | bytes 15597568 | tf_op jit(solution)/shard_map/srd,hd->srh/dot_general | solution.py:62
  146.5 82.0 %all-to-all-done = bf16[16,56,3584]{2,1,0:T(8,128)(2,1)} async-done(((bf16[16,56,3584]{2,1,0:T(8,128)(2,1)}), bf16[16,56,3584]{2,1,0:T(8,128)(2,1)}, u32[]{:S(2)}, u32[]{:S(2)}) %all-to-all-start) | async-done | bytes 6422560 | tf_op jit(solution)/shard_map/all_to_all | solution.py:64
  228.5 12.5 %all-to-all-start.3 = ((bf16[16,56,1024]{2,1,0:T(8,128)(2,1)}), bf16[16,56,1024]{2,1,0:T(8,128)(2,1)S(1)}, u32[]{:S(2)}, u32[]{:S(2)}) async-start(bf16[16,56,1024]{2,1,0:T(8,128)(2,1)} %fusion.23), calls=%async_computation.3 | async-start | bytes 3670016 | tf_op jit(solution)/shard_map/all_to_all | solution.py:68
  240.9 12.1 %fusion.20 = bf16[16,56,1024]{2,1,0:T(8,128)(2,1)} fusion(bf16[16,56,3584]{2,1,0:T(8,128)(2,1)} %all-to-all-done, bf16[1,2,1,1024,3584]{4,3,2,1,0:T(8,128)(2,1)} %param.10), kind=kOutput, calls=%fused_computation.33 | convolution fusion | flops 6577586176 | bytes 15597568 | tf_op jit(solution)/shard_map/srd,hd->srh/dot_general | solution.py:62
  253.0 13.5 %all-to-all-done.3 = bf16[16,56,1024]{2,1,0:T(8,128)(2,1)S(1)} async-done(((bf16[16,56,1024]{2,1,0:T(8,128)(2,1)}), bf16[16,56,1024]{2,1,0:T(8,128)(2,1)S(1)}, u32[]{:S(2)}, u32[]{:S(2)}) %all-to-all-start.3) | async-done | bytes 1835040 | tf_op jit(solution)/shard_map/all_to_all | solution.py:68
  266.6 1.2 copy-done
  267.8 5.2 %all-to-all-start.1 = ((bf16[16,56,1024]{2,1,0:T(8,128)(2,1)}), bf16[16,56,1024]{2,1,0:T(8,128)(2,1)S(1)}, u32[]{:S(2)}, u32[]{:S(2)}) async-start(bf16[16,56,1024]{2,1,0:T(8,128)(2,1)} %fusion.20), calls=%async_computation.1 | async-start | bytes 3670016 | tf_op jit(solution)/shard_map/all_to_all | solution.py:68
  273.3 5.2 %bitcast_convert_fusion = bf16[64,8,1024]{2,1,0:T(8,128)(2,1)} fusion(bf16[16,56,1024]{2,1,0:T(8,128)(2,1)} %copy-done, pred[64,8,56]{2,1,0:T(8,128)(4,1)S(1)} %iota_compare_fusion.2, pred[64,8,16]{1,2,0:T(8,128)(4,1)S(1)} %get-tuple-element.14), kind=kOutput, calls=%fused_computation.25 | convolution fusion | flops 940507136 | bytes 2920448 | tf_op jit(solution)/shard_map/tkec,ech->tkh/dot_general | solution.py:69
  278.5 20.1 %all-to-all-done.1 = bf16[16,56,1024]{2,1,0:T(8,128)(2,1)S(1)} async-done(((bf16[16,56,1024]{2,1,0:T(8,128)(2,1)}), bf16[16,56,1024]{2,1,0:T(8,128)(2,1)S(1)}, u32[]{:S(2)}, u32[]{:S(2)}) %all-to-all-start.1) | async-done | bytes 1835040 | tf_op jit(solution)/shard_map/all_to_all | solution.py:68
  298.6 5.9 %fusion.11 = (f32[64,8]{1,0:T(8,128)S(1)}, f32[64,8]{1,0:T(8,128)S(1)}, bf16[1,64,8,1024]{3,2,1,0:T(8,128)(2,1)S(1)}, bf16[1,64,8,1024]{3,2,1,0:T(8,128)(2,1)}) fusion(bf16[1,2,64,8,1024]{4,3,2,1,0:T(8,128)(2,1)} %param.8, bf16[64,8,1024]{2,1,0:T(8,128)(2,1)} %bitcast_convert_fusion, f32[64,8]{1,0:T(8,128)S(1)} %multiply_divide_fusion, ...), kind=kOutput, calls=%fused_computation.21 | convolution fusion | flops 946797568 | bytes 7122944 | tf_op jit(solution)/shard_map/tkec,ech->tkh/dot_general | solution.py:69
  305.2 1.4 convolution_bitcast_fusion.1
  306.9 1.4 convolution_bitcast_fusion
  309.1 135.0 %all-reduce.2.cloned.1.call-done = f32[2,16,3584]{2,1,0:T(8,128)} async-done(((f32[2,16,3584]{2,1,0:T(8,128)}), f32[2,16,3584]{2,1,0:T(8,128)}) %all-reduce.2.cloned.1.call-update) | async-done | bytes 458768 | tf_op jit(solution)/shard_map/psum | solution.py:82
  445.2 1.4 collective-permute-start
  446.5 3.6 collective-permute-done
  450.1 2.9 collective-permute-start.1
  453.0 4.7 collective-permute-done.1
  457.7 1.2 collective-permute-start.2
  458.9 1.5 maximum_bitcast_fusion
  460.4 2.1 collective-permute-done.2
  (42 shorter events, 5.9 us)
Async XLA Ops:
  19.3 8.7 %copy-start.3 = (bf16[1,2,64,3584]{3,2,1,0:T(8,128)(2,1)S(1)}, bf16[1,2,64,3584]{3,2,1,0:T(8,128)(2,1)}, u32[]{:S(2)}) copy-start(bf16[1,2,64,3584]{3,2,1,0:T(8,128)(2,1)} %param.7) | copy-start | bytes 2752516
  19.4 8.7 %copy-start.5 = (bf16[1,2,16,3584]{3,2,1,0:T(8,128)(2,1)S(1)}, bf16[1,2,16,3584]{3,2,1,0:T(8,128)(2,1)}, u32[]{:S(2)}) copy-start(bf16[1,2,16,3584]{3,2,1,0:T(8,128)(2,1)} %param.11) | copy-start | bytes 688132
  19.4 13.4 %copy-start.4 = (bf16[1,2,64,3584]{3,2,1,0:T(8,128)(2,1)S(1)}, bf16[1,2,64,3584]{3,2,1,0:T(8,128)(2,1)}, u32[]{:S(2)}) copy-start(bf16[1,2,64,3584]{3,2,1,0:T(8,128)(2,1)} %param.6) | copy-start | bytes 2752516
  19.4 102.6 %all-to-all-start.2 = ((bf16[16,56,3584]{2,1,0:T(8,128)(2,1)}), bf16[16,56,3584]{2,1,0:T(8,128)(2,1)}, u32[]{:S(2)}, u32[]{:S(2)}) async-start(bf16[16,56,3584]{2,1,0:T(8,128)(2,1)} %convolution_convert_fusion), calls=%async_computation.2 | async-start | bytes 12845056 | tf_op jit(solution)/shard_map/all_to_all | solution.py:64
  122.0 106.5 %all-to-all-start = ((bf16[16,56,3584]{2,1,0:T(8,128)(2,1)}), bf16[16,56,3584]{2,1,0:T(8,128)(2,1)}, u32[]{:S(2)}, u32[]{:S(2)}) async-start(bf16[16,56,3584]{2,1,0:T(8,128)(2,1)} %convolution_convert_fusion.1), calls=%async_computation | async-start | bytes 12845056 | tf_op jit(solution)/shard_map/all_to_all | solution.py:64
  228.5 38.1 %all-to-all-start.3 = ((bf16[16,56,1024]{2,1,0:T(8,128)(2,1)}), bf16[16,56,1024]{2,1,0:T(8,128)(2,1)S(1)}, u32[]{:S(2)}, u32[]{:S(2)}) async-start(bf16[16,56,1024]{2,1,0:T(8,128)(2,1)} %fusion.23), calls=%async_computation.3 | async-start | bytes 3670016 | tf_op jit(solution)/shard_map/all_to_all | solution.py:68
  266.6 1.2 copy-start
  267.8 30.8 %all-to-all-start.1 = ((bf16[16,56,1024]{2,1,0:T(8,128)(2,1)}), bf16[16,56,1024]{2,1,0:T(8,128)(2,1)S(1)}, u32[]{:S(2)}, u32[]{:S(2)}) async-start(bf16[16,56,1024]{2,1,0:T(8,128)(2,1)} %fusion.20), calls=%async_computation.1 | async-start | bytes 3670016 | tf_op jit(solution)/shard_map/all_to_all | solution.py:68
  273.0 171.1 %all-reduce.2.cloned.1.call-start = ((), (), s32[]{:S(2)}) async-start(), calls=%async_computation.4 | async-start | bytes 917504 | tf_op jit(solution)/shard_map/psum | solution.py:82
  304.5 154.4 %copy-start.2 = (bf16[1,64,8,1024]{3,2,1,0:T(8,128)(2,1)S(1)}, bf16[1,64,8,1024]{3,2,1,0:T(8,128)(2,1)}, u32[]{:S(2)}) copy-start(bf16[1,64,8,1024]{3,2,1,0:T(8,128)(2,1)} %get-tuple-element.11) | copy-start | bytes 3145732
  445.2 5.0 %collective-permute-start = (bf16[2,16,3584]{2,1,0:T(8,128)(2,1)S(1)}, bf16[2,16,3584]{2,1,0:T(8,128)(2,1)S(1)}, u32[]{:S(2)}, u32[]{:S(2)}) collective-permute-start(bf16[2,16,3584]{2,1,0:T(8,128)(2,1)S(1)} %convert_element_type.77), channel_id=1, source_target_pairs={{0,16},{16,0},{32,48},{48,32},{64,80},{80,64},{96,112},{112,96},{1... | collective-permute-start | bytes 688136 | tf_op jit(solution)/shard_map/ppermute | solution.py:19
  450.1 7.6 %collective-permute-start.1 = (bf16[2,16,3584]{2,1,0:T(8,128)(2,1)S(1)}, bf16[2,16,3584]{2,1,0:T(8,128)(2,1)S(1)}, u32[]{:S(2)}, u32[]{:S(2)}) collective-permute-start(bf16[2,16,3584]{2,1,0:T(8,128)(2,1)S(1)} %collective-permute-done), channel_id=1, source_target_pairs={{0,32},{32,0},{16,48},{48,16},{64,96},{96,64},{80,112},{112,80},{1... | collective-permute-start | bytes 688136 | tf_op jit(solution)/shard_map/ppermute | solution.py:19
  457.7 4.9 %collective-permute-start.2 = (bf16[2,16,3584]{2,1,0:T(8,128)(2,1)S(1)}, bf16[2,16,3584]{2,1,0:T(8,128)(2,1)S(1)}, u32[]{:S(2)}, u32[]{:S(2)}) collective-permute-start(bf16[2,16,3584]{2,1,0:T(8,128)(2,1)S(1)} %collective-permute-done.1), channel_id=1, source_target_pairs={{0,64},{64,0},{16,80},{80,16},{32,96},{96,32},{48,112},{112,48},{1... | collective-permute-start | bytes 688136 | tf_op jit(solution)/shard_map/ppermute | solution.py:19
  458.9 3.7 copy-start.1
Sparse Core Ops, SparseCore 0:
  309.2 134.8 all-reduce.1
where the time goes:
time: 475 us; the launch traced here: 470 us
  waiting for transfers between devices  346 us (73%)
  matrix products  49.9 us (11%)
  starting transfers between devices  44.2 us (9%)
  between operations  14.2 us (3%)
  other arithmetic  13.7 us (3%)
    all_to_all x2, waiting for transfers between devices, local(): lax.all_to_all(send, 'expert', split_axis=0, concat_axis=0, tiled=True)  167 us
    psum x1, waiting for transfers between devices, local(): summed = lax.psum(stacked, 'expert')  135 us
    all_to_all x2, waiting for transfers between devices, local(): lax.all_to_all(proj, 'expert', split_axis=0, concat_axis=0, tiled=True)  33.6 us
    dot_general x2, matrix products, local(): jnp.einsum('srd,hd->srh', lax.all_to_all(send, 'expert', split_axis=0, co...  24.2 us
    all_to_all x2, starting transfers between devices, local(): lax.all_to_all(send, 'expert', split_axis=0, concat_axis=0, tiled=True)  21 us
    all_to_all x2, starting transfers between devices, local(): lax.all_to_all(proj, 'expert', split_axis=0, concat_axis=0, tiled=True)  17.6 us
    dot_general x2, matrix products, local(): jnp.einsum('tkec,ech->tkh', pick.astype(jnp.bfloat16), returned, preferre...  11.1 us
    ppermute x3, waiting for transfers between devices, partner(): return lax.ppermute(block, axis, route)  10.4 us
  transfers between devices with their start and end apart: 8, of which 8 were waited for; matrix products, arithmetic and copies ran while one was open for 9% of the time, Pallas kernels for 0%

commit v1 on v0

v1 whole, which is shorter than its diff:
```python
import functools

import jax
import jax.numpy as jnp
from jax import lax
from jax.experimental import pallas as pl
from jax.experimental.pallas import tpu as pltpu
from jax.sharding import PartitionSpec as P

ROUTE_SCALE = 2.5
NX, NY, NC = 4, 2, 2
N_PIPE = 8
EXPERTS = NX * NY * NC
MIB = 1024 * 1024


def expert_at(x, y, c):
    return ((x % NX) * NY + y % NY) * NC + c % NC


def shift(dx, dy, dc):
    return [
        (expert_at(x, y, c), expert_at(x + dx, y + dy, c + dc))
        for x in range(NX)
        for y in range(NY)
        for c in range(NC)
    ]


def send(block, dx, dy, dc):
    return lax.ppermute(block, "expert", shift(dx, dy, dc))


def send_mirror(block, dy, dc):
    route = [
        (p * EXPERTS + low, (N_PIPE - 1 - p) * EXPERTS + high)
        for p in range(N_PIPE)
        for low, high in shift(0, dy, dc)
    ]
    return lax.ppermute(block, ("pipe", "expert"), route)


def project_kernel(n, *refs):
    blocks, weight, outs = refs[:n], refs[n], refs[n + 1 :]
    slot, tile = pl.program_id(0), pl.program_id(1)
    tok = blocks[0].shape[0] // 2
    wide = weight.shape[2]
    rows = pl.ds(pl.multiple_of(slot * tok, tok), tok)
    cols = pl.ds(pl.multiple_of(tile * wide, wide), wide)
    tokens = jnp.concatenate([b[rows, :] for b in blocks], axis=0)
    made = lax.dot_general(
        tokens, weight[0, 0], (((1,), (1,)), ((), ())), preferred_element_type=jnp.float32
    ).astype(jnp.bfloat16)
    for i, out in enumerate(outs):
        out[rows, cols] = made[i * tok : (i + 1) * tok]


def project(blocks, weight):
    n = len(blocks)
    rows, depth = blocks[0].shape
    hid = weight.shape[1]
    wide = 512
    whole = pl.BlockSpec((rows, depth), lambda s, h: (0, 0))
    return pl.pallas_call(
        functools.partial(project_kernel, n),
        grid=(2, hid // wide),
        in_specs=[whole] * n
        + [pl.BlockSpec((1, 1, wide, depth), lambda s, h: (s, 0, h, 0))],
        out_specs=[pl.BlockSpec((rows, hid), lambda s, h: (0, 0))] * n,
        out_shape=[jax.ShapeDtypeStruct((rows, hid), jnp.bfloat16)] * n,
        compiler_params=pltpu.CompilerParams(vmem_limit_bytes=36 * MIB),
        cost_estimate=pl.CostEstimate(
            flops=2 * n * rows * depth * hid,
            bytes_accessed=2 * (2 * hid * depth + n * rows * (depth + hid)),
            transcendentals=0,
        ),
    )(*blocks, weight[:, None])


def token_kernel(source, ids, probs, inputs, hidden, *refs):
    returned, (grad, part, held) = refs[:EXPERTS], refs[EXPERTS:]
    slot, group = pl.program_id(0), pl.program_id(1)
    tok, top = 16, 8
    first = pl.multiple_of((slot * pl.num_programs(1) + group) * tok, tok)
    rows = jnp.concatenate([r[pl.ds(first, tok), :] for r in returned], axis=0)
    routes = ids[...]
    shape = (tok * top, EXPERTS * tok)
    mine = lax.broadcasted_iota(jnp.int32, shape, 0) // top == lax.broadcasted_iota(
        jnp.int32, shape, 1
    ) % tok
    pick = jnp.where(jnp.logical_and(mine, routes == source[...]), 1.0, 0.0).astype(jnp.bfloat16)
    back = jnp.dot(pick, rows, preferred_element_type=jnp.float32)
    dgate = jnp.sum(hidden[...].astype(jnp.float32) * back, axis=1, keepdims=True)
    dgate = dgate.reshape(tok, top, 1)
    member = routes.reshape(tok, top, 1) == lax.broadcasted_iota(
        jnp.int32, (tok, top, EXPERTS), 2
    )
    chosen = jnp.sum(jnp.where(member, probs[...][:, None, :], 0.0), axis=2, keepdims=True)
    total = jnp.sum(chosen, axis=1, keepdims=True)
    share = chosen / total
    grad[...] = ((ROUTE_SCALE * share).reshape(tok * top, 1) * back).astype(jnp.bfloat16)
    centred = dgate - jnp.sum(share * dgate, axis=1, keepdims=True)
    selected = ROUTE_SCALE / total * centred * chosen * (1.0 - chosen)
    held[pl.ds(pl.multiple_of(group * tok, tok), tok), :] = jnp.sum(
        jnp.where(member, selected, 0.0), axis=1
    )

    @pl.when(group == pl.num_programs(1) - 1)
    def _():
        logit = held[...]
        high = logit.astype(jnp.bfloat16)
        low = (logit - high.astype(jnp.float32)).astype(jnp.bfloat16)
        over = (((0,), (0,)), ((), ()))
        values = inputs[...]
        made = lax.dot_general(high, values, over, preferred_element_type=jnp.float32)
        made += lax.dot_general(low, values, over, preferred_element_type=jnp.float32)
        part[0] = made.astype(jnp.bfloat16)


def token_math(source, ids, probs, inputs, hidden, returned):
    rows, depth = inputs.shape
    tok, top, hid = 16, 8, hidden.shape[1]
    slot_rows = rows // 2
    groups = slot_rows // tok
    step = lambda s, g: (s * groups + g, 0)
    fixed = lambda s, g: (0, 0)
    return pl.pallas_call(
        token_kernel,
        grid=(2, groups),
        in_specs=[
            pl.BlockSpec((1, EXPERTS * tok), fixed),
            pl.BlockSpec((tok * top, 1), step),
            pl.BlockSpec((tok, EXPERTS), step),
            pl.BlockSpec((slot_rows, depth), lambda s, g: (s, 0)),
            pl.BlockSpec((tok * top, hid), step),
        ]
        + [pl.BlockSpec((rows, hid), fixed)] * EXPERTS,
        out_specs=[
            pl.BlockSpec((tok * top, hid), step),
            pl.BlockSpec((1, EXPERTS, depth), lambda s, g: (s, 0, 0)),
        ],
        out_shape=[
            jax.ShapeDtypeStruct((rows * top, hid), jnp.bfloat16),
            jax.ShapeDtypeStruct((2, EXPERTS, depth), jnp.bfloat16),
        ],
        scratch_shapes=[pltpu.VMEM((slot_rows, EXPERTS), jnp.float32)],
        compiler_params=pltpu.CompilerParams(vmem_limit_bytes=32 * MIB),
        cost_estimate=pl.CostEstimate(
            flops=2 * rows * top * hid * EXPERTS * tok,
            bytes_accessed=2 * rows * hid * (2 * top + EXPERTS),
            transcendentals=0,
        ),
    )(source, ids, probs, inputs, hidden, *returned)


def gather(own):
    across = send(own, 0, 1, 0)
    from_low = send(own, 1, 0, 0)
    from_high = send(own, -1, 0, 0)
    from_low_across = send(across, 1, 0, 0)
    from_high_across = send(across, -1, 0, 0)
    far = send(from_low, 1, 0, 0)
    far_across = send(from_high_across, -1, 0, 0)
    return {
        0: (own, across),
        -1: (from_low, from_low_across),
        1: (from_high, from_high_across),
        2: (far, far_across),
    }


def reduce_router(part, core):
    wide = jnp.float32
    narrow = jnp.bfloat16
    first = core == 0
    keep = jnp.where(first, part[0], part[1])
    give = jnp.where(first, part[1], part[0])
    pair = (keep.astype(wide) + send(give, 0, 0, 1).astype(wide)).astype(narrow)
    low, high, far = send(pair, 1, 0, 0), send(pair, -1, 0, 0), send(pair, 2, 0, 0)
    line = (
        (pair.astype(wide) + far.astype(wide)) + (low.astype(wide) + high.astype(wide))
    ).astype(narrow)
    other = send(line, 0, 1, 0)
    mirror, mirror_other = send_mirror(line, 0, 1), send_mirror(line, 1, 1)
    total = (line.astype(wide) + other.astype(wide)) + (
        mirror.astype(wide) + mirror_other.astype(wide)
    )
    sibling = send(total, 0, 0, 1)
    return jnp.stack([jnp.where(first, total, sibling), jnp.where(first, sibling, total)])


def local(out_grad, saved_input, saved_hidden, expert_ids, down_weight, router_weight):
    tok, depth = out_grad.shape[2:]
    top, hid = saved_hidden.shape[3:]
    rows = 2 * tok
    me = lax.axis_index("expert")
    x, y, c = me // (NY * NC), me // NC % NY, me % NC

    logits = jnp.einsum(
        "std,sed->ste", saved_input[0], router_weight[0], preferred_element_type=jnp.float32
    )
    probs = jax.nn.sigmoid(logits).reshape(rows, EXPERTS)
    ids = expert_ids.reshape(rows * top, 1)

    own = out_grad.reshape(rows, depth)
    weight = down_weight.reshape(2, hid, depth)
    returned, source = [], []
    for dx, (near, across) in gather(own).items():
        blocks = [near, across, send(near, 0, 0, 1), send(across, 0, 0, 1)]
        projected = project(blocks, weight)
        for i, made in enumerate(projected):
            dy, dc = i % 2, i // 2
            away = (dx, dy, dc)
            returned.append(send(made, *away) if any(away) else made)
            source.append(expert_at(x - dx, y + dy, c + dc))
    marks = jnp.repeat(jnp.stack(source).astype(jnp.int32), 16)[None]
    grad, part = token_math(
        marks, ids, probs, saved_input.reshape(rows, depth), saved_hidden.reshape(rows * top, hid), returned
    )
    return grad.reshape(saved_hidden.shape), reduce_router(part, c)[None]


def solution(mesh):
    in_specs = (
        P("pipe", None, "expert", None),
        P("pipe", None, "expert", None),
        P("pipe", None, "expert", None, None),
        P("pipe", None, "expert", None),
        P("pipe", None, "expert", None, None),
        P("pipe", None, None, None),
    )
    out_specs = (P("pipe", None, "expert", None, None), P("pipe", None, None, None))
    return jax.shard_map(local, mesh=mesh, in_specs=in_specs, out_specs=out_specs, check_vma=False)
```

time: 475 us -> 205 us (0.43)
  waiting for transfers between devices: 346 us -> 84.1 us
  matrix products: 49.9 us -> 0.36 us
  Pallas kernels: 0 us -> 41.4 us
  starting transfers between devices: 44.2 us -> 60.6 us
  between operations: 14.2 us -> 0.88 us
  local copies, waits for them, and re-layouts: 2.74 us -> 15.7 us
  other arithmetic: 13.7 us -> 1 us
    all_to_all x4 -> x0, waiting for transfers between devices: 200 us -> none  [the longest x2 167 us: local(): lax.all_to_all(send, 'expert', split_axis=0, concat_axis=0, tiled=True)]
    psum x1 -> x0, waiting for transfers between devices: 135 us -> none  [local(): summed = lax.psum(stacked, 'expert')]
    ppermute x3 -> x38, waiting for transfers between devices: 10.4 us -> 84.1 us  [the longest x36 76.8 us: send(): return lax.ppermute(block, 'expert', shift(dx, dy, dc))]
    ppermute x3 -> x38, starting transfers between devices: 5.47 us -> 60.6 us  [the longest x36 55.1 us: send(): return lax.ppermute(block, 'expert', shift(dx, dy, dc))]
    dot_general x12 -> x1, matrix products: 49.9 us -> 0.36 us  [local(): jnp.einsum('std,sed->ste', saved_input[0], router_weight[0], preferred_el...]
    pallas_call x0 -> x5, Pallas kernels: none -> 41.4 us  [the longest x4 34.7 us: project(): pl.pallas_call(functools.partial(project_kernel, n), grid=(2, hid // wide...]
    all_to_all x4 -> x0, starting transfers between devices: 38.7 us -> none  [the longest x2 21 us: local(): lax.all_to_all(send, 'expert', split_axis=0, concat_axis=0, tiled=True)]
    unnamed x12 -> x59, local copies, waits for them, and re-layouts: 1.25 us -> 15.2 us
  transfers between devices with their start and end apart: 8 -> 38, of which waited for: 8 -> 13; matrix products, arithmetic and copies ran while one was open for 9% -> 0% of each run, Pallas kernels for 0% -> 17%
where the time goes in v1:
time: 205 us; the launch traced here: 204 us
  waiting for transfers between devices  84.1 us (41%)
  starting transfers between devices  60.6 us (30%)
  Pallas kernels  41.4 us (20%)
  local copies, waits for them, and re-layouts  15.7 us (8%)
    ppermute x36, waiting for transfers between devices, send(): return lax.ppermute(block, 'expert', shift(dx, dy, dc))  76.8 us
    ppermute x36, starting transfers between devices, send(): return lax.ppermute(block, 'expert', shift(dx, dy, dc))  55.1 us
    pallas_call x4, Pallas kernels, project(): pl.pallas_call(functools.partial(project_kernel, n), grid=(2, hid // wide...  34.7 us
    unnamed x59, local copies, waits for them, and re-layouts  15.2 us
    ppermute x2, waiting for transfers between devices, send_mirror(): return lax.ppermute(block, ('pipe', 'expert'), route)  7.25 us
    pallas_call x1, Pallas kernels, token_math(): pl.pallas_call(token_kernel, grid=(2, groups), in_specs=[pl.BlockSpec((1,...  6.69 us
    ppermute x2, starting transfers between devices, send_mirror(): return lax.ppermute(block, ('pipe', 'expert'), route)  5.5 us
  transfers between devices with their start and end apart: 38, of which 13 were waited for; matrix products, arithmetic and copies ran while one was open for 0% of the time, Pallas kernels for 17%

profile of v1, /device:TPU:1, one launch (start us, length us, event | category | flops | bytes accessed | tf_op | source)
XLA Modules:
  0.0 204.0 jit_solution(6439050425556943793)
XLA Ops:
  0.6 3.8 %collective-permute-start = (bf16[128,3584]{1,0:T(8,128)(2,1)}, bf16[128,3584]{1,0:T(8,128)(2,1)}, u32[]{:S(2)}, u32[]{:S(2)}) collective-permute-start(bf16[128,3584]{1,0:T(8,128)(2,1)} %bitcast.43), channel_id=1, source_target_pairs={{0,2},{1,3},{2,0},{3,1},{4,6},{5,7},{6,4},{7,5},{8,10},{9,11},{10,... | collective-permute-start | bytes 2752520 | tf_op jit(solution)/shard_map/ppermute | solution.py:31
  8.7 15.9 %collective-permute-done.refs_1_ = bf16[128,3584]{1,0:T(8,128)(2,1)} collective-permute-done((bf16[128,3584]{1,0:T(8,128)(2,1)}, bf16[128,3584]{1,0:T(8,128)(2,1)}, u32[]{:S(2)}, u32[]{:S(2)}) %collective-permute-start) | collective-permute-done | bytes 917536 | tf_op jit(solution)/shard_map/ppermute | solution.py:31
  24.6 2.5 %collective-permute-start.15 = (bf16[128,3584]{1,0:T(8,128)(2,1)}, bf16[128,3584]{1,0:T(8,128)(2,1)}, u32[]{:S(2)}, u32[]{:S(2)}) collective-permute-start(bf16[128,3584]{1,0:T(8,128)(2,1)} %collective-permute-done.refs_1_), channel_id=1, source_target_pairs={{0,12},{1,13},{2,14},{3,15},{4,0},{5,1},{6,2},{7,3},{8,4},{9,5},{1... | collective-permute-start | bytes 2752520 | tf_op jit(solution)/shard_map/ppermute | solution.py:31
  28.1 2.3 %collective-permute-start.8 = (bf16[128,3584]{1,0:T(8,128)(2,1)S(1)}, bf16[128,3584]{1,0:T(8,128)(2,1)S(1)}, u32[]{:S(2)}, u32[]{:S(2)}) collective-permute-start(bf16[128,3584]{1,0:T(8,128)(2,1)S(1)} %collective-permute-done.6.refs_0_), channel_id=1, source_target_pairs={{0,1},{1,0},{2,3},{3,2},{4,5},{5,4},{6,7},{7,6},{8,9},{9,8},{10,11... | collective-permute-start | bytes 2752520 | tf_op jit(solution)/shard_map/ppermute | solution.py:31
  32.3 14.5 %collective-permute-done.15.refs_1_ = bf16[128,3584]{1,0:T(8,128)(2,1)} collective-permute-done((bf16[128,3584]{1,0:T(8,128)(2,1)}, bf16[128,3584]{1,0:T(8,128)(2,1)}, u32[]{:S(2)}, u32[]{:S(2)}) %collective-permute-start.15) | collective-permute-done | bytes 917536 | tf_op jit(solution)/shard_map/ppermute | solution.py:31
  46.8 2.1 %collective-permute-start.23 = (bf16[128,3584]{1,0:T(8,128)(2,1)}, bf16[128,3584]{1,0:T(8,128)(2,1)S(1)}, u32[]{:S(2)}, u32[]{:S(2)}) collective-permute-start(bf16[128,3584]{1,0:T(8,128)(2,1)} %collective-permute-done.15.refs_1_), channel_id=1, source_target_pairs={{0,12},{1,13},{2,14},{3,15},{4,0},{5,1},{6,2},{7,3},{8,4},{9,5},{1... | collective-permute-start | bytes 2752520 | tf_op jit(solution)/shard_map/ppermute | solution.py:31
  48.9 4.5 %collective-permute-start.16 = (bf16[128,3584]{1,0:T(8,128)(2,1)S(1)}, bf16[128,3584]{1,0:T(8,128)(2,1)}, u32[]{:S(2)}, u32[]{:S(2)}) collective-permute-start(bf16[128,3584]{1,0:T(8,128)(2,1)S(1)} %collective-permute-done.14.refs_0_), channel_id=1, source_target_pairs={{0,1},{1,0},{2,3},{3,2},{4,5},{5,4},{6,7},{7,6},{8,9},{9,8},{10,11... | collective-permute-start | bytes 2752520 | tf_op jit(solution)/shard_map/ppermute | solution.py:31
  53.4 14.7 %collective-permute-done.7.refs_1_ = bf16[128,3584]{1,0:T(8,128)(2,1)} collective-permute-done((bf16[128,3584]{1,0:T(8,128)(2,1)}, bf16[128,3584]{1,0:T(8,128)(2,1)}, u32[]{:S(2)}, u32[]{:S(2)}) %collective-permute-start.7) | collective-permute-done | bytes 917536 | tf_op jit(solution)/shard_map/ppermute | solution.py:31
  68.1 2.7 %collective-permute-start.9 = (bf16[128,3584]{1,0:T(8,128)(2,1)}, bf16[128,3584]{1,0:T(8,128)(2,1)}, u32[]{:S(2)}, u32[]{:S(2)}) collective-permute-start(bf16[128,3584]{1,0:T(8,128)(2,1)} %collective-permute-done.7.refs_1_), channel_id=1, source_target_pairs={{0,1},{1,0},{2,3},{3,2},{4,5},{5,4},{6,7},{7,6},{8,9},{9,8},{10,11... | collective-permute-start | bytes 2752520 | tf_op jit(solution)/shard_map/ppermute | solution.py:31
  74.8 8.5 %shard_map.77 = (bf16[128,1024]{1,0:T(8,128)(2,1)S(1)}, bf16[128,1024]{1,0:T(8,128)(2,1)S(1)}, bf16[128,1024]{1,0:T(8,128)(2,1)S(1)}, bf16[128,1024]{1,0:T(8,128)(2,1)S(1)}) custom-call(bf16[128,3584]{1,0:T(8,128)(2,1)S(1)} %bitcast.47, bf16[128,3584]{1,0:T(8,128)(2,1)} %collective-permute-done.refs_1_, bf16[128,3584]{1,0:T(8,128)(2,1)S(1)} %copy-done.7, ...), custom_call_target="tpu_custom_call" | custom-call | flops 3758096384 | bytes 19398656 | tf_op jit(solution)/shard_map/pallas_call | solution.py:64
  83.3 3.0 %collective-permute-start.3 = (bf16[128,1024]{1,0:T(8,128)(2,1)S(1)}, bf16[128,1024]{1,0:T(8,128)(2,1)S(1)}, u32[]{:S(2)}, u32[]{:S(2)}) collective-permute-start(bf16[128,1024]{1,0:T(8,128)(2,1)S(1)} %get-tuple-element.21), channel_id=1, source_target_pairs={{0,2},{1,3},{2,0},{3,1},{4,6},{5,7},{6,4},{7,5},{8,10},{9,11},{10,... | collective-permute-start | bytes 786440 | tf_op jit(solution)/shard_map/ppermute | solution.py:31
  87.0 8.3 %shard_map.78 = (bf16[128,1024]{1,0:T(8,128)(2,1)S(1)}, bf16[128,1024]{1,0:T(8,128)(2,1)S(1)}, bf16[128,1024]{1,0:T(8,128)(2,1)S(1)}, bf16[128,1024]{1,0:T(8,128)(2,1)S(1)}) custom-call(bf16[128,3584]{1,0:T(8,128)(2,1)S(1)} %copy-done.5, bf16[128,3584]{1,0:T(8,128)(2,1)} %collective-permute-done.7.refs_1_, bf16[128,3584]{1,0:T(8,128)(2,1)S(1)} %copy-done.9, ...), custom_call_target="tpu_custom_call" | custom-call | flops 3758096384 | bytes 19398656 | tf_op jit(solution)/shard_map/pallas_call | solution.py:64
  98.5 9.3 %shard_map.79 = (bf16[128,1024]{1,0:T(8,128)(2,1)S(1)}, bf16[128,1024]{1,0:T(8,128)(2,1)S(1)}, bf16[128,1024]{1,0:T(8,128)(2,1)S(1)}, bf16[128,1024]{1,0:T(8,128)(2,1)}) custom-call(bf16[128,3584]{1,0:T(8,128)(2,1)S(1)} %collective-permute-done.14.refs_0_, bf16[128,3584]{1,0:T(8,128)(2,1)} %collective-permute-done.15.refs_1_, ...), custom_call_target="tpu_custom_call" | custom-call | flops 3758096384 | bytes 19398656 | tf_op jit(solution)/shard_map/pallas_call | solution.py:64
  109.1 2.8 %collective-permute-start.13 = (bf16[128,1024]{1,0:T(8,128)(2,1)S(1)}, bf16[128,1024]{1,0:T(8,128)(2,1)S(1)}, u32[]{:S(2)}, u32[]{:S(2)}) collective-permute-start(bf16[128,1024]{1,0:T(8,128)(2,1)S(1)} %get-tuple-element.27), channel_id=1, source_target_pairs={{0,15},{1,14},{2,13},{3,12},{4,3},{5,2},{6,1},{7,0},{8,7},{9,6},{1... | collective-permute-start | bytes 786440 | tf_op jit(solution)/shard_map/ppermute | solution.py:31
  112.0 2.0 collective-permute-start.19
  114.0 2.2 %collective-permute-start.20 = (bf16[128,1024]{1,0:T(8,128)(2,1)S(1)}, bf16[128,1024]{1,0:T(8,128)(2,1)S(1)}, u32[]{:S(2)}, u32[]{:S(2)}) collective-permute-start(bf16[128,1024]{1,0:T(8,128)(2,1)S(1)} %get-tuple-element.30), channel_id=1, source_target_pairs={{0,5},{1,4},{2,7},{3,6},{4,9},{5,8},{6,11},{7,10},{8,13},{9,12},{1... | collective-permute-start | bytes 786440 | tf_op jit(solution)/shard_map/ppermute | solution.py:31
  116.2 8.7 %shard_map.80 = (bf16[128,1024]{1,0:T(8,128)(2,1)}, bf16[128,1024]{1,0:T(8,128)(2,1)}, bf16[128,1024]{1,0:T(8,128)(2,1)}, bf16[128,1024]{1,0:T(8,128)(2,1)}) custom-call(bf16[128,3584]{1,0:T(8,128)(2,1)S(1)} %collective-permute-done.22.refs_0_, bf16[128,3584]{1,0:T(8,128)(2,1)S(1)} %collective-permute-done.23.refs_1_, ...), custom_call_target="tpu_custom_call" | custom-call | flops 3758096384 | bytes 19398656 | tf_op jit(solution)/shard_map/pallas_call | solution.py:64
  125.6 2.0 collective-permute-start.21
  130.1 3.6 %collective-permute-start.27 = (bf16[128,1024]{1,0:T(8,128)(2,1)}, bf16[128,1024]{1,0:T(8,128)(2,1)}, u32[]{:S(2)}, u32[]{:S(2)}) collective-permute-start(bf16[128,1024]{1,0:T(8,128)(2,1)} %get-tuple-element.33), channel_id=1, source_target_pairs={{0,10},{1,11},{2,8},{3,9},{4,14},{5,15},{6,12},{7,13},{8,2},{9,3},... | collective-permute-start | bytes 786440 | tf_op jit(solution)/shard_map/ppermute | solution.py:31
  134.3 3.5 %collective-permute-start.28 = (bf16[128,1024]{1,0:T(8,128)(2,1)}, bf16[128,1024]{1,0:T(8,128)(2,1)}, u32[]{:S(2)}, u32[]{:S(2)}) collective-permute-start(bf16[128,1024]{1,0:T(8,128)(2,1)} %get-tuple-element.34), channel_id=1, source_target_pairs={{0,9},{1,8},{2,11},{3,10},{4,13},{5,12},{6,15},{7,14},{8,1},{9,0},... | collective-permute-start | bytes 786440 | tf_op jit(solution)/shard_map/ppermute | solution.py:31
  140.1 5.4 %collective-permute-done.26.refs_12_ = bf16[128,1024]{1,0:T(8,128)(2,1)} collective-permute-done((bf16[128,1024]{1,0:T(8,128)(2,1)}, bf16[128,1024]{1,0:T(8,128)(2,1)}, u32[]{:S(2)}, u32[]{:S(2)}) %collective-permute-start.26) | collective-permute-done | bytes 262176 | tf_op jit(solution)/shard_map/ppermute | solution.py:31
  145.5 6.3 %collective-permute-done.27.refs_13_ = bf16[128,1024]{1,0:T(8,128)(2,1)} collective-permute-done((bf16[128,1024]{1,0:T(8,128)(2,1)}, bf16[128,1024]{1,0:T(8,128)(2,1)}, u32[]{:S(2)}, u32[]{:S(2)}) %collective-permute-start.27) | collective-permute-done | bytes 262176 | tf_op jit(solution)/shard_map/ppermute | solution.py:31
  151.9 6.3 %collective-permute-done.28.refs_14_ = bf16[128,1024]{1,0:T(8,128)(2,1)} collective-permute-done((bf16[128,1024]{1,0:T(8,128)(2,1)}, bf16[128,1024]{1,0:T(8,128)(2,1)}, u32[]{:S(2)}, u32[]{:S(2)}) %collective-permute-start.28) | collective-permute-done | bytes 262176 | tf_op jit(solution)/shard_map/ppermute | solution.py:31
  158.2 5.6 %collective-permute-done.29.refs_15_ = bf16[128,1024]{1,0:T(8,128)(2,1)} collective-permute-done((bf16[128,1024]{1,0:T(8,128)(2,1)}, bf16[128,1024]{1,0:T(8,128)(2,1)}, u32[]{:S(2)}, u32[]{:S(2)}) %collective-permute-start.29) | collective-permute-done | bytes 262176 | tf_op jit(solution)/shard_map/ppermute | solution.py:31
  163.9 1.6 copy-done.2
  170.2 6.7 %shard_map.81 = (bf16[1024,1024]{1,0:T(8,128)(2,1)}, bf16[2,16,3584]{2,1,0:T(8,128)(2,1)S(1)}) custom-call(s32[1,256]{1,0:T(1,128)S(1)} %broadcast_in_dim_reshape.4.source, s32[1024,1]{1,0:T(8,128)S(1)} %reshape.35.ids, f32[128,16]{1,0:T(8,128)S(1)} %bitcast.48, bf16[128,3584]{1,0:T(8,128)(2,1)S(1)} %bitcast.41, bf16[1024,1024]{1,0:T(8,128)(2,1)S(1)} %bitcast.42, ...), custom_call_target="tpu_custom_call" | custom-call | flops 536870912 | bytes 8388608 | tf_op jit(solution)/shard_map/pallas_call | solution.py:127
  179.6 2.7 %collective-permute-start.33 = (bf16[16,3584]{1,0:T(8,128)(2,1)S(1)}, bf16[16,3584]{1,0:T(8,128)(2,1)S(1)}, u32[]{:S(2)}, u32[]{:S(2)}) collective-permute-start(bf16[16,3584]{1,0:T(8,128)(2,1)S(1)} %fusion.4), channel_id=1, source_target_pairs={{0,12},{1,13},{2,14},{3,15},{4,0},{5,1},{6,2},{7,3},{8,4},{9,5},{1... | collective-permute-start | bytes 344072 | tf_op jit(solution)/shard_map/ppermute | solution.py:31
  182.2 2.3 %collective-permute-done.31 = bf16[16,3584]{1,0:T(8,128)(2,1)S(1)} collective-permute-done((bf16[16,3584]{1,0:T(8,128)(2,1)S(1)}, bf16[16,3584]{1,0:T(8,128)(2,1)S(1)}, u32[]{:S(2)}, u32[]{:S(2)}) %collective-permute-start.31) | collective-permute-done | bytes 114720 | tf_op jit(solution)/shard_map/ppermute | solution.py:31
  184.5 2.9 %collective-permute-done.32 = bf16[16,3584]{1,0:T(8,128)(2,1)S(1)} collective-permute-done((bf16[16,3584]{1,0:T(8,128)(2,1)S(1)}, bf16[16,3584]{1,0:T(8,128)(2,1)S(1)}, u32[]{:S(2)}, u32[]{:S(2)}) %collective-permute-start.32) | collective-permute-done | bytes 114720 | tf_op jit(solution)/shard_map/ppermute | solution.py:31
  188.8 4.9 %collective-permute-start.35 = (bf16[16,3584]{1,0:T(8,128)(2,1)S(1)}, bf16[16,3584]{1,0:T(8,128)(2,1)S(1)}, u32[]{:S(2)}, u32[]{:S(2)}) collective-permute-start(bf16[16,3584]{1,0:T(8,128)(2,1)S(1)} %add_convert_fusion), channel_id=1, source_target_pairs={{0,113},{1,112},{2,115},{3,114},{4,117},{5,116},{6,119},{7,118},{8... | collective-permute-start | bytes 344072 | tf_op jit(solution)/shard_map/ppermute | solution.py:40
  194.3 4.6 %collective-permute-done.35 = bf16[16,3584]{1,0:T(8,128)(2,1)S(1)} collective-permute-done((bf16[16,3584]{1,0:T(8,128)(2,1)S(1)}, bf16[16,3584]{1,0:T(8,128)(2,1)S(1)}, u32[]{:S(2)}, u32[]{:S(2)}) %collective-permute-start.35) | collective-permute-done | bytes 114720 | tf_op jit(solution)/shard_map/ppermute | solution.py:40
  199.0 2.6 %collective-permute-done.36 = bf16[16,3584]{1,0:T(8,128)(2,1)S(1)} collective-permute-done((bf16[16,3584]{1,0:T(8,128)(2,1)S(1)}, bf16[16,3584]{1,0:T(8,128)(2,1)S(1)}, u32[]{:S(2)}, u32[]{:S(2)}) %collective-permute-start.36) | collective-permute-done | bytes 114720 | tf_op jit(solution)/shard_map/ppermute | solution.py:40
  (120 shorter events, 34.2 us)
Async XLA Ops:
  0.6 23.9 %collective-permute-start = (bf16[128,3584]{1,0:T(8,128)(2,1)}, bf16[128,3584]{1,0:T(8,128)(2,1)}, u32[]{:S(2)}, u32[]{:S(2)}) collective-permute-start(bf16[128,3584]{1,0:T(8,128)(2,1)} %bitcast.43), channel_id=1, source_target_pairs={{0,2},{1,3},{2,0},{3,1},{4,6},{5,7},{6,4},{7,5},{8,10},{9,11},{10,... | collective-permute-start | bytes 2752520 | tf_op jit(solution)/shard_map/ppermute | solution.py:31
  4.5 22.6 %collective-permute-start.6 = (bf16[128,3584]{1,0:T(8,128)(2,1)}, bf16[128,3584]{1,0:T(8,128)(2,1)S(1)}, u32[]{:S(2)}, u32[]{:S(2)}) collective-permute-start(bf16[128,3584]{1,0:T(8,128)(2,1)} %bitcast.44), channel_id=1, source_target_pairs={{0,4},{1,5},{2,6},{3,7},{4,8},{5,9},{6,10},{7,11},{8,12},{9,13},{1... | collective-permute-start | bytes 2752520 | tf_op jit(solution)/shard_map/ppermute | solution.py:31
  5.7 22.4 %collective-permute-start.14 = (bf16[128,3584]{1,0:T(8,128)(2,1)}, bf16[128,3584]{1,0:T(8,128)(2,1)S(1)}, u32[]{:S(2)}, u32[]{:S(2)}) collective-permute-start(bf16[128,3584]{1,0:T(8,128)(2,1)} %bitcast.45), channel_id=1, source_target_pairs={{0,12},{1,13},{2,14},{3,15},{4,0},{5,1},{6,2},{7,3},{8,4},{9,5},{1... | collective-permute-start | bytes 2752520 | tf_op jit(solution)/shard_map/ppermute | solution.py:31
  7.1 24.2 %collective-permute-start.1 = (bf16[128,3584]{1,0:T(8,128)(2,1)}, bf16[128,3584]{1,0:T(8,128)(2,1)S(1)}, u32[]{:S(2)}, u32[]{:S(2)}) collective-permute-start(bf16[128,3584]{1,0:T(8,128)(2,1)} %bitcast.46), channel_id=1, source_target_pairs={{0,1},{1,0},{2,3},{3,2},{4,5},{5,4},{6,7},{7,6},{8,9},{9,8},{10,11... | collective-permute-start | bytes 2752520 | tf_op jit(solution)/shard_map/ppermute | solution.py:31
  24.6 22.2 %collective-permute-start.15 = (bf16[128,3584]{1,0:T(8,128)(2,1)}, bf16[128,3584]{1,0:T(8,128)(2,1)}, u32[]{:S(2)}, u32[]{:S(2)}) collective-permute-start(bf16[128,3584]{1,0:T(8,128)(2,1)} %collective-permute-done.refs_1_), channel_id=1, source_target_pairs={{0,12},{1,13},{2,14},{3,15},{4,0},{5,1},{6,2},{7,3},{8,4},{9,5},{1... | collective-permute-start | bytes 2752520 | tf_op jit(solution)/shard_map/ppermute | solution.py:31
  27.1 21.8 %collective-permute-start.22 = (bf16[128,3584]{1,0:T(8,128)(2,1)S(1)}, bf16[128,3584]{1,0:T(8,128)(2,1)S(1)}, u32[]{:S(2)}, u32[]{:S(2)}) collective-permute-start(bf16[128,3584]{1,0:T(8,128)(2,1)S(1)} %collective-permute-done.6.refs_0_), channel_id=1, source_target_pairs={{0,4},{1,5},{2,6},{3,7},{4,8},{5,9},{6,10},{7,11},{8,12},{9,13},{1... | collective-permute-start | bytes 2752520 | tf_op jit(solution)/shard_map/ppermute | solution.py:31
  27.1 41.0 %collective-permute-start.7 = (bf16[128,3584]{1,0:T(8,128)(2,1)}, bf16[128,3584]{1,0:T(8,128)(2,1)}, u32[]{:S(2)}, u32[]{:S(2)}) collective-permute-start(bf16[128,3584]{1,0:T(8,128)(2,1)} %collective-permute-done.refs_1_), channel_id=1, source_target_pairs={{0,4},{1,5},{2,6},{3,7},{4,8},{5,9},{6,10},{7,11},{8,12},{9,13},{1... | collective-permute-start | bytes 2752520 | tf_op jit(solution)/shard_map/ppermute | solution.py:31
  28.1 42.7 %collective-permute-start.8 = (bf16[128,3584]{1,0:T(8,128)(2,1)S(1)}, bf16[128,3584]{1,0:T(8,128)(2,1)S(1)}, u32[]{:S(2)}, u32[]{:S(2)}) collective-permute-start(bf16[128,3584]{1,0:T(8,128)(2,1)S(1)} %collective-permute-done.6.refs_0_), channel_id=1, source_target_pairs={{0,1},{1,0},{2,3},{3,2},{4,5},{5,4},{6,7},{7,6},{8,9},{9,8},{10,11... | collective-permute-start | bytes 2752520 | tf_op jit(solution)/shard_map/ppermute | solution.py:31
  32.3 39.5 %collective-permute-start.2 = (bf16[128,3584]{1,0:T(8,128)(2,1)}, bf16[128,3584]{1,0:T(8,128)(2,1)}, u32[]{:S(2)}, u32[]{:S(2)}) collective-permute-start(bf16[128,3584]{1,0:T(8,128)(2,1)} %collective-permute-done.refs_1_), channel_id=1, source_target_pairs={{0,1},{1,0},{2,3},{3,2},{4,5},{5,4},{6,7},{7,6},{8,9},{9,8},{10,11... | collective-permute-start | bytes 2752520 | tf_op jit(solution)/shard_map/ppermute | solution.py:31
  46.8 25.6 %collective-permute-start.23 = (bf16[128,3584]{1,0:T(8,128)(2,1)}, bf16[128,3584]{1,0:T(8,128)(2,1)S(1)}, u32[]{:S(2)}, u32[]{:S(2)}) collective-permute-start(bf16[128,3584]{1,0:T(8,128)(2,1)} %collective-permute-done.15.refs_1_), channel_id=1, source_target_pairs={{0,12},{1,13},{2,14},{3,15},{4,0},{5,1},{6,2},{7,3},{8,4},{9,5},{1... | collective-permute-start | bytes 2752520 | tf_op jit(solution)/shard_map/ppermute | solution.py:31
  48.9 34.4 %collective-permute-start.16 = (bf16[128,3584]{1,0:T(8,128)(2,1)S(1)}, bf16[128,3584]{1,0:T(8,128)(2,1)}, u32[]{:S(2)}, u32[]{:S(2)}) collective-permute-start(bf16[128,3584]{1,0:T(8,128)(2,1)S(1)} %collective-permute-done.14.refs_0_), channel_id=1, source_target_pairs={{0,1},{1,0},{2,3},{3,2},{4,5},{5,4},{6,7},{7,6},{8,9},{9,8},{10,11... | collective-permute-start | bytes 2752520 | tf_op jit(solution)/shard_map/ppermute | solution.py:31
  68.1 18.2 %collective-permute-start.9 = (bf16[128,3584]{1,0:T(8,128)(2,1)}, bf16[128,3584]{1,0:T(8,128)(2,1)}, u32[]{:S(2)}, u32[]{:S(2)}) collective-permute-start(bf16[128,3584]{1,0:T(8,128)(2,1)} %collective-permute-done.7.refs_1_), channel_id=1, source_target_pairs={{0,1},{1,0},{2,3},{3,2},{4,5},{5,4},{6,7},{7,6},{8,9},{9,8},{10,11... | collective-permute-start | bytes 2752520 | tf_op jit(solution)/shard_map/ppermute | solution.py:31
  71.8 25.2 %collective-permute-start.17 = (bf16[128,3584]{1,0:T(8,128)(2,1)}, bf16[128,3584]{1,0:T(8,128)(2,1)}, u32[]{:S(2)}, u32[]{:S(2)}) collective-permute-start(bf16[128,3584]{1,0:T(8,128)(2,1)} %collective-permute-done.15.refs_1_), channel_id=1, source_target_pairs={{0,1},{1,0},{2,3},{3,2},{4,5},{5,4},{6,7},{7,6},{8,9},{9,8},{10,11... | collective-permute-start | bytes 2752520 | tf_op jit(solution)/shard_map/ppermute | solution.py:31
  71.8 37.3 %collective-permute-start.24 = (bf16[128,3584]{1,0:T(8,128)(2,1)S(1)}, bf16[128,3584]{1,0:T(8,128)(2,1)S(1)}, u32[]{:S(2)}, u32[]{:S(2)}) collective-permute-start(bf16[128,3584]{1,0:T(8,128)(2,1)S(1)} %collective-permute-done.22.refs_0_), channel_id=1, source_target_pairs={{0,1},{1,0},{2,3},{3,2},{4,5},{5,4},{6,7},{7,6},{8,9},{9,8},{10,11... | collective-permute-start | bytes 2752520 | tf_op jit(solution)/shard_map/ppermute | solution.py:31
  72.3 41.6 %collective-permute-start.25 = (bf16[128,3584]{1,0:T(8,128)(2,1)S(1)}, bf16[128,3584]{1,0:T(8,128)(2,1)S(1)}, u32[]{:S(2)}, u32[]{:S(2)}) collective-permute-start(bf16[128,3584]{1,0:T(8,128)(2,1)S(1)} %collective-permute-done.23.refs_1_), channel_id=1, source_target_pairs={{0,1},{1,0},{2,3},{3,2},{4,5},{5,4},{6,7},{7,6},{8,9},{9,8},{10,11... | collective-permute-start | bytes 2752520 | tf_op jit(solution)/shard_map/ppermute | solution.py:31
  83.3 12.0 %collective-permute-start.3 = (bf16[128,1024]{1,0:T(8,128)(2,1)S(1)}, bf16[128,1024]{1,0:T(8,128)(2,1)S(1)}, u32[]{:S(2)}, u32[]{:S(2)}) collective-permute-start(bf16[128,1024]{1,0:T(8,128)(2,1)S(1)} %get-tuple-element.21), channel_id=1, source_target_pairs={{0,2},{1,3},{2,0},{3,1},{4,6},{5,7},{6,4},{7,5},{8,10},{9,11},{10,... | collective-permute-start | bytes 786440 | tf_op jit(solution)/shard_map/ppermute | solution.py:31
  86.3 10.1 %collective-permute-start.4 = (bf16[128,1024]{1,0:T(8,128)(2,1)S(1)}, bf16[128,1024]{1,0:T(8,128)(2,1)S(1)}, u32[]{:S(2)}, u32[]{:S(2)}) collective-permute-start(bf16[128,1024]{1,0:T(8,128)(2,1)S(1)} %get-tuple-element.22), channel_id=1, source_target_pairs={{0,1},{1,0},{2,3},{3,2},{4,5},{5,4},{6,7},{7,6},{8,9},{9,8},{10,11... | collective-permute-start | bytes 786440 | tf_op jit(solution)/shard_map/ppermute | solution.py:31
  95.3 12.5 %collective-permute-start.5 = (bf16[128,1024]{1,0:T(8,128)(2,1)S(1)}, bf16[128,1024]{1,0:T(8,128)(2,1)S(1)}, u32[]{:S(2)}, u32[]{:S(2)}) collective-permute-start(bf16[128,1024]{1,0:T(8,128)(2,1)S(1)} %get-tuple-element.23), channel_id=1, source_target_pairs={{0,3},{1,2},{2,1},{3,0},{4,7},{5,6},{6,5},{7,4},{8,11},{9,10},{10,... | collective-permute-start | bytes 786440 | tf_op jit(solution)/shard_map/ppermute | solution.py:31
  96.4 15.6 %collective-permute-start.10 = (bf16[128,1024]{1,0:T(8,128)(2,1)S(1)}, bf16[128,1024]{1,0:T(8,128)(2,1)S(1)}, u32[]{:S(2)}, u32[]{:S(2)}) collective-permute-start(bf16[128,1024]{1,0:T(8,128)(2,1)S(1)} %get-tuple-element.24), channel_id=1, source_target_pairs={{0,12},{1,13},{2,14},{3,15},{4,0},{5,1},{6,2},{7,3},{8,4},{9,5},{1... | collective-permute-start | bytes 786440 | tf_op jit(solution)/shard_map/ppermute | solution.py:31
  97.0 14.9 %collective-permute-start.11 = (bf16[128,1024]{1,0:T(8,128)(2,1)S(1)}, bf16[128,1024]{1,0:T(8,128)(2,1)S(1)}, u32[]{:S(2)}, u32[]{:S(2)}) collective-permute-start(bf16[128,1024]{1,0:T(8,128)(2,1)S(1)} %get-tuple-element.25), channel_id=1, source_target_pairs={{0,14},{1,15},{2,12},{3,13},{4,2},{5,3},{6,0},{7,1},{8,6},{9,7},{1... | collective-permute-start | bytes 786440 | tf_op jit(solution)/shard_map/ppermute | solution.py:31
  107.8 17.1 %collective-permute-start.12 = (bf16[128,1024]{1,0:T(8,128)(2,1)S(1)}, bf16[128,1024]{1,0:T(8,128)(2,1)S(1)}, u32[]{:S(2)}, u32[]{:S(2)}) collective-permute-start(bf16[128,1024]{1,0:T(8,128)(2,1)S(1)} %get-tuple-element.26), channel_id=1, source_target_pairs={{0,13},{1,12},{2,15},{3,14},{4,1},{5,0},{6,3},{7,2},{8,5},{9,4},{1... | collective-permute-start | bytes 786440 | tf_op jit(solution)/shard_map/ppermute | solution.py:31
  109.1 18.5 %collective-permute-start.13 = (bf16[128,1024]{1,0:T(8,128)(2,1)S(1)}, bf16[128,1024]{1,0:T(8,128)(2,1)S(1)}, u32[]{:S(2)}, u32[]{:S(2)}) collective-permute-start(bf16[128,1024]{1,0:T(8,128)(2,1)S(1)} %get-tuple-element.27), channel_id=1, source_target_pairs={{0,15},{1,14},{2,13},{3,12},{4,3},{5,2},{6,1},{7,0},{8,7},{9,6},{1... | collective-permute-start | bytes 786440 | tf_op jit(solution)/shard_map/ppermute | solution.py:31
  112.0 17.4 %collective-permute-start.18 = (bf16[128,1024]{1,0:T(8,128)(2,1)S(1)}, bf16[128,1024]{1,0:T(8,128)(2,1)S(1)}, u32[]{:S(2)}, u32[]{:S(2)}) collective-permute-start(bf16[128,1024]{1,0:T(8,128)(2,1)S(1)} %get-tuple-element.28), channel_id=1, source_target_pairs={{0,4},{1,5},{2,6},{3,7},{4,8},{5,9},{6,10},{7,11},{8,12},{9,13},{1... | collective-permute-start | bytes 786440 | tf_op jit(solution)/shard_map/ppermute | solution.py:31
  112.0 21.6 %collective-permute-start.19 = (bf16[128,1024]{1,0:T(8,128)(2,1)S(1)}, bf16[128,1024]{1,0:T(8,128)(2,1)S(1)}, u32[]{:S(2)}, u32[]{:S(2)}) collective-permute-start(bf16[128,1024]{1,0:T(8,128)(2,1)S(1)} %get-tuple-element.29), channel_id=1, source_target_pairs={{0,6},{1,7},{2,4},{3,5},{4,10},{5,11},{6,8},{7,9},{8,14},{9,15},{1... | collective-permute-start | bytes 786440 | tf_op jit(solution)/shard_map/ppermute | solution.py:31
  114.0 23.9 %collective-permute-start.20 = (bf16[128,1024]{1,0:T(8,128)(2,1)S(1)}, bf16[128,1024]{1,0:T(8,128)(2,1)S(1)}, u32[]{:S(2)}, u32[]{:S(2)}) collective-permute-start(bf16[128,1024]{1,0:T(8,128)(2,1)S(1)} %get-tuple-element.30), channel_id=1, source_target_pairs={{0,5},{1,4},{2,7},{3,6},{4,9},{5,8},{6,11},{7,10},{8,13},{9,12},{1... | collective-permute-start | bytes 786440 | tf_op jit(solution)/shard_map/ppermute | solution.py:31
  125.6 14.5 %collective-permute-start.21 = (bf16[128,1024]{1,0:T(8,128)(2,1)}, bf16[128,1024]{1,0:T(8,128)(2,1)}, u32[]{:S(2)}, u32[]{:S(2)}) collective-permute-start(bf16[128,1024]{1,0:T(8,128)(2,1)} %get-tuple-element.31), channel_id=1, source_target_pairs={{0,7},{1,6},{2,5},{3,4},{4,11},{5,10},{6,9},{7,8},{8,15},{9,14},{1... | collective-permute-start | bytes 786440 | tf_op jit(solution)/shard_map/ppermute | solution.py:31
  128.3 17.2 %collective-permute-start.26 = (bf16[128,1024]{1,0:T(8,128)(2,1)}, bf16[128,1024]{1,0:T(8,128)(2,1)}, u32[]{:S(2)}, u32[]{:S(2)}) collective-permute-start(bf16[128,1024]{1,0:T(8,128)(2,1)} %get-tuple-element.32), channel_id=1, source_target_pairs={{0,8},{1,9},{2,10},{3,11},{4,12},{5,13},{6,14},{7,15},{8,0},{9,1},... | collective-permute-start | bytes 786440 | tf_op jit(solution)/shard_map/ppermute | solution.py:31
  130.1 21.8 %collective-permute-start.27 = (bf16[128,1024]{1,0:T(8,128)(2,1)}, bf16[128,1024]{1,0:T(8,128)(2,1)}, u32[]{:S(2)}, u32[]{:S(2)}) collective-permute-start(bf16[128,1024]{1,0:T(8,128)(2,1)} %get-tuple-element.33), channel_id=1, source_target_pairs={{0,10},{1,11},{2,8},{3,9},{4,14},{5,15},{6,12},{7,13},{8,2},{9,3},... | collective-permute-start | bytes 786440 | tf_op jit(solution)/shard_map/ppermute | solution.py:31
  134.3 23.8 %collective-permute-start.28 = (bf16[128,1024]{1,0:T(8,128)(2,1)}, bf16[128,1024]{1,0:T(8,128)(2,1)}, u32[]{:S(2)}, u32[]{:S(2)}) collective-permute-start(bf16[128,1024]{1,0:T(8,128)(2,1)} %get-tuple-element.34), channel_id=1, source_target_pairs={{0,9},{1,8},{2,11},{3,10},{4,13},{5,12},{6,15},{7,14},{8,1},{9,0},... | collective-permute-start | bytes 786440 | tf_op jit(solution)/shard_map/ppermute | solution.py:31
  138.6 25.2 %collective-permute-start.29 = (bf16[128,1024]{1,0:T(8,128)(2,1)}, bf16[128,1024]{1,0:T(8,128)(2,1)}, u32[]{:S(2)}, u32[]{:S(2)}) collective-permute-start(bf16[128,1024]{1,0:T(8,128)(2,1)} %get-tuple-element.35), channel_id=1, source_target_pairs={{0,11},{1,10},{2,9},{3,8},{4,15},{5,14},{6,13},{7,12},{8,3},{9,2},... | collective-permute-start | bytes 786440 | tf_op jit(solution)/shard_map/ppermute | solution.py:31
  179.6 7.9 %collective-permute-start.32 = (bf16[16,3584]{1,0:T(8,128)(2,1)S(1)}, bf16[16,3584]{1,0:T(8,128)(2,1)S(1)}, u32[]{:S(2)}, u32[]{:S(2)}) collective-permute-start(bf16[16,3584]{1,0:T(8,128)(2,1)S(1)} %fusion.4), channel_id=1, source_target_pairs={{0,4},{1,5},{2,6},{3,7},{4,8},{5,9},{6,10},{7,11},{8,12},{9,13},{1... | collective-permute-start | bytes 344072 | tf_op jit(solution)/shard_map/ppermute | solution.py:31
  188.8 10.1 %collective-permute-start.35 = (bf16[16,3584]{1,0:T(8,128)(2,1)S(1)}, bf16[16,3584]{1,0:T(8,128)(2,1)S(1)}, u32[]{:S(2)}, u32[]{:S(2)}) collective-permute-start(bf16[16,3584]{1,0:T(8,128)(2,1)S(1)} %add_convert_fusion), channel_id=1, source_target_pairs={{0,113},{1,112},{2,115},{3,114},{4,117},{5,116},{6,119},{7,118},{8... | collective-permute-start | bytes 344072 | tf_op jit(solution)/shard_map/ppermute | solution.py:40
  (35 other events, 469.1 us)

commit v2 on v1

v2 whole, which is shorter than its diff:
```python
import functools

import jax
import jax.numpy as jnp
import numpy as np
from jax import lax
from jax.experimental import pallas as pl
from jax.experimental.pallas import tpu as pltpu
from jax.sharding import PartitionSpec as P

ROUTE_SCALE = 2.5
NX, NY, NC = 4, 2, 2
N_PIPE = 8
CUTS = 2
EXPERTS = NX * NY * NC
MIB = 1024 * 1024


def expert_at(x, y, c):
    return ((x % NX) * NY + y % NY) * NC + c % NC


def shift(dx, dy, dc):
    return [
        (expert_at(x, y, c), expert_at(x + dx, y + dy, c + dc))
        for x in range(NX)
        for y in range(NY)
        for c in range(NC)
    ]


def send(block, dx, dy, dc):
    return lax.ppermute(block, "expert", shift(dx, dy, dc))


def after(block, *earlier):
    return lax.optimization_barrier((block, *earlier))[0]


def send_mirror(block, dy, dc):
    route = [
        (p * EXPERTS + low, (N_PIPE - 1 - p) * EXPERTS + high)
        for p in range(N_PIPE)
        for low, high in shift(0, dy, dc)
    ]
    return lax.ppermute(block, ("pipe", "expert"), route)


def project_kernel(layout, depth_of, *refs):
    n, n_in = len(layout), sum(len(group) for group in layout)
    blocks, weights, outs = refs[:n_in], refs[n_in : n_in + NC], refs[n_in + NC : n_in + NC + n]
    tokens, held, stage, token_sem, weight_sem, out_sem = refs[n_in + NC + n :]
    tok = tokens.shape[0] // (2 * n)
    wide = held.shape[2]
    tiles = weights[0].shape[1] // wide

    def token_copy(slot, i):
        group = layout[i]
        if len(group) == 1:
            source = blocks[group[0]].at[pl.ds(slot * tok, tok)]
        else:
            source = blocks[group[slot]]
        target = tokens.at[pl.ds((slot * n + i) * tok, tok)]
        return pltpu.make_async_copy(source, target, token_sem.at[slot, i])

    def weight_copy(step, e):
        place = lax.rem(step, depth_of)
        return pltpu.make_async_copy(
            weights[e].at[step // tiles, pl.ds(lax.rem(step, tiles) * wide, wide)],
            held.at[place, e],
            weight_sem.at[place, e],
        )

    def out_copy(slot, i):
        return pltpu.make_async_copy(
            stage.at[slot, i], outs[i].at[:, pl.ds(slot * tok, tok)], out_sem.at[slot, i]
        )

    for i in range(n):
        token_copy(0, i).start()
    for e in range(NC):
        weight_copy(0, e).start()
    for i in range(n):
        token_copy(1, i).start()
    for step in range(1, depth_of):
        for e in range(NC):
            weight_copy(step, e).start()

    def body(step, carry):
        slot, tile = step // tiles, lax.rem(step, tiles)
        for s in range(2):

            @pl.when(step == s * tiles)
            def _(s=s):
                for i in range(n):
                    token_copy(s, i).wait()

        rows = pl.ds(pl.multiple_of(slot * n * tok, tok), n * tok)
        cols = pl.ds(pl.multiple_of(tile * wide, wide), wide)
        for e in range(NC):
            weight_copy(step, e).wait()
            made = lax.dot_general(
                tokens[rows, :],
                held[lax.rem(step, depth_of), e],
                (((1,), (1,)), ((), ())),
                preferred_element_type=jnp.float32,
            ).astype(jnp.bfloat16)
            for i in range(n):
                stage[slot, i, e, :, cols] = made[i * tok : (i + 1) * tok]

            @pl.when(step + depth_of < 2 * tiles)
            def _(e=e):
                weight_copy(step + depth_of, e).start()

        for s in range(2):

            @pl.when(step == (s + 1) * tiles - 1)
            def _(s=s):
                for i in range(n):
                    out_copy(s, i).start()

        return carry

    lax.fori_loop(0, 2 * tiles, body, 0)
    for s in range(2):
        for i in range(n):
            out_copy(s, i).wait()


def project(shards, own, sibling):
    layout, blocks = [], []
    for shard in shards:
        shard = shard if isinstance(shard, tuple) else (shard,)
        layout.append(tuple(range(len(blocks), len(blocks) + len(shard))))
        blocks += shard
    n = len(shards)
    _, hid, depth = own.shape
    tok = blocks[0].shape[0] // 2
    wide, depth_of = 512, 2
    anywhere = pl.BlockSpec(memory_space=pl.ANY)
    return pl.pallas_call(
        functools.partial(project_kernel, layout, depth_of),
        in_specs=[anywhere] * (len(blocks) + NC),
        out_specs=[anywhere] * n,
        out_shape=[jax.ShapeDtypeStruct((NC, 2 * tok, hid), jnp.bfloat16)] * n,
        scratch_shapes=[
            pltpu.VMEM((2 * n * tok, depth), jnp.bfloat16),
            pltpu.VMEM((depth_of, NC, wide, depth), jnp.bfloat16),
            pltpu.VMEM((2, n, NC, tok, hid), jnp.bfloat16),
            pltpu.SemaphoreType.DMA((2, n)),
            pltpu.SemaphoreType.DMA((depth_of, NC)),
            pltpu.SemaphoreType.DMA((2, n)),
        ],
        compiler_params=pltpu.CompilerParams(vmem_limit_bytes=48 * MIB),
        cost_estimate=pl.CostEstimate(
            flops=8 * n * tok * depth * hid,
            bytes_accessed=8 * hid * depth + 4 * n * tok * (depth + 2 * hid),
            transcendentals=0,
        ),
    )(*blocks, own, sibling)


def token_kernel(n, source, ids, probs, inputs, hidden, *refs):
    returned, (grad, part) = refs[:n], refs[n : n + 2]
    rows_in, hidden_in, inputs_in, grad_out, logits, row_sem, sems, out_sem = refs[n + 2 :]
    chunks, tok, top = hidden_in.shape[0], 16, 8
    span = rows_in.shape[1] // chunks
    half = rows_in.shape[1] // 2

    def row_copy(q, i):
        place = pl.ds(q * span, span)
        return pltpu.make_async_copy(
            returned[i].at[:, place], rows_in.at[pl.ds(NC * i, NC), place], row_sem.at[q, i]
        )

    def hidden_copy(q):
        source = hidden.at[pl.ds(q * span * top, span * top)]
        return pltpu.make_async_copy(source, hidden_in.at[q], sems.at[q])

    def out_copy(q):
        target = grad.at[pl.ds(q * span * top, span * top)]
        return pltpu.make_async_copy(grad_out.at[q], target, out_sem.at[q])

    inputs_copy = pltpu.make_async_copy(inputs, inputs_in, sems.at[chunks])
    for q in range(chunks):
        for i in range(n):
            row_copy(q, i).start()
        hidden_copy(q).start()
    inputs_copy.start()

    shape = (tok * top, EXPERTS * tok)
    mine = lax.broadcasted_iota(jnp.int32, shape, 0) // top == lax.broadcasted_iota(
        jnp.int32, shape, 1
    ) % tok
    for q in range(chunks):
        for i in range(n):
            row_copy(q, i).wait()
        hidden_copy(q).wait()
        for g in range(span // tok):
            first = q * span + g * tok
            at = slice(g * tok * top, (g + 1) * tok * top)
            rows = jnp.concatenate(
                [rows_in[e, first : first + tok, :] for e in range(EXPERTS)], axis=0
            )
            routes = ids[first * top : (first + tok) * top, :]
            pick = jnp.where(jnp.logical_and(mine, routes == source[...]), 1.0, 0.0)
            back = jnp.dot(pick.astype(jnp.bfloat16), rows, preferred_element_type=jnp.float32)
            dgate = jnp.sum(hidden_in[q, at, :].astype(jnp.float32) * back, axis=1, keepdims=True)
            dgate = dgate.reshape(tok, top, 1)
            member = routes.reshape(tok, top, 1) == lax.broadcasted_iota(
                jnp.int32, (tok, top, EXPERTS), 2
            )
            chosen = jnp.sum(
                jnp.where(member, probs[first : first + tok, :][:, None, :], 0.0),
                axis=2,
                keepdims=True,
            )
            total = jnp.sum(chosen, axis=1, keepdims=True)
            share = chosen / total
            weights = (ROUTE_SCALE * share).reshape(tok * top, 1)
            grad_out[q, at, :] = (weights * back).astype(jnp.bfloat16)
            centred = dgate - jnp.sum(share * dgate, axis=1, keepdims=True)
            selected = ROUTE_SCALE / total * centred * chosen * (1.0 - chosen)
            logits[first : first + tok, :] = jnp.sum(jnp.where(member, selected, 0.0), axis=1)
        out_copy(q).start()

    inputs_copy.wait()
    for s in range(2):
        logit = logits[s * half : (s + 1) * half, :]
        high = logit.astype(jnp.bfloat16)
        low = (logit - high.astype(jnp.float32)).astype(jnp.bfloat16)
        over = (((0,), (0,)), ((), ()))
        values = inputs_in[s * half : (s + 1) * half, :]
        made = lax.dot_general(high, values, over, preferred_element_type=jnp.float32)
        part[s] = made + lax.dot_general(low, values, over, preferred_element_type=jnp.float32)
    for q in range(chunks):
        out_copy(q).wait()


def token_math(source, ids, probs, inputs, hidden, returned):
    rows, depth = inputs.shape
    top, hid = 8, hidden.shape[1]
    n, chunks = len(returned), 4
    span = rows // chunks
    inside = pl.BlockSpec(memory_space=pltpu.VMEM)
    anywhere = pl.BlockSpec(memory_space=pl.ANY)
    return pl.pallas_call(
        functools.partial(token_kernel, n),
        in_specs=[inside] * 3 + [anywhere] * (2 + n),
        out_specs=[anywhere, inside],
        out_shape=[
            jax.ShapeDtypeStruct((rows * top, hid), jnp.bfloat16),
            jax.ShapeDtypeStruct((2, EXPERTS, depth), jnp.float32),
        ],
        scratch_shapes=[
            pltpu.VMEM((EXPERTS, rows, hid), jnp.bfloat16),
            pltpu.VMEM((chunks, span * top, hid), jnp.bfloat16),
            pltpu.VMEM((rows, depth), jnp.bfloat16),
            pltpu.VMEM((chunks, span * top, hid), jnp.bfloat16),
            pltpu.VMEM((rows, EXPERTS), jnp.float32),
            pltpu.SemaphoreType.DMA((chunks, n)),
            pltpu.SemaphoreType.DMA((chunks + 1,)),
            pltpu.SemaphoreType.DMA((chunks,)),
        ],
        compiler_params=pltpu.CompilerParams(vmem_limit_bytes=32 * MIB),
        cost_estimate=pl.CostEstimate(
            flops=2 * rows * top * hid * EXPERTS * 16,
            bytes_accessed=2 * rows * hid * (2 * top + EXPERTS),
            transcendentals=0,
        ),
    )(source, ids, probs, inputs, hidden, *returned)


def reduce_router(part, core):
    wide = jnp.float32
    narrow = jnp.bfloat16
    first = core == 0
    keep = jnp.where(first, part[0], part[1])
    give = jnp.where(first, part[1], part[0])
    pair = (keep + send(give, 0, 0, 1)).astype(narrow)
    low, high, far = send(pair, 1, 0, 0), send(pair, -1, 0, 0), send(pair, 2, 0, 0)
    line = (
        (pair.astype(wide) + far.astype(wide)) + (low.astype(wide) + high.astype(wide))
    ).astype(narrow)
    other = send(line, 0, 1, 0)
    mirror, mirror_other = send_mirror(line, 0, 1), send_mirror(line, 1, 1)
    total = (line.astype(wide) + other.astype(wide)) + (
        mirror.astype(wide) + mirror_other.astype(wide)
    )
    sibling = send(total, 0, 0, 1)
    return jnp.stack([jnp.where(first, total, sibling), jnp.where(first, sibling, total)])


def local(out_grad, saved_input, saved_hidden, expert_ids, down_weight, router_weight):
    tok, depth = out_grad.shape[2:]
    top, hid = saved_hidden.shape[3:]
    rows = 2 * tok
    me = lax.axis_index("expert")

    logits = jnp.einsum(
        "std,sed->ste", saved_input[0], router_weight[0], preferred_element_type=jnp.float32
    )
    probs = jax.nn.sigmoid(logits).reshape(rows, EXPERTS)
    ids = expert_ids.reshape(rows * top, 1)

    own = out_grad.reshape(rows, depth)
    weight = down_weight.reshape(2, hid, depth)

    across = send(own, 0, 1, 0)
    sibling_weight = send(weight, 0, 0, 1)
    first, second = out_grad[0, 0], out_grad[0, 1]
    low, high = [send(first, 1, 0, 0)], [send(second, -1, 0, 0)]
    far = send(low[0], 1, 0, 0), send(high[0], -1, 0, 0)
    low, high = (low[0], send(second, 1, 0, 0)), (send(first, -1, 0, 0), high[0])
    far_across = send(far[0], 0, 1, 0), send(far[1], 0, 1, 0)
    low_across, high_across = send(across, 1, 0, 0), send(across, -1, 0, 0)
    early = project([own, across, low, high, far], weight, sibling_weight)
    low_across = after(low_across, early[0])
    late = project([low_across, high_across, far_across], weight, sibling_weight)
    places = [(0, 0), (0, 1), (-1, 0), (1, 0), (2, 0), (-1, 1), (1, 1), (2, 1)]
    returned = []
    for i, ((dx, dy), made) in enumerate(zip(places, early + late)):
        if i >= len(early):
            made = after(made, returned[1])
        returned.append(send(made, dx, dy, 0) if dx or dy else made)
    table = np.array(
        [
            [
                expert_at(me // (NY * NC) - dx, me // NC % NY + dy, me % NC + dc)
                for dx, dy in places
                for dc in range(NC)
                for _ in range(16)
            ]
            for me in range(EXPERTS)
        ],
        np.int32,
    )
    marks = lax.dynamic_slice_in_dim(jnp.asarray(table), me, 1, 0)
    grad, part = token_math(
        marks, ids, probs, saved_input.reshape(rows, depth), saved_hidden.reshape(rows * top, hid), returned
    )
    return grad.reshape(saved_hidden.shape), reduce_router(part, lax.rem(me, NC))[None]


def solution(mesh):
    in_specs = (
        P("pipe", None, "expert", None),
        P("pipe", None, "expert", None),
        P("pipe", None, "expert", None, None),
        P("pipe", None, "expert", None),
        P("pipe", None, "expert", None, None),
        P("pipe", None, None, None),
    )
    out_specs = (P("pipe", None, "expert", None, None), P("pipe", None, None, None))
    return jax.shard_map(local, mesh=mesh, in_specs=in_specs, out_specs=out_specs, check_vma=False)
```

time: 205 us -> 155 us (0.76)
  starting transfers between devices: 60.6 us -> 43.5 us
  waiting for transfers between devices: 84.1 us -> 71.1 us
  local copies, waits for them, and re-layouts: 15.7 us -> 3.9 us
  Pallas kernels: 41.4 us -> 34.5 us
    ppermute x36 -> x25, starting transfers between devices: 55.1 us -> 35.9 us  [send(): return lax.ppermute(block, 'expert', shift(dx, dy, dc))]
    unnamed x59 -> x11, local copies, waits for them, and re-layouts: 15.2 us -> 1.7 us
    ppermute x36 -> x25, waiting for transfers between devices: 76.8 us -> 65 us  [send(): return lax.ppermute(block, 'expert', shift(dx, dy, dc))]
    pallas_call x5 -> x3, Pallas kernels: 41.4 us -> 34.5 us  [the longest x2 29.8 us: project(): pl.pallas_call(functools.partial(project_kernel, layout, depth_of), in_sp...]
    ppermute x2, starting transfers between devices: 5.5 us -> 7.64 us  [send_mirror(): return lax.ppermute(block, ('pipe', 'expert'), route)]
  transfers between devices with their start and end apart: 38 -> 27, of which waited for: 13 -> 16; matrix products, arithmetic and copies ran while one was open for 0% -> 2% of each run, Pallas kernels for 17% -> 19%
where the time goes in v2:
time: 155 us
  waiting for transfers between devices  71.1 us (46%)
  starting transfers between devices  43.5 us (28%)
  Pallas kernels  34.5 us (22%)
  local copies, waits for them, and re-layouts  3.9 us (3%)
    ppermute x25, waiting for transfers between devices, send(): return lax.ppermute(block, 'expert', shift(dx, dy, dc))  65 us
    ppermute x25, starting transfers between devices, send(): return lax.ppermute(block, 'expert', shift(dx, dy, dc))  35.9 us
    pallas_call x2, Pallas kernels, project(): pl.pallas_call(functools.partial(project_kernel, layout, depth_of), in_sp...  29.8 us
    ppermute x2, starting transfers between devices, send_mirror(): return lax.ppermute(block, ('pipe', 'expert'), route)  7.64 us
    ppermute x2, waiting for transfers between devices, send_mirror(): return lax.ppermute(block, ('pipe', 'expert'), route)  6.08 us
    pallas_call x1, Pallas kernels, token_math(): pl.pallas_call(functools.partial(token_kernel, n), in_specs=[inside] * 3...  4.71 us
  transfers between devices with their start and end apart: 27, of which 16 were waited for; matrix products, arithmetic and copies ran while one was open for 2% of the time, Pallas kernels for 19%

profile of v2, /device:TPU:1, one launch (start us, length us, event | category | flops | bytes accessed | tf_op | source)
XLA Modules:
  0.0 155.1 jit_solution(1178913301450570191)
XLA Ops:
  0.6 1.5 collective-permute-start.7
  2.1 3.0 %collective-permute-start = (bf16[128,3584]{1,0:T(8,128)(2,1)}, bf16[128,3584]{1,0:T(8,128)(2,1)S(1)}, u32[]{:S(2)}, u32[]{:S(2)}) collective-permute-start(bf16[128,3584]{1,0:T(8,128)(2,1)} %bitcast.36), channel_id=1, source_target_pairs={{0,2},{1,3},{2,0},{3,1},{4,6},{5,7},{6,4},{7,5},{8,10},{9,11},{10,... | collective-permute-start | bytes 2752520 | tf_op jit(solution)/shard_map/ppermute | solution.py:33
  5.2 1.2 slice_bitcast_fusion
  6.4 1.3 collective-permute-start.1
  7.7 1.5 collective-permute-start.4
  9.1 10.3 %collective-permute-done.1.refs_2_ = bf16[64,3584]{1,0:T(8,128)(2,1)S(1)} collective-permute-done((bf16[64,3584]{1,0:T(8,128)(2,1)S(1)}, bf16[64,3584]{1,0:T(8,128)(2,1)S(1)}, u32[]{:S(2)}, u32[]{:S(2)}) %collective-permute-start.1) | collective-permute-done | bytes 458784 | tf_op jit(solution)/shard_map/ppermute | solution.py:33
  19.4 1.3 collective-permute-start.3
  20.9 8.4 %collective-permute-done.2.refs_3_ = bf16[64,3584]{1,0:T(8,128)(2,1)S(1)} collective-permute-done((bf16[64,3584]{1,0:T(8,128)(2,1)S(1)}, bf16[64,3584]{1,0:T(8,128)(2,1)S(1)}, u32[]{:S(2)}, u32[]{:S(2)}) %collective-permute-start.2) | collective-permute-done | bytes 458784 | tf_op jit(solution)/shard_map/ppermute | solution.py:33
  29.2 1.3 collective-permute-start.6
  30.7 2.5 %collective-permute-start.13 = (bf16[128,3584]{1,0:T(8,128)(2,1)S(1)}, bf16[128,3584]{1,0:T(8,128)(2,1)S(1)}, u32[]{:S(2)}, u32[]{:S(2)}) collective-permute-start(bf16[128,3584]{1,0:T(8,128)(2,1)S(1)} %collective-permute-done.refs_1_), channel_id=1, source_target_pairs={{0,12},{1,13},{2,14},{3,15},{4,0},{5,1},{6,2},{7,3},{8,4},{9,5},{1... | collective-permute-start | bytes 2752520 | tf_op jit(solution)/shard_map/ppermute | solution.py:33
  33.2 5.9 %collective-permute-done.5.refs_6_ = bf16[64,3584]{1,0:T(8,128)(2,1)S(1)} collective-permute-done((bf16[64,3584]{1,0:T(8,128)(2,1)S(1)}, bf16[64,3584]{1,0:T(8,128)(2,1)S(1)}, u32[]{:S(2)}, u32[]{:S(2)}) %collective-permute-start.5) | collective-permute-done | bytes 458784 | tf_op jit(solution)/shard_map/ppermute | solution.py:33
  39.3 2.8 %collective-permute-start.15 = (bf16[64,3584]{1,0:T(8,128)(2,1)S(1)}, bf16[64,3584]{1,0:T(8,128)(2,1)S(1)}, u32[]{:S(2)}, u32[]{:S(2)}) collective-permute-start(bf16[64,3584]{1,0:T(8,128)(2,1)S(1)} %collective-permute-done.6.refs_7_), channel_id=1, source_target_pairs={{0,2},{1,3},{2,0},{3,1},{4,6},{5,7},{6,4},{7,5},{8,10},{9,11},{10,... | collective-permute-start | bytes 1376264 | tf_op jit(solution)/shard_map/ppermute | solution.py:33
  42.0 15.1 %shard_map.86 = (bf16[2,128,1024]{2,1,0:T(8,128)(2,1)S(1)}, bf16[2,128,1024]{2,1,0:T(8,128)(2,1)S(1)}, bf16[2,128,1024]{2,1,0:T(8,128)(2,1)}, bf16[2,128,1024]{2,1,0:T(8,128)(2,1)S(1)}, bf16[2,128,1024]{2,1,0:T(8,128)(2,1)}) custom-call(bf16[128,3584]{1,0:T(8,128)(2,1)} %bitcast.37, bf16[128,3584]{1,0:T(8,128)(2,1)} %copy-done.4, ...), custom_call_target="tpu_custom_call" | custom-call | flops 9395240960 | bytes 36569088 | tf_op jit(solution)/shard_map/pallas_call | solution.py:141
  57.2 1.5 collective-permute-done.12.refs_0_
  58.8 2.5 %collective-permute-start.11 = (bf16[2,128,1024]{2,1,0:T(8,128)(2,1)}, bf16[2,128,1024]{2,1,0:T(8,128)(2,1)}, u32[]{:S(2)}, u32[]{:S(2)}) collective-permute-start(bf16[2,128,1024]{2,1,0:T(8,128)(2,1)} %get-tuple-element.20), channel_id=1, source_target_pairs={{0,8},{1,9},{2,10},{3,11},{4,12},{5,13},{6,14},{7,15},{8,0},{9,1},... | collective-permute-start | bytes 1572872 | tf_op jit(solution)/shard_map/ppermute | solution.py:33
  61.2 1.2 collective-permute-start.9
  62.4 14.6 %shard_map.87 = (bf16[2,128,1024]{2,1,0:T(8,128)(2,1)}, bf16[2,128,1024]{2,1,0:T(8,128)(2,1)}, bf16[2,128,1024]{2,1,0:T(8,128)(2,1)}) custom-call(bf16[128,3584]{1,0:T(8,128)(2,1)S(1)} %collective-permute-done.12.refs_0_, bf16[128,3584]{1,0:T(8,128)(2,1)S(1)} %collective-permute-done.13.refs_1_, bf16[64,3584]{1,0:T(8,128)(2,1)S(1)} %collective-permute-done.14.refs_2_, ...), custom_call_target="tpu_custom_call" | custom-call | flops 5637144576 | bytes 33685504 | tf_op jit(solution)/shard_map/pallas_call | solution.py:141
  77.0 4.1 %collective-permute-start.18 = (bf16[2,128,1024]{2,1,0:T(8,128)(2,1)}, bf16[2,128,1024]{2,1,0:T(8,128)(2,1)}, u32[]{:S(2)}, u32[]{:S(2)}) collective-permute-start(bf16[2,128,1024]{2,1,0:T(8,128)(2,1)} %get-tuple-element.27), channel_id=1, source_target_pairs={{0,10},{1,11},{2,8},{3,9},{4,14},{5,15},{6,12},{7,13},{8,2},{9,3},... | collective-permute-start | bytes 1572872 | tf_op jit(solution)/shard_map/ppermute | solution.py:33
  81.2 5.1 %collective-permute-start.16 = (bf16[2,128,1024]{2,1,0:T(8,128)(2,1)}, bf16[2,128,1024]{2,1,0:T(8,128)(2,1)}, u32[]{:S(2)}, u32[]{:S(2)}) collective-permute-start(bf16[2,128,1024]{2,1,0:T(8,128)(2,1)} %get-tuple-element.23), channel_id=1, source_target_pairs={{0,14},{1,15},{2,12},{3,13},{4,2},{5,3},{6,0},{7,1},{8,6},{9,7},{1... | collective-permute-start | bytes 1572872 | tf_op jit(solution)/shard_map/ppermute | solution.py:33
  87.9 7.5 %collective-permute-done.18.refs_7_ = bf16[2,128,1024]{2,1,0:T(8,128)(2,1)} collective-permute-done((bf16[2,128,1024]{2,1,0:T(8,128)(2,1)}, bf16[2,128,1024]{2,1,0:T(8,128)(2,1)}, u32[]{:S(2)}, u32[]{:S(2)}) %collective-permute-start.18) | collective-permute-done | bytes 524320 | tf_op jit(solution)/shard_map/ppermute | solution.py:33
  95.4 22.4 %collective-permute-done.17.refs_6_ = bf16[2,128,1024]{2,1,0:T(8,128)(2,1)} collective-permute-done((bf16[2,128,1024]{2,1,0:T(8,128)(2,1)}, bf16[2,128,1024]{2,1,0:T(8,128)(2,1)}, u32[]{:S(2)}, u32[]{:S(2)}) %collective-permute-start.17) | collective-permute-done | bytes 524320 | tf_op jit(solution)/shard_map/ppermute | solution.py:33
  118.9 1.6 %copy-done.2 = bf16[1,2,64,8,1024]{4,3,2,1,0:T(8,128)(2,1)S(1)} copy-done((bf16[1,2,64,8,1024]{4,3,2,1,0:T(8,128)(2,1)S(1)}, bf16[1,2,64,8,1024]{4,3,2,1,0:T(8,128)(2,1)}, u32[]{:S(2)}) %copy-start.2) | copy-done | bytes 2097176
  120.5 4.7 %shard_map.88 = (bf16[1024,1024]{1,0:T(8,128)(2,1)}, f32[2,16,3584]{2,1,0:T(8,128)S(1)}) custom-call(s32[1,256]{1,0:T(1,128)S(1)} %constant_dynamic-slice_fusion.source, s32[1024,1]{1,0:T(8,128)S(1)} %reshape.36.ids, f32[128,16]{1,0:T(8,128)S(1)} %bitcast.32, bf16[128,3584]{1,0:T(8,128)(2,1)S(1)} %bitcast.30, bf16[1024,1024]{1,0:T(8,128)(2,1)S(1)} %bitcast.31, ...), custom_call_target="tpu_custom_call" | custom-call | flops 536870912 | bytes 8388608 | tf_op jit(solution)/shard_map/pallas_call | solution.py:247
  125.3 3.2 %collective-permute-start.19 = (f32[16,3584]{1,0:T(8,128)S(1)}, f32[16,3584]{1,0:T(8,128)S(1)}, u32[]{:S(2)}, u32[]{:S(2)}) collective-permute-start(f32[16,3584]{1,0:T(8,128)S(1)} %select_bitcast_fusion.2), channel_id=1, source_target_pairs={{0,1},{1,0},{2,3},{3,2},{4,5},{5,4},{6,7},{7,6},{8,9},{9,8},{10,11... | collective-permute-start | bytes 688136 | tf_op jit(solution)/shard_map/ppermute | solution.py:33
  130.0 3.4 %collective-permute-start.21 = (bf16[16,3584]{1,0:T(8,128)(2,1)S(1)}, bf16[16,3584]{1,0:T(8,128)(2,1)S(1)}, u32[]{:S(2)}, u32[]{:S(2)}) collective-permute-start(bf16[16,3584]{1,0:T(8,128)(2,1)S(1)} %fusion.4), channel_id=1, source_target_pairs={{0,4},{1,5},{2,6},{3,7},{4,8},{5,9},{6,10},{7,11},{8,12},{9,13},{1... | collective-permute-start | bytes 344072 | tf_op jit(solution)/shard_map/ppermute | solution.py:33
  133.8 1.7 %collective-permute-done.20 = bf16[16,3584]{1,0:T(8,128)(2,1)S(1)} collective-permute-done((bf16[16,3584]{1,0:T(8,128)(2,1)S(1)}, bf16[16,3584]{1,0:T(8,128)(2,1)S(1)}, u32[]{:S(2)}, u32[]{:S(2)}) %collective-permute-start.20) | collective-permute-done | bytes 114720 | tf_op jit(solution)/shard_map/ppermute | solution.py:33
  135.5 3.2 %collective-permute-done.21 = bf16[16,3584]{1,0:T(8,128)(2,1)S(1)} collective-permute-done((bf16[16,3584]{1,0:T(8,128)(2,1)S(1)}, bf16[16,3584]{1,0:T(8,128)(2,1)S(1)}, u32[]{:S(2)}, u32[]{:S(2)}) %collective-permute-start.21) | collective-permute-done | bytes 114720 | tf_op jit(solution)/shard_map/ppermute | solution.py:33
  138.9 6.2 %collective-permute-start.24 = (bf16[16,3584]{1,0:T(8,128)(2,1)S(1)}, bf16[16,3584]{1,0:T(8,128)(2,1)S(1)}, u32[]{:S(2)}, u32[]{:S(2)}) collective-permute-start(bf16[16,3584]{1,0:T(8,128)(2,1)S(1)} %add_convert_fusion), channel_id=1, source_target_pairs={{0,113},{1,112},{2,115},{3,114},{4,117},{5,116},{6,119},{7,118},{8... | collective-permute-start | bytes 344072 | tf_op jit(solution)/shard_map/ppermute | solution.py:46
  145.1 1.5 collective-permute-start.25
  146.6 3.0 %collective-permute-done.24 = bf16[16,3584]{1,0:T(8,128)(2,1)S(1)} collective-permute-done((bf16[16,3584]{1,0:T(8,128)(2,1)S(1)}, bf16[16,3584]{1,0:T(8,128)(2,1)S(1)}, u32[]{:S(2)}, u32[]{:S(2)}) %collective-permute-start.24) | collective-permute-done | bytes 114720 | tf_op jit(solution)/shard_map/ppermute | solution.py:46
  149.6 3.0 %collective-permute-done.25 = bf16[16,3584]{1,0:T(8,128)(2,1)S(1)} collective-permute-done((bf16[16,3584]{1,0:T(8,128)(2,1)S(1)}, bf16[16,3584]{1,0:T(8,128)(2,1)S(1)}, u32[]{:S(2)}, u32[]{:S(2)}) %collective-permute-start.25) | collective-permute-done | bytes 114720 | tf_op jit(solution)/shard_map/ppermute | solution.py:46
  152.8 1.5 collective-permute-done.26
  (47 shorter events, 6.5 us)
Async XLA Ops:
  0.6 85.9 %copy-start = (bf16[1,2,16,3584]{3,2,1,0:T(8,128)(2,1)S(1)}, bf16[1,2,16,3584]{3,2,1,0:T(8,128)(2,1)}, u32[]{:S(2)}) copy-start(bf16[1,2,16,3584]{3,2,1,0:T(8,128)(2,1)} %param.12) | copy-start | bytes 688132
  0.6 41.4 %collective-permute-start.7 = (bf16[2,1024,3584]{2,1,0:T(8,128)(2,1)}, bf16[2,1024,3584]{2,1,0:T(8,128)(2,1)}, u32[]{:S(2)}, u32[]{:S(2)}) collective-permute-start(bf16[2,1024,3584]{2,1,0:T(8,128)(2,1)} %bitcast.33), channel_id=1, source_target_pairs={{0,1},{1,0},{2,3},{3,2},{4,5},{5,4},{6,7},{7,6},{8,9},{9,8},{10,11... | collective-permute-start | bytes 44040200 | tf_op jit(solution)/shard_map/ppermute | solution.py:33
  2.1 28.4 %collective-permute-start = (bf16[128,3584]{1,0:T(8,128)(2,1)}, bf16[128,3584]{1,0:T(8,128)(2,1)S(1)}, u32[]{:S(2)}, u32[]{:S(2)}) collective-permute-start(bf16[128,3584]{1,0:T(8,128)(2,1)} %bitcast.36), channel_id=1, source_target_pairs={{0,2},{1,3},{2,0},{3,1},{4,6},{5,7},{6,4},{7,5},{8,10},{9,11},{10,... | collective-permute-start | bytes 2752520 | tf_op jit(solution)/shard_map/ppermute | solution.py:33
  6.4 13.0 %collective-permute-start.1 = (bf16[64,3584]{1,0:T(8,128)(2,1)S(1)}, bf16[64,3584]{1,0:T(8,128)(2,1)S(1)}, u32[]{:S(2)}, u32[]{:S(2)}) collective-permute-start(bf16[64,3584]{1,0:T(8,128)(2,1)S(1)} %get-tuple-element.31), channel_id=1, source_target_pairs={{0,4},{1,5},{2,6},{3,7},{4,8},{5,9},{6,10},{7,11},{8,12},{9,13},{1... | collective-permute-start | bytes 1376264 | tf_op jit(solution)/shard_map/ppermute | solution.py:33
  7.7 13.0 %collective-permute-start.4 = (bf16[64,3584]{1,0:T(8,128)(2,1)S(1)}, bf16[64,3584]{1,0:T(8,128)(2,1)S(1)}, u32[]{:S(2)}, u32[]{:S(2)}) collective-permute-start(bf16[64,3584]{1,0:T(8,128)(2,1)S(1)} %get-tuple-element.30), channel_id=1, source_target_pairs={{0,12},{1,13},{2,14},{3,15},{4,0},{5,1},{6,2},{7,3},{8,4},{9,5},{1... | collective-permute-start | bytes 1376264 | tf_op jit(solution)/shard_map/ppermute | solution.py:33
  9.1 20.1 %collective-permute-start.2 = (bf16[64,3584]{1,0:T(8,128)(2,1)S(1)}, bf16[64,3584]{1,0:T(8,128)(2,1)S(1)}, u32[]{:S(2)}, u32[]{:S(2)}) collective-permute-start(bf16[64,3584]{1,0:T(8,128)(2,1)S(1)} %get-tuple-element.30), channel_id=1, source_target_pairs={{0,4},{1,5},{2,6},{3,7},{4,8},{5,9},{6,10},{7,11},{8,12},{9,13},{1... | collective-permute-start | bytes 1376264 | tf_op jit(solution)/shard_map/ppermute | solution.py:33
  19.4 11.3 %collective-permute-start.3 = (bf16[64,3584]{1,0:T(8,128)(2,1)S(1)}, bf16[64,3584]{1,0:T(8,128)(2,1)S(1)}, u32[]{:S(2)}, u32[]{:S(2)}) collective-permute-start(bf16[64,3584]{1,0:T(8,128)(2,1)S(1)} %get-tuple-element.31), channel_id=1, source_target_pairs={{0,12},{1,13},{2,14},{3,15},{4,0},{5,1},{6,2},{7,3},{8,4},{9,5},{1... | collective-permute-start | bytes 1376264 | tf_op jit(solution)/shard_map/ppermute | solution.py:33
  20.7 18.4 %collective-permute-start.5 = (bf16[64,3584]{1,0:T(8,128)(2,1)S(1)}, bf16[64,3584]{1,0:T(8,128)(2,1)S(1)}, u32[]{:S(2)}, u32[]{:S(2)}) collective-permute-start(bf16[64,3584]{1,0:T(8,128)(2,1)S(1)} %collective-permute-done.1.refs_2_), channel_id=1, source_target_pairs={{0,4},{1,5},{2,6},{3,7},{4,8},{5,9},{6,10},{7,11},{8,12},{9,13},{1... | collective-permute-start | bytes 1376264 | tf_op jit(solution)/shard_map/ppermute | solution.py:33
  29.2 10.0 %collective-permute-start.6 = (bf16[64,3584]{1,0:T(8,128)(2,1)S(1)}, bf16[64,3584]{1,0:T(8,128)(2,1)S(1)}, u32[]{:S(2)}, u32[]{:S(2)}) collective-permute-start(bf16[64,3584]{1,0:T(8,128)(2,1)S(1)} %collective-permute-done.4.refs_5_), channel_id=1, source_target_pairs={{0,12},{1,13},{2,14},{3,15},{4,0},{5,1},{6,2},{7,3},{8,4},{9,5},{1... | collective-permute-start | bytes 1376264 | tf_op jit(solution)/shard_map/ppermute | solution.py:33
  30.5 11.5 %copy-start.4 = (bf16[128,3584]{1,0:T(8,128)(2,1)}, bf16[128,3584]{1,0:T(8,128)(2,1)S(1)}, u32[]{:S(2)}) copy-start(bf16[128,3584]{1,0:T(8,128)(2,1)S(1)} %collective-permute-done.refs_1_) | copy-start | bytes 2752516
  30.5 28.2 %collective-permute-start.12 = (bf16[128,3584]{1,0:T(8,128)(2,1)S(1)}, bf16[128,3584]{1,0:T(8,128)(2,1)S(1)}, u32[]{:S(2)}, u32[]{:S(2)}) collective-permute-start(bf16[128,3584]{1,0:T(8,128)(2,1)S(1)} %collective-permute-done.refs_1_), channel_id=1, source_target_pairs={{0,4},{1,5},{2,6},{3,7},{4,8},{5,9},{6,10},{7,11},{8,12},{9,13},{1... | collective-permute-start | bytes 2752520 | tf_op jit(solution)/shard_map/ppermute | solution.py:33
  30.7 31.7 %collective-permute-start.13 = (bf16[128,3584]{1,0:T(8,128)(2,1)S(1)}, bf16[128,3584]{1,0:T(8,128)(2,1)S(1)}, u32[]{:S(2)}, u32[]{:S(2)}) collective-permute-start(bf16[128,3584]{1,0:T(8,128)(2,1)S(1)} %collective-permute-done.refs_1_), channel_id=1, source_target_pairs={{0,12},{1,13},{2,14},{3,15},{4,0},{5,1},{6,2},{7,3},{8,4},{9,5},{1... | collective-permute-start | bytes 2752520 | tf_op jit(solution)/shard_map/ppermute | solution.py:33
  39.1 19.7 %collective-permute-start.14 = (bf16[64,3584]{1,0:T(8,128)(2,1)S(1)}, bf16[64,3584]{1,0:T(8,128)(2,1)S(1)}, u32[]{:S(2)}, u32[]{:S(2)}) collective-permute-start(bf16[64,3584]{1,0:T(8,128)(2,1)S(1)} %collective-permute-done.5.refs_6_), channel_id=1, source_target_pairs={{0,2},{1,3},{2,0},{3,1},{4,6},{5,7},{6,4},{7,5},{8,10},{9,11},{10,... | collective-permute-start | bytes 1376264 | tf_op jit(solution)/shard_map/ppermute | solution.py:33
  39.3 22.0 %collective-permute-start.15 = (bf16[64,3584]{1,0:T(8,128)(2,1)S(1)}, bf16[64,3584]{1,0:T(8,128)(2,1)S(1)}, u32[]{:S(2)}, u32[]{:S(2)}) collective-permute-start(bf16[64,3584]{1,0:T(8,128)(2,1)S(1)} %collective-permute-done.6.refs_7_), channel_id=1, source_target_pairs={{0,2},{1,3},{2,0},{3,1},{4,6},{5,7},{6,4},{7,5},{8,10},{9,11},{10,... | collective-permute-start | bytes 1376264 | tf_op jit(solution)/shard_map/ppermute | solution.py:33
  58.7 18.3 %collective-permute-start.8 = (bf16[2,128,1024]{2,1,0:T(8,128)(2,1)S(1)}, bf16[2,128,1024]{2,1,0:T(8,128)(2,1)S(1)}, u32[]{:S(2)}, u32[]{:S(2)}) collective-permute-start(bf16[2,128,1024]{2,1,0:T(8,128)(2,1)S(1)} %get-tuple-element.17), channel_id=1, source_target_pairs={{0,2},{1,3},{2,0},{3,1},{4,6},{5,7},{6,4},{7,5},{8,10},{9,11},{10,... | collective-permute-start | bytes 1572872 | tf_op jit(solution)/shard_map/ppermute | solution.py:33
  58.7 22.5 %collective-permute-start.10 = (bf16[2,128,1024]{2,1,0:T(8,128)(2,1)S(1)}, bf16[2,128,1024]{2,1,0:T(8,128)(2,1)S(1)}, u32[]{:S(2)}, u32[]{:S(2)}) collective-permute-start(bf16[2,128,1024]{2,1,0:T(8,128)(2,1)S(1)} %get-tuple-element.19), channel_id=1, source_target_pairs={{0,4},{1,5},{2,6},{3,7},{4,8},{5,9},{6,10},{7,11},{8,12},{9,13},{1... | collective-permute-start | bytes 1572872 | tf_op jit(solution)/shard_map/ppermute | solution.py:33
  58.8 28.9 %collective-permute-start.11 = (bf16[2,128,1024]{2,1,0:T(8,128)(2,1)}, bf16[2,128,1024]{2,1,0:T(8,128)(2,1)}, u32[]{:S(2)}, u32[]{:S(2)}) collective-permute-start(bf16[2,128,1024]{2,1,0:T(8,128)(2,1)} %get-tuple-element.20), channel_id=1, source_target_pairs={{0,8},{1,9},{2,10},{3,11},{4,12},{5,13},{6,14},{7,15},{8,0},{9,1},... | collective-permute-start | bytes 1572872 | tf_op jit(solution)/shard_map/ppermute | solution.py:33
  61.2 25.0 %copy-start.3 = (s32[1,2,64,8]{2,3,1,0:T(8,128)S(1)}, s32[1,2,64,8]{2,3,1,0:T(8,128)}, u32[]{:S(2)}) copy-start(s32[1,2,64,8]{2,3,1,0:T(8,128)} %param.10) | copy-start | bytes 12292
  61.2 25.3 %copy-start.1 = (bf16[1,2,64,3584]{3,2,1,0:T(8,128)(2,1)S(1)}, bf16[1,2,64,3584]{3,2,1,0:T(8,128)(2,1)}, u32[]{:S(2)}) copy-start(bf16[1,2,64,3584]{3,2,1,0:T(8,128)(2,1)} %param.8) | copy-start | bytes 2752516
  61.2 26.6 %collective-permute-start.9 = (bf16[2,128,1024]{2,1,0:T(8,128)(2,1)}, bf16[2,128,1024]{2,1,0:T(8,128)(2,1)}, u32[]{:S(2)}, u32[]{:S(2)}) collective-permute-start(bf16[2,128,1024]{2,1,0:T(8,128)(2,1)} %get-tuple-element.18), channel_id=1, source_target_pairs={{0,12},{1,13},{2,14},{3,15},{4,0},{5,1},{6,2},{7,3},{8,4},{9,5},{1... | collective-permute-start | bytes 1572872 | tf_op jit(solution)/shard_map/ppermute | solution.py:33
  77.0 18.4 %collective-permute-start.18 = (bf16[2,128,1024]{2,1,0:T(8,128)(2,1)}, bf16[2,128,1024]{2,1,0:T(8,128)(2,1)}, u32[]{:S(2)}, u32[]{:S(2)}) collective-permute-start(bf16[2,128,1024]{2,1,0:T(8,128)(2,1)} %get-tuple-element.27), channel_id=1, source_target_pairs={{0,10},{1,11},{2,8},{3,9},{4,14},{5,15},{6,12},{7,13},{8,2},{9,3},... | collective-permute-start | bytes 1572872 | tf_op jit(solution)/shard_map/ppermute | solution.py:33
  81.2 36.7 %collective-permute-start.17 = (bf16[2,128,1024]{2,1,0:T(8,128)(2,1)}, bf16[2,128,1024]{2,1,0:T(8,128)(2,1)}, u32[]{:S(2)}, u32[]{:S(2)}) collective-permute-start(bf16[2,128,1024]{2,1,0:T(8,128)(2,1)} %get-tuple-element.25), channel_id=1, source_target_pairs={{0,6},{1,7},{2,4},{3,5},{4,10},{5,11},{6,8},{7,9},{8,14},{9,15},{1... | collective-permute-start | bytes 1572872 | tf_op jit(solution)/shard_map/ppermute | solution.py:33
  81.2 37.7 %collective-permute-start.16 = (bf16[2,128,1024]{2,1,0:T(8,128)(2,1)}, bf16[2,128,1024]{2,1,0:T(8,128)(2,1)}, u32[]{:S(2)}, u32[]{:S(2)}) collective-permute-start(bf16[2,128,1024]{2,1,0:T(8,128)(2,1)} %get-tuple-element.23), channel_id=1, source_target_pairs={{0,14},{1,15},{2,12},{3,13},{4,2},{5,3},{6,0},{7,1},{8,6},{9,7},{1... | collective-permute-start | bytes 1572872 | tf_op jit(solution)/shard_map/ppermute | solution.py:33
  118.9 1.6 %copy-start.2 = (bf16[1,2,64,8,1024]{4,3,2,1,0:T(8,128)(2,1)S(1)}, bf16[1,2,64,8,1024]{4,3,2,1,0:T(8,128)(2,1)}, u32[]{:S(2)}) copy-start(bf16[1,2,64,8,1024]{4,3,2,1,0:T(8,128)(2,1)} %param.9) | copy-start | bytes 6291460
  125.3 4.3 %collective-permute-start.19 = (f32[16,3584]{1,0:T(8,128)S(1)}, f32[16,3584]{1,0:T(8,128)S(1)}, u32[]{:S(2)}, u32[]{:S(2)}) collective-permute-start(f32[16,3584]{1,0:T(8,128)S(1)} %select_bitcast_fusion.2), channel_id=1, source_target_pairs={{0,1},{1,0},{2,3},{3,2},{4,5},{5,4},{6,7},{7,6},{8,9},{9,8},{10,11... | collective-permute-start | bytes 688136 | tf_op jit(solution)/shard_map/ppermute | solution.py:33
  129.6 5.9 %collective-permute-start.20 = (bf16[16,3584]{1,0:T(8,128)(2,1)S(1)}, bf16[16,3584]{1,0:T(8,128)(2,1)S(1)}, u32[]{:S(2)}, u32[]{:S(2)}) collective-permute-start(bf16[16,3584]{1,0:T(8,128)(2,1)S(1)} %fusion.4), channel_id=1, source_target_pairs={{0,8},{1,9},{2,10},{3,11},{4,12},{5,13},{6,14},{7,15},{8,0},{9,1},... | collective-permute-start | bytes 344072 | tf_op jit(solution)/shard_map/ppermute | solution.py:33
  130.0 8.7 %collective-permute-start.21 = (bf16[16,3584]{1,0:T(8,128)(2,1)S(1)}, bf16[16,3584]{1,0:T(8,128)(2,1)S(1)}, u32[]{:S(2)}, u32[]{:S(2)}) collective-permute-start(bf16[16,3584]{1,0:T(8,128)(2,1)S(1)} %fusion.4), channel_id=1, source_target_pairs={{0,4},{1,5},{2,6},{3,7},{4,8},{5,9},{6,10},{7,11},{8,12},{9,13},{1... | collective-permute-start | bytes 344072 | tf_op jit(solution)/shard_map/ppermute | solution.py:33
  133.4 5.4 %collective-permute-start.22 = (bf16[16,3584]{1,0:T(8,128)(2,1)S(1)}, bf16[16,3584]{1,0:T(8,128)(2,1)S(1)}, u32[]{:S(2)}, u32[]{:S(2)}) collective-permute-start(bf16[16,3584]{1,0:T(8,128)(2,1)S(1)} %fusion.4), channel_id=1, source_target_pairs={{0,12},{1,13},{2,14},{3,15},{4,0},{5,1},{6,2},{7,3},{8,4},{9,5},{1... | collective-permute-start | bytes 344072 | tf_op jit(solution)/shard_map/ppermute | solution.py:33
  138.8 7.7 %collective-permute-start.23 = (bf16[16,3584]{1,0:T(8,128)(2,1)S(1)}, bf16[16,3584]{1,0:T(8,128)(2,1)S(1)}, u32[]{:S(2)}, u32[]{:S(2)}) collective-permute-start(bf16[16,3584]{1,0:T(8,128)(2,1)S(1)} %add_convert_fusion), channel_id=1, source_target_pairs={{0,2},{1,3},{2,0},{3,1},{4,6},{5,7},{6,4},{7,5},{8,10},{9,11},{10,... | collective-permute-start | bytes 344072 | tf_op jit(solution)/shard_map/ppermute | solution.py:33
  138.9 10.7 %collective-permute-start.24 = (bf16[16,3584]{1,0:T(8,128)(2,1)S(1)}, bf16[16,3584]{1,0:T(8,128)(2,1)S(1)}, u32[]{:S(2)}, u32[]{:S(2)}) collective-permute-start(bf16[16,3584]{1,0:T(8,128)(2,1)S(1)} %add_convert_fusion), channel_id=1, source_target_pairs={{0,113},{1,112},{2,115},{3,114},{4,117},{5,116},{6,119},{7,118},{8... | collective-permute-start | bytes 344072 | tf_op jit(solution)/shard_map/ppermute | solution.py:46
  145.1 7.5 %collective-permute-start.25 = (bf16[16,3584]{1,0:T(8,128)(2,1)S(1)}, bf16[16,3584]{1,0:T(8,128)(2,1)S(1)}, u32[]{:S(2)}, u32[]{:S(2)}) collective-permute-start(bf16[16,3584]{1,0:T(8,128)(2,1)S(1)} %add_convert_fusion), channel_id=1, source_target_pairs={{0,115},{1,114},{2,113},{3,112},{4,119},{5,118},{6,117},{7,116},{8... | collective-permute-start | bytes 344072 | tf_op jit(solution)/shard_map/ppermute | solution.py:46
  152.7 1.6 %collective-permute-start.26 = (f32[16,3584]{1,0:T(8,128)S(1)}, f32[16,3584]{1,0:T(8,128)S(1)}, u32[]{:S(2)}, u32[]{:S(2)}) collective-permute-start(f32[16,3584]{1,0:T(8,128)S(1)} %add_add_fusion), channel_id=1, source_target_pairs={{0,1},{1,0},{2,3},{3,2},{4,5},{5,4},{6,7},{7,6},{8,9},{9,8},{10,11... | collective-permute-start | bytes 688136 | tf_op jit(solution)/shard_map/ppermute | solution.py:33

commit v3 on v2

--- a/solution.py
+++ b/solution.py
@@ -160,53 +160,34 @@
     )(*blocks, own, sibling)
 
 
-def token_kernel(n, source, ids, probs, inputs, hidden, *refs):
-    returned, (grad, part) = refs[:n], refs[n : n + 2]
-    rows_in, hidden_in, inputs_in, grad_out, logits, row_sem, sems, out_sem = refs[n + 2 :]
-    chunks, tok, top = hidden_in.shape[0], 16, 8
-    span = rows_in.shape[1] // chunks
-    half = rows_in.shape[1] // 2
-
-    def row_copy(q, i):
-        place = pl.ds(q * span, span)
-        return pltpu.make_async_copy(
-            returned[i].at[:, place], rows_in.at[pl.ds(NC * i, NC), place], row_sem.at[q, i]
-        )
-
-    def hidden_copy(q):
-        source = hidden.at[pl.ds(q * span * top, span * top)]
-        return pltpu.make_async_copy(source, hidden_in.at[q], sems.at[q])
+def token_kernel(n, source, ids, probs, inputs, *refs):
+    hidden, returned, (grad, part) = refs[:2], refs[2 : n + 2], refs[n + 2 : n + 4]
+    grad_out, logits, out_sem = refs[n + 4 :]
+    chunks, tok, top = grad_out.shape[0], 16, 8
+    half = inputs.shape[0] // 2
+    span = 2 * half // chunks
 
     def out_copy(q):
         target = grad.at[pl.ds(q * span * top, span * top)]
         return pltpu.make_async_copy(grad_out.at[q], target, out_sem.at[q])
-
-    inputs_copy = pltpu.make_async_copy(inputs, inputs_in, sems.at[chunks])
-    for q in range(chunks):
-        for i in range(n):
-            row_copy(q, i).start()
-        hidden_copy(q).start()
-    inputs_copy.start()
 
     shape = (tok * top, EXPERTS * tok)
     mine = lax.broadcasted_iota(jnp.int32, shape, 0) // top == lax.broadcasted_iota(
         jnp.int32, shape, 1
     ) % tok
     for q in range(chunks):
-        for i in range(n):
-            row_copy(q, i).wait()
-        hidden_copy(q).wait()
         for g in range(span // tok):
             first = q * span + g * tok
             at = slice(g * tok * top, (g + 1) * tok * top)
+            slot, within = first // half, first % half * top
             rows = jnp.concatenate(
-                [rows_in[e, first : first + tok, :] for e in range(EXPERTS)], axis=0
+                [r[e, first : first + tok, :] for r in returned for e in range(NC)], axis=0
             )
             routes = ids[first * top : (first + tok) * top, :]
             pick = jnp.where(jnp.logical_and(mine, routes == source[...]), 1.0, 0.0)
             back = jnp.dot(pick.astype(jnp.bfloat16), rows, preferred_element_type=jnp.float32)
-            dgate = jnp.sum(hidden_in[q, at, :].astype(jnp.float32) * back, axis=1, keepdims=True)
-            dgate = dgate.reshape(tok, top, 1)
+            saved = hidden[slot][within : within + tok * top, :].astype(jnp.float32)
+            dgate = jnp.sum(saved * back, axis=1, keepdims=True).reshape(tok, top, 1)
             member = routes.reshape(tok, top, 1) == lax.broadcasted_iota(
                 jnp.int32, (tok, top, EXPERTS), 2
             )
@@ -224,13 +205,12 @@
             logits[first : first + tok, :] = jnp.sum(jnp.where(member, selected, 0.0), axis=1)
         out_copy(q).start()
 
-    inputs_copy.wait()
     for s in range(2):
         logit = logits[s * half : (s + 1) * half, :]
         high = logit.astype(jnp.bfloat16)
         low = (logit - high.astype(jnp.float32)).astype(jnp.bfloat16)
         over = (((0,), (0,)), ((), ()))
-        values = inputs_in[s * half : (s + 1) * half, :]
+        values = inputs[s * half : (s + 1) * half, :]
         made = lax.dot_general(high, values, over, preferred_element_type=jnp.float32)
         part[s] = made + lax.dot_general(low, values, over, preferred_element_type=jnp.float32)
     for q in range(chunks):
@@ -239,36 +219,31 @@
 
 def token_math(source, ids, probs, inputs, hidden, returned):
     rows, depth = inputs.shape
-    top, hid = 8, hidden.shape[1]
+    top, hid = 8, hidden[0].shape[1]
     n, chunks = len(returned), 4
     span = rows // chunks
     inside = pl.BlockSpec(memory_space=pltpu.VMEM)
     anywhere = pl.BlockSpec(memory_space=pl.ANY)
     return pl.pallas_call(
         functools.partial(token_kernel, n),
-        in_specs=[inside] * 3 + [anywhere] * (2 + n),
+        in_specs=[inside] * (6 + n),
         out_specs=[anywhere, inside],
         out_shape=[
             jax.ShapeDtypeStruct((rows * top, hid), jnp.bfloat16),
             jax.ShapeDtypeStruct((2, EXPERTS, depth), jnp.float32),
         ],
         scratch_shapes=[
-            pltpu.VMEM((EXPERTS, rows, hid), jnp.bfloat16),
-            pltpu.VMEM((chunks, span * top, hid), jnp.bfloat16),
-            pltpu.VMEM((rows, depth), jnp.bfloat16),
             pltpu.VMEM((chunks, span * top, hid), jnp.bfloat16),
             pltpu.VMEM((rows, EXPERTS), jnp.float32),
-            pltpu.SemaphoreType.DMA((chunks, n)),
-            pltpu.SemaphoreType.DMA((chunks + 1,)),
             pltpu.SemaphoreType.DMA((chunks,)),
         ],
-        compiler_params=pltpu.CompilerParams(vmem_limit_bytes=32 * MIB),
+        compiler_params=pltpu.CompilerParams(vmem_limit_bytes=16 * MIB),
         cost_estimate=pl.CostEstimate(
             flops=2 * rows * top * hid * EXPERTS * 16,
             bytes_accessed=2 * rows * hid * (2 * top + EXPERTS),
             transcendentals=0,
         ),
-    )(source, ids, probs, inputs, hidden, *returned)
+    )(source, ids, probs, inputs, *hidden, *returned)
 
 
 def reduce_router(part, core):
@@ -337,7 +312,7 @@
     )
     marks = lax.dynamic_slice_in_dim(jnp.asarray(table), me, 1, 0)
     grad, part = token_math(
-        marks, ids, probs, saved_input.reshape(rows, depth), saved_hidden.reshape(rows * top, hid), returned
+        marks, ids, probs, saved_input.reshape(rows, depth), [saved_hidden[0, s].reshape(tok * top, hid) for s in range(2)], returned
     )
     return grad.reshape(saved_hidden.shape), reduce_router(part, lax.rem(me, NC))[None]
 

time: 155 us -> 153 us (0.987)
  waiting for transfers between devices: 71.1 us -> 69.4 us
    another operation x0 -> x1, local copies, waits for them, and re-layouts: none -> 1.71 us  [local(): saved_hidden[0, s].reshape(tok * top, hid)]
    ppermute x25, waiting for transfers between devices: 65 us -> 63.3 us  [send(): return lax.ppermute(block, 'expert', shift(dx, dy, dc))]
    unnamed x11 -> x9, local copies, waits for them, and re-layouts: 1.7 us -> 0.11 us
  transfers between devices with their start and end apart: 27 -> 27, of which waited for: 16 -> 15; matrix products, arithmetic and copies ran while one was open for 2% -> 3% of each run, Pallas kernels for 19% -> 19%
where the time goes in v3:
time: 153 us
  waiting for transfers between devices  69.4 us (45%)
  starting transfers between devices  43.5 us (28%)
  Pallas kernels  34 us (22%)
  local copies, waits for them, and re-layouts  4.01 us (3%)
    ppermute x25, waiting for transfers between devices, send(): return lax.ppermute(block, 'expert', shift(dx, dy, dc))  63.3 us
    ppermute x25, starting transfers between devices, send(): return lax.ppermute(block, 'expert', shift(dx, dy, dc))  35.9 us
    pallas_call x2, Pallas kernels, project(): pl.pallas_call(functools.partial(project_kernel, layout, depth_of), in_sp...  29.8 us
    ppermute x2, starting transfers between devices, send_mirror(): return lax.ppermute(block, ('pipe', 'expert'), route)  7.62 us
    ppermute x2, waiting for transfers between devices, send_mirror(): return lax.ppermute(block, ('pipe', 'expert'), route)  6.1 us
    pallas_call x1, Pallas kernels, token_math(): pl.pallas_call(functools.partial(token_kernel, n), in_specs=[inside] * (6...  4.26 us
  transfers between devices with their start and end apart: 27, of which 15 were waited for; matrix products, arithmetic and copies ran while one was open for 3% of the time, Pallas kernels for 19%

profile of v3, /device:TPU:1, one launch (start us, length us, event | category | flops | bytes accessed | tf_op | source)
XLA Modules:
  0.0 153.1 jit_solution(8666613239176760879)
XLA Ops:
  0.6 1.5 collective-permute-start.7
  2.1 3.0 %collective-permute-start = (bf16[128,3584]{1,0:T(8,128)(2,1)}, bf16[128,3584]{1,0:T(8,128)(2,1)S(1)}, u32[]{:S(2)}, u32[]{:S(2)}) collective-permute-start(bf16[128,3584]{1,0:T(8,128)(2,1)} %bitcast.38), channel_id=1, source_target_pairs={{0,2},{1,3},{2,0},{3,1},{4,6},{5,7},{6,4},{7,5},{8,10},{9,11},{10,... | collective-permute-start | bytes 2752520 | tf_op jit(solution)/shard_map/ppermute | solution.py:33
  5.2 1.2 slice_bitcast_fusion.2
  6.4 1.3 collective-permute-start.1
  7.7 1.5 collective-permute-start.4
  9.1 10.3 %collective-permute-done.1.refs_2_ = bf16[64,3584]{1,0:T(8,128)(2,1)S(1)} collective-permute-done((bf16[64,3584]{1,0:T(8,128)(2,1)S(1)}, bf16[64,3584]{1,0:T(8,128)(2,1)S(1)}, u32[]{:S(2)}, u32[]{:S(2)}) %collective-permute-start.1) | collective-permute-done | bytes 458784 | tf_op jit(solution)/shard_map/ppermute | solution.py:33
  19.4 1.3 collective-permute-start.3
  20.9 8.4 %collective-permute-done.2.refs_3_ = bf16[64,3584]{1,0:T(8,128)(2,1)S(1)} collective-permute-done((bf16[64,3584]{1,0:T(8,128)(2,1)S(1)}, bf16[64,3584]{1,0:T(8,128)(2,1)S(1)}, u32[]{:S(2)}, u32[]{:S(2)}) %collective-permute-start.2) | collective-permute-done | bytes 458784 | tf_op jit(solution)/shard_map/ppermute | solution.py:33
  29.2 1.3 collective-permute-start.6
  30.7 2.5 %collective-permute-start.13 = (bf16[128,3584]{1,0:T(8,128)(2,1)S(1)}, bf16[128,3584]{1,0:T(8,128)(2,1)S(1)}, u32[]{:S(2)}, u32[]{:S(2)}) collective-permute-start(bf16[128,3584]{1,0:T(8,128)(2,1)S(1)} %collective-permute-done.refs_1_), channel_id=1, source_target_pairs={{0,12},{1,13},{2,14},{3,15},{4,0},{5,1},{6,2},{7,3},{8,4},{9,5},{1... | collective-permute-start | bytes 2752520 | tf_op jit(solution)/shard_map/ppermute | solution.py:33
  33.2 5.9 %collective-permute-done.5.refs_6_ = bf16[64,3584]{1,0:T(8,128)(2,1)S(1)} collective-permute-done((bf16[64,3584]{1,0:T(8,128)(2,1)S(1)}, bf16[64,3584]{1,0:T(8,128)(2,1)S(1)}, u32[]{:S(2)}, u32[]{:S(2)}) %collective-permute-start.5) | collective-permute-done | bytes 458784 | tf_op jit(solution)/shard_map/ppermute | solution.py:33
  39.3 2.8 %collective-permute-start.15 = (bf16[64,3584]{1,0:T(8,128)(2,1)S(1)}, bf16[64,3584]{1,0:T(8,128)(2,1)S(1)}, u32[]{:S(2)}, u32[]{:S(2)}) collective-permute-start(bf16[64,3584]{1,0:T(8,128)(2,1)S(1)} %collective-permute-done.6.refs_7_), channel_id=1, source_target_pairs={{0,2},{1,3},{2,0},{3,1},{4,6},{5,7},{6,4},{7,5},{8,10},{9,11},{10,... | collective-permute-start | bytes 1376264 | tf_op jit(solution)/shard_map/ppermute | solution.py:33
  42.0 15.1 %shard_map.86 = (bf16[2,128,1024]{2,1,0:T(8,128)(2,1)S(1)}, bf16[2,128,1024]{2,1,0:T(8,128)(2,1)S(1)}, bf16[2,128,1024]{2,1,0:T(8,128)(2,1)}, bf16[2,128,1024]{2,1,0:T(8,128)(2,1)S(1)}, bf16[2,128,1024]{2,1,0:T(8,128)(2,1)}) custom-call(bf16[128,3584]{1,0:T(8,128)(2,1)} %bitcast.39, bf16[128,3584]{1,0:T(8,128)(2,1)} %copy-done.3, ...), custom_call_target="tpu_custom_call" | custom-call | flops 9395240960 | bytes 36569088 | tf_op jit(solution)/shard_map/pallas_call | solution.py:141
  57.2 1.5 %collective-permute-done.12.refs_0_ = bf16[128,3584]{1,0:T(8,128)(2,1)S(1)} collective-permute-done((bf16[128,3584]{1,0:T(8,128)(2,1)S(1)}, bf16[128,3584]{1,0:T(8,128)(2,1)S(1)}, u32[]{:S(2)}, u32[]{:S(2)}) %collective-permute-start.12) | collective-permute-done | bytes 917536 | tf_op jit(solution)/shard_map/ppermute | solution.py:33
  58.8 2.5 %collective-permute-start.11 = (bf16[2,128,1024]{2,1,0:T(8,128)(2,1)}, bf16[2,128,1024]{2,1,0:T(8,128)(2,1)}, u32[]{:S(2)}, u32[]{:S(2)}) collective-permute-start(bf16[2,128,1024]{2,1,0:T(8,128)(2,1)} %get-tuple-element.20), channel_id=1, source_target_pairs={{0,8},{1,9},{2,10},{3,11},{4,12},{5,13},{6,14},{7,15},{8,0},{9,1},... | collective-permute-start | bytes 1572872 | tf_op jit(solution)/shard_map/ppermute | solution.py:33
  61.2 1.2 collective-permute-start.9
  62.4 14.6 %shard_map.87 = (bf16[2,128,1024]{2,1,0:T(8,128)(2,1)}, bf16[2,128,1024]{2,1,0:T(8,128)(2,1)}, bf16[2,128,1024]{2,1,0:T(8,128)(2,1)}) custom-call(bf16[128,3584]{1,0:T(8,128)(2,1)S(1)} %collective-permute-done.12.refs_0_, bf16[128,3584]{1,0:T(8,128)(2,1)S(1)} %collective-permute-done.13.refs_1_, bf16[64,3584]{1,0:T(8,128)(2,1)S(1)} %collective-permute-done.14.refs_2_, ...), custom_call_target="tpu_custom_call" | custom-call | flops 5637144576 | bytes 33685504 | tf_op jit(solution)/shard_map/pallas_call | solution.py:141
  77.0 4.1 %collective-permute-start.18 = (bf16[2,128,1024]{2,1,0:T(8,128)(2,1)}, bf16[2,128,1024]{2,1,0:T(8,128)(2,1)}, u32[]{:S(2)}, u32[]{:S(2)}) collective-permute-start(bf16[2,128,1024]{2,1,0:T(8,128)(2,1)} %get-tuple-element.27), channel_id=1, source_target_pairs={{0,10},{1,11},{2,8},{3,9},{4,14},{5,15},{6,12},{7,13},{8,2},{9,3},... | collective-permute-start | bytes 1572872 | tf_op jit(solution)/shard_map/ppermute | solution.py:33
  81.2 5.1 %collective-permute-start.16 = (bf16[2,128,1024]{2,1,0:T(8,128)(2,1)}, bf16[2,128,1024]{2,1,0:T(8,128)(2,1)}, u32[]{:S(2)}, u32[]{:S(2)}) collective-permute-start(bf16[2,128,1024]{2,1,0:T(8,128)(2,1)} %get-tuple-element.23), channel_id=1, source_target_pairs={{0,14},{1,15},{2,12},{3,13},{4,2},{5,3},{6,0},{7,1},{8,6},{9,7},{1... | collective-permute-start | bytes 1572872 | tf_op jit(solution)/shard_map/ppermute | solution.py:33
  87.7 1.7 %slice_bitcast_fusion = (bf16[512,1024]{1,0:T(8,128)(2,1)S(1)}, bf16[512,1024]{1,0:T(8,128)(2,1)S(1)}) fusion(bf16[1,2,64,8,1024]{4,3,2,1,0:T(8,128)(2,1)} %param.9), kind=kLoop, calls=%fused_computation.4 | loop fusion | bytes 4194304 | tf_op jit(solution)/shard_map/reshape;squeeze | solution.py:315
  89.5 6.0 %collective-permute-done.18.refs_9_ = bf16[2,128,1024]{2,1,0:T(8,128)(2,1)} collective-permute-done((bf16[2,128,1024]{2,1,0:T(8,128)(2,1)}, bf16[2,128,1024]{2,1,0:T(8,128)(2,1)}, u32[]{:S(2)}, u32[]{:S(2)}) %collective-permute-start.18) | collective-permute-done | bytes 524320 | tf_op jit(solution)/shard_map/ppermute | solution.py:33
  95.4 22.4 %collective-permute-done.17.refs_8_ = bf16[2,128,1024]{2,1,0:T(8,128)(2,1)} collective-permute-done((bf16[2,128,1024]{2,1,0:T(8,128)(2,1)}, bf16[2,128,1024]{2,1,0:T(8,128)(2,1)}, u32[]{:S(2)}, u32[]{:S(2)}) %collective-permute-start.17) | collective-permute-done | bytes 524320 | tf_op jit(solution)/shard_map/ppermute | solution.py:33
  118.9 4.3 %shard_map.88 = (bf16[1024,1024]{1,0:T(8,128)(2,1)}, f32[2,16,3584]{2,1,0:T(8,128)S(1)}) custom-call(s32[1,256]{1,0:T(1,128)S(1)} %constant_dynamic-slice_fusion.source, s32[1024,1]{1,0:T(8,128)S(1)} %reshape.32.ids, f32[128,16]{1,0:T(8,128)S(1)} %bitcast.34, bf16[128,3584]{1,0:T(8,128)(2,1)S(1)} %bitcast.33, ...), custom_call_target="tpu_custom_call" | custom-call | flops 536870912 | bytes 8388608 | tf_op jit(solution)/shard_map/pallas_call | solution.py:227
  123.2 3.2 %collective-permute-start.19 = (f32[16,3584]{1,0:T(8,128)S(1)}, f32[16,3584]{1,0:T(8,128)S(1)}, u32[]{:S(2)}, u32[]{:S(2)}) collective-permute-start(f32[16,3584]{1,0:T(8,128)S(1)} %select_bitcast_fusion.2), channel_id=1, source_target_pairs={{0,1},{1,0},{2,3},{3,2},{4,5},{5,4},{6,7},{7,6},{8,9},{9,8},{10,11... | collective-permute-start | bytes 688136 | tf_op jit(solution)/shard_map/ppermute | solution.py:33
  128.0 3.4 %collective-permute-start.21 = (bf16[16,3584]{1,0:T(8,128)(2,1)S(1)}, bf16[16,3584]{1,0:T(8,128)(2,1)S(1)}, u32[]{:S(2)}, u32[]{:S(2)}) collective-permute-start(bf16[16,3584]{1,0:T(8,128)(2,1)S(1)} %fusion.4), channel_id=1, source_target_pairs={{0,4},{1,5},{2,6},{3,7},{4,8},{5,9},{6,10},{7,11},{8,12},{9,13},{1... | collective-permute-start | bytes 344072 | tf_op jit(solution)/shard_map/ppermute | solution.py:33
  131.8 1.7 %collective-permute-done.20 = bf16[16,3584]{1,0:T(8,128)(2,1)S(1)} collective-permute-done((bf16[16,3584]{1,0:T(8,128)(2,1)S(1)}, bf16[16,3584]{1,0:T(8,128)(2,1)S(1)}, u32[]{:S(2)}, u32[]{:S(2)}) %collective-permute-start.20) | collective-permute-done | bytes 114720 | tf_op jit(solution)/shard_map/ppermute | solution.py:33
  133.5 3.2 %collective-permute-done.21 = bf16[16,3584]{1,0:T(8,128)(2,1)S(1)} collective-permute-done((bf16[16,3584]{1,0:T(8,128)(2,1)S(1)}, bf16[16,3584]{1,0:T(8,128)(2,1)S(1)}, u32[]{:S(2)}, u32[]{:S(2)}) %collective-permute-start.21) | collective-permute-done | bytes 114720 | tf_op jit(solution)/shard_map/ppermute | solution.py:33
  136.9 6.2 %collective-permute-start.24 = (bf16[16,3584]{1,0:T(8,128)(2,1)S(1)}, bf16[16,3584]{1,0:T(8,128)(2,1)S(1)}, u32[]{:S(2)}, u32[]{:S(2)}) collective-permute-start(bf16[16,3584]{1,0:T(8,128)(2,1)S(1)} %add_convert_fusion), channel_id=1, source_target_pairs={{0,113},{1,112},{2,115},{3,114},{4,117},{5,116},{6,119},{7,118},{8... | collective-permute-start | bytes 344072 | tf_op jit(solution)/shard_map/ppermute | solution.py:46
  143.1 1.4 collective-permute-start.25
  144.5 3.1 %collective-permute-done.24 = bf16[16,3584]{1,0:T(8,128)(2,1)S(1)} collective-permute-done((bf16[16,3584]{1,0:T(8,128)(2,1)S(1)}, bf16[16,3584]{1,0:T(8,128)(2,1)S(1)}, u32[]{:S(2)}, u32[]{:S(2)}) %collective-permute-start.24) | collective-permute-done | bytes 114720 | tf_op jit(solution)/shard_map/ppermute | solution.py:46
  147.6 3.0 %collective-permute-done.25 = bf16[16,3584]{1,0:T(8,128)(2,1)S(1)} collective-permute-done((bf16[16,3584]{1,0:T(8,128)(2,1)S(1)}, bf16[16,3584]{1,0:T(8,128)(2,1)S(1)}, u32[]{:S(2)}, u32[]{:S(2)}) %collective-permute-start.25) | collective-permute-done | bytes 114720 | tf_op jit(solution)/shard_map/ppermute | solution.py:46
  150.8 1.5 collective-permute-done.26
  (46 shorter events, 6.3 us)
Async XLA Ops:
  0.6 85.6 %copy-start = (bf16[1,2,16,3584]{3,2,1,0:T(8,128)(2,1)S(1)}, bf16[1,2,16,3584]{3,2,1,0:T(8,128)(2,1)}, u32[]{:S(2)}) copy-start(bf16[1,2,16,3584]{3,2,1,0:T(8,128)(2,1)} %param.12) | copy-start | bytes 688132
  0.6 41.4 %collective-permute-start.7 = (bf16[2,1024,3584]{2,1,0:T(8,128)(2,1)}, bf16[2,1024,3584]{2,1,0:T(8,128)(2,1)}, u32[]{:S(2)}, u32[]{:S(2)}) collective-permute-start(bf16[2,1024,3584]{2,1,0:T(8,128)(2,1)} %bitcast.35), channel_id=1, source_target_pairs={{0,1},{1,0},{2,3},{3,2},{4,5},{5,4},{6,7},{7,6},{8,9},{9,8},{10,11... | collective-permute-start | bytes 44040200 | tf_op jit(solution)/shard_map/ppermute | solution.py:33
  2.1 28.4 %collective-permute-start = (bf16[128,3584]{1,0:T(8,128)(2,1)}, bf16[128,3584]{1,0:T(8,128)(2,1)S(1)}, u32[]{:S(2)}, u32[]{:S(2)}) collective-permute-start(bf16[128,3584]{1,0:T(8,128)(2,1)} %bitcast.38), channel_id=1, source_target_pairs={{0,2},{1,3},{2,0},{3,1},{4,6},{5,7},{6,4},{7,5},{8,10},{9,11},{10,... | collective-permute-start | bytes 2752520 | tf_op jit(solution)/shard_map/ppermute | solution.py:33
  6.4 13.0 %collective-permute-start.1 = (bf16[64,3584]{1,0:T(8,128)(2,1)S(1)}, bf16[64,3584]{1,0:T(8,128)(2,1)S(1)}, u32[]{:S(2)}, u32[]{:S(2)}) collective-permute-start(bf16[64,3584]{1,0:T(8,128)(2,1)S(1)} %get-tuple-element.33), channel_id=1, source_target_pairs={{0,4},{1,5},{2,6},{3,7},{4,8},{5,9},{6,10},{7,11},{8,12},{9,13},{1... | collective-permute-start | bytes 1376264 | tf_op jit(solution)/shard_map/ppermute | solution.py:33
  7.7 13.0 %collective-permute-start.4 = (bf16[64,3584]{1,0:T(8,128)(2,1)S(1)}, bf16[64,3584]{1,0:T(8,128)(2,1)S(1)}, u32[]{:S(2)}, u32[]{:S(2)}) collective-permute-start(bf16[64,3584]{1,0:T(8,128)(2,1)S(1)} %get-tuple-element.32), channel_id=1, source_target_pairs={{0,12},{1,13},{2,14},{3,15},{4,0},{5,1},{6,2},{7,3},{8,4},{9,5},{1... | collective-permute-start | bytes 1376264 | tf_op jit(solution)/shard_map/ppermute | solution.py:33
  9.1 20.1 %collective-permute-start.2 = (bf16[64,3584]{1,0:T(8,128)(2,1)S(1)}, bf16[64,3584]{1,0:T(8,128)(2,1)S(1)}, u32[]{:S(2)}, u32[]{:S(2)}) collective-permute-start(bf16[64,3584]{1,0:T(8,128)(2,1)S(1)} %get-tuple-element.32), channel_id=1, source_target_pairs={{0,4},{1,5},{2,6},{3,7},{4,8},{5,9},{6,10},{7,11},{8,12},{9,13},{1... | collective-permute-start | bytes 1376264 | tf_op jit(solution)/shard_map/ppermute | solution.py:33
  19.4 11.3 %collective-permute-start.3 = (bf16[64,3584]{1,0:T(8,128)(2,1)S(1)}, bf16[64,3584]{1,0:T(8,128)(2,1)S(1)}, u32[]{:S(2)}, u32[]{:S(2)}) collective-permute-start(bf16[64,3584]{1,0:T(8,128)(2,1)S(1)} %get-tuple-element.33), channel_id=1, source_target_pairs={{0,12},{1,13},{2,14},{3,15},{4,0},{5,1},{6,2},{7,3},{8,4},{9,5},{1... | collective-permute-start | bytes 1376264 | tf_op jit(solution)/shard_map/ppermute | solution.py:33
  20.7 18.4 %collective-permute-start.5 = (bf16[64,3584]{1,0:T(8,128)(2,1)S(1)}, bf16[64,3584]{1,0:T(8,128)(2,1)S(1)}, u32[]{:S(2)}, u32[]{:S(2)}) collective-permute-start(bf16[64,3584]{1,0:T(8,128)(2,1)S(1)} %collective-permute-done.1.refs_2_), channel_id=1, source_target_pairs={{0,4},{1,5},{2,6},{3,7},{4,8},{5,9},{6,10},{7,11},{8,12},{9,13},{1... | collective-permute-start | bytes 1376264 | tf_op jit(solution)/shard_map/ppermute | solution.py:33
  29.2 10.0 %collective-permute-start.6 = (bf16[64,3584]{1,0:T(8,128)(2,1)S(1)}, bf16[64,3584]{1,0:T(8,128)(2,1)S(1)}, u32[]{:S(2)}, u32[]{:S(2)}) collective-permute-start(bf16[64,3584]{1,0:T(8,128)(2,1)S(1)} %collective-permute-done.4.refs_5_), channel_id=1, source_target_pairs={{0,12},{1,13},{2,14},{3,15},{4,0},{5,1},{6,2},{7,3},{8,4},{9,5},{1... | collective-permute-start | bytes 1376264 | tf_op jit(solution)/shard_map/ppermute | solution.py:33
  30.5 11.5 %copy-start.3 = (bf16[128,3584]{1,0:T(8,128)(2,1)}, bf16[128,3584]{1,0:T(8,128)(2,1)S(1)}, u32[]{:S(2)}) copy-start(bf16[128,3584]{1,0:T(8,128)(2,1)S(1)} %collective-permute-done.refs_1_) | copy-start | bytes 2752516
  30.5 28.2 %collective-permute-start.12 = (bf16[128,3584]{1,0:T(8,128)(2,1)S(1)}, bf16[128,3584]{1,0:T(8,128)(2,1)S(1)}, u32[]{:S(2)}, u32[]{:S(2)}) collective-permute-start(bf16[128,3584]{1,0:T(8,128)(2,1)S(1)} %collective-permute-done.refs_1_), channel_id=1, source_target_pairs={{0,4},{1,5},{2,6},{3,7},{4,8},{5,9},{6,10},{7,11},{8,12},{9,13},{1... | collective-permute-start | bytes 2752520 | tf_op jit(solution)/shard_map/ppermute | solution.py:33
  30.7 31.7 %collective-permute-start.13 = (bf16[128,3584]{1,0:T(8,128)(2,1)S(1)}, bf16[128,3584]{1,0:T(8,128)(2,1)S(1)}, u32[]{:S(2)}, u32[]{:S(2)}) collective-permute-start(bf16[128,3584]{1,0:T(8,128)(2,1)S(1)} %collective-permute-done.refs_1_), channel_id=1, source_target_pairs={{0,12},{1,13},{2,14},{3,15},{4,0},{5,1},{6,2},{7,3},{8,4},{9,5},{1... | collective-permute-start | bytes 2752520 | tf_op jit(solution)/shard_map/ppermute | solution.py:33
  39.1 19.7 %collective-permute-start.14 = (bf16[64,3584]{1,0:T(8,128)(2,1)S(1)}, bf16[64,3584]{1,0:T(8,128)(2,1)S(1)}, u32[]{:S(2)}, u32[]{:S(2)}) collective-permute-start(bf16[64,3584]{1,0:T(8,128)(2,1)S(1)} %collective-permute-done.5.refs_6_), channel_id=1, source_target_pairs={{0,2},{1,3},{2,0},{3,1},{4,6},{5,7},{6,4},{7,5},{8,10},{9,11},{10,... | collective-permute-start | bytes 1376264 | tf_op jit(solution)/shard_map/ppermute | solution.py:33
  39.3 22.0 %collective-permute-start.15 = (bf16[64,3584]{1,0:T(8,128)(2,1)S(1)}, bf16[64,3584]{1,0:T(8,128)(2,1)S(1)}, u32[]{:S(2)}, u32[]{:S(2)}) collective-permute-start(bf16[64,3584]{1,0:T(8,128)(2,1)S(1)} %collective-permute-done.6.refs_7_), channel_id=1, source_target_pairs={{0,2},{1,3},{2,0},{3,1},{4,6},{5,7},{6,4},{7,5},{8,10},{9,11},{10,... | collective-permute-start | bytes 1376264 | tf_op jit(solution)/shard_map/ppermute | solution.py:33
  58.7 18.3 %collective-permute-start.8 = (bf16[2,128,1024]{2,1,0:T(8,128)(2,1)S(1)}, bf16[2,128,1024]{2,1,0:T(8,128)(2,1)S(1)}, u32[]{:S(2)}, u32[]{:S(2)}) collective-permute-start(bf16[2,128,1024]{2,1,0:T(8,128)(2,1)S(1)} %get-tuple-element.17), channel_id=1, source_target_pairs={{0,2},{1,3},{2,0},{3,1},{4,6},{5,7},{6,4},{7,5},{8,10},{9,11},{10,... | collective-permute-start | bytes 1572872 | tf_op jit(solution)/shard_map/ppermute | solution.py:33
  58.7 22.5 %collective-permute-start.10 = (bf16[2,128,1024]{2,1,0:T(8,128)(2,1)S(1)}, bf16[2,128,1024]{2,1,0:T(8,128)(2,1)S(1)}, u32[]{:S(2)}, u32[]{:S(2)}) collective-permute-start(bf16[2,128,1024]{2,1,0:T(8,128)(2,1)S(1)} %get-tuple-element.19), channel_id=1, source_target_pairs={{0,4},{1,5},{2,6},{3,7},{4,8},{5,9},{6,10},{7,11},{8,12},{9,13},{1... | collective-permute-start | bytes 1572872 | tf_op jit(solution)/shard_map/ppermute | solution.py:33
  58.8 30.7 %collective-permute-start.11 = (bf16[2,128,1024]{2,1,0:T(8,128)(2,1)}, bf16[2,128,1024]{2,1,0:T(8,128)(2,1)}, u32[]{:S(2)}, u32[]{:S(2)}) collective-permute-start(bf16[2,128,1024]{2,1,0:T(8,128)(2,1)} %get-tuple-element.20), channel_id=1, source_target_pairs={{0,8},{1,9},{2,10},{3,11},{4,12},{5,13},{6,14},{7,15},{8,0},{9,1},... | collective-permute-start | bytes 1572872 | tf_op jit(solution)/shard_map/ppermute | solution.py:33
  61.2 25.0 %copy-start.1 = (bf16[1,2,64,3584]{3,2,1,0:T(8,128)(2,1)S(1)}, bf16[1,2,64,3584]{3,2,1,0:T(8,128)(2,1)}, u32[]{:S(2)}) copy-start(bf16[1,2,64,3584]{3,2,1,0:T(8,128)(2,1)} %param.8) | copy-start | bytes 2752516
  61.2 25.4 %copy-start.2 = (s32[1,2,64,8]{2,3,1,0:T(8,128)S(1)}, s32[1,2,64,8]{2,3,1,0:T(8,128)}, u32[]{:S(2)}) copy-start(s32[1,2,64,8]{2,3,1,0:T(8,128)} %param.10) | copy-start | bytes 12292
  61.2 28.2 %collective-permute-start.9 = (bf16[2,128,1024]{2,1,0:T(8,128)(2,1)}, bf16[2,128,1024]{2,1,0:T(8,128)(2,1)}, u32[]{:S(2)}, u32[]{:S(2)}) collective-permute-start(bf16[2,128,1024]{2,1,0:T(8,128)(2,1)} %get-tuple-element.18), channel_id=1, source_target_pairs={{0,12},{1,13},{2,14},{3,15},{4,0},{5,1},{6,2},{7,3},{8,4},{9,5},{1... | collective-permute-start | bytes 1572872 | tf_op jit(solution)/shard_map/ppermute | solution.py:33
  77.0 18.4 %collective-permute-start.18 = (bf16[2,128,1024]{2,1,0:T(8,128)(2,1)}, bf16[2,128,1024]{2,1,0:T(8,128)(2,1)}, u32[]{:S(2)}, u32[]{:S(2)}) collective-permute-start(bf16[2,128,1024]{2,1,0:T(8,128)(2,1)} %get-tuple-element.27), channel_id=1, source_target_pairs={{0,10},{1,11},{2,8},{3,9},{4,14},{5,15},{6,12},{7,13},{8,2},{9,3},... | collective-permute-start | bytes 1572872 | tf_op jit(solution)/shard_map/ppermute | solution.py:33
  81.2 36.7 %collective-permute-start.17 = (bf16[2,128,1024]{2,1,0:T(8,128)(2,1)}, bf16[2,128,1024]{2,1,0:T(8,128)(2,1)}, u32[]{:S(2)}, u32[]{:S(2)}) collective-permute-start(bf16[2,128,1024]{2,1,0:T(8,128)(2,1)} %get-tuple-element.25), channel_id=1, source_target_pairs={{0,6},{1,7},{2,4},{3,5},{4,10},{5,11},{6,8},{7,9},{8,14},{9,15},{1... | collective-permute-start | bytes 1572872 | tf_op jit(solution)/shard_map/ppermute | solution.py:33
  81.2 37.7 %collective-permute-start.16 = (bf16[2,128,1024]{2,1,0:T(8,128)(2,1)}, bf16[2,128,1024]{2,1,0:T(8,128)(2,1)}, u32[]{:S(2)}, u32[]{:S(2)}) collective-permute-start(bf16[2,128,1024]{2,1,0:T(8,128)(2,1)} %get-tuple-element.23), channel_id=1, source_target_pairs={{0,14},{1,15},{2,12},{3,13},{4,2},{5,3},{6,0},{7,1},{8,6},{9,7},{1... | collective-permute-start | bytes 1572872 | tf_op jit(solution)/shard_map/ppermute | solution.py:33
  123.2 4.3 %collective-permute-start.19 = (f32[16,3584]{1,0:T(8,128)S(1)}, f32[16,3584]{1,0:T(8,128)S(1)}, u32[]{:S(2)}, u32[]{:S(2)}) collective-permute-start(f32[16,3584]{1,0:T(8,128)S(1)} %select_bitcast_fusion.2), channel_id=1, source_target_pairs={{0,1},{1,0},{2,3},{3,2},{4,5},{5,4},{6,7},{7,6},{8,9},{9,8},{10,11... | collective-permute-start | bytes 688136 | tf_op jit(solution)/shard_map/ppermute | solution.py:33
  127.6 5.9 %collective-permute-start.20 = (bf16[16,3584]{1,0:T(8,128)(2,1)S(1)}, bf16[16,3584]{1,0:T(8,128)(2,1)S(1)}, u32[]{:S(2)}, u32[]{:S(2)}) collective-permute-start(bf16[16,3584]{1,0:T(8,128)(2,1)S(1)} %fusion.4), channel_id=1, source_target_pairs={{0,8},{1,9},{2,10},{3,11},{4,12},{5,13},{6,14},{7,15},{8,0},{9,1},... | collective-permute-start | bytes 344072 | tf_op jit(solution)/shard_map/ppermute | solution.py:33
  128.0 8.7 %collective-permute-start.21 = (bf16[16,3584]{1,0:T(8,128)(2,1)S(1)}, bf16[16,3584]{1,0:T(8,128)(2,1)S(1)}, u32[]{:S(2)}, u32[]{:S(2)}) collective-permute-start(bf16[16,3584]{1,0:T(8,128)(2,1)S(1)} %fusion.4), channel_id=1, source_target_pairs={{0,4},{1,5},{2,6},{3,7},{4,8},{5,9},{6,10},{7,11},{8,12},{9,13},{1... | collective-permute-start | bytes 344072 | tf_op jit(solution)/shard_map/ppermute | solution.py:33
  131.4 5.4 %collective-permute-start.22 = (bf16[16,3584]{1,0:T(8,128)(2,1)S(1)}, bf16[16,3584]{1,0:T(8,128)(2,1)S(1)}, u32[]{:S(2)}, u32[]{:S(2)}) collective-permute-start(bf16[16,3584]{1,0:T(8,128)(2,1)S(1)} %fusion.4), channel_id=1, source_target_pairs={{0,12},{1,13},{2,14},{3,15},{4,0},{5,1},{6,2},{7,3},{8,4},{9,5},{1... | collective-permute-start | bytes 344072 | tf_op jit(solution)/shard_map/ppermute | solution.py:33
  136.8 7.7 %collective-permute-start.23 = (bf16[16,3584]{1,0:T(8,128)(2,1)S(1)}, bf16[16,3584]{1,0:T(8,128)(2,1)S(1)}, u32[]{:S(2)}, u32[]{:S(2)}) collective-permute-start(bf16[16,3584]{1,0:T(8,128)(2,1)S(1)} %add_convert_fusion), channel_id=1, source_target_pairs={{0,2},{1,3},{2,0},{3,1},{4,6},{5,7},{6,4},{7,5},{8,10},{9,11},{10,... | collective-permute-start | bytes 344072 | tf_op jit(solution)/shard_map/ppermute | solution.py:33
  136.9 10.7 %collective-permute-start.24 = (bf16[16,3584]{1,0:T(8,128)(2,1)S(1)}, bf16[16,3584]{1,0:T(8,128)(2,1)S(1)}, u32[]{:S(2)}, u32[]{:S(2)}) collective-permute-start(bf16[16,3584]{1,0:T(8,128)(2,1)S(1)} %add_convert_fusion), channel_id=1, source_target_pairs={{0,113},{1,112},{2,115},{3,114},{4,117},{5,116},{6,119},{7,118},{8... | collective-permute-start | bytes 344072 | tf_op jit(solution)/shard_map/ppermute | solution.py:46
  143.1 7.5 %collective-permute-start.25 = (bf16[16,3584]{1,0:T(8,128)(2,1)S(1)}, bf16[16,3584]{1,0:T(8,128)(2,1)S(1)}, u32[]{:S(2)}, u32[]{:S(2)}) collective-permute-start(bf16[16,3584]{1,0:T(8,128)(2,1)S(1)} %add_convert_fusion), channel_id=1, source_target_pairs={{0,115},{1,114},{2,113},{3,112},{4,119},{5,118},{6,117},{7,116},{8... | collective-permute-start | bytes 344072 | tf_op jit(solution)/shard_map/ppermute | solution.py:46
  150.7 1.6 %collective-permute-start.26 = (f32[16,3584]{1,0:T(8,128)S(1)}, f32[16,3584]{1,0:T(8,128)S(1)}, u32[]{:S(2)}, u32[]{:S(2)}) collective-permute-start(f32[16,3584]{1,0:T(8,128)S(1)} %add_add_fusion), channel_id=1, source_target_pairs={{0,1},{1,0},{2,3},{3,2},{4,5},{5,4},{6,7},{7,6},{8,9},{9,8},{10,11... | collective-permute-start | bytes 688136 | tf_op jit(solution)/shard_map/ppermute | solution.py:33

commit v4 on v3

--- a/solution.py
+++ b/solution.py
@@ -263,7 +263,8 @@
         mirror.astype(wide) + mirror_other.astype(wide)
     )
     sibling = send(total, 0, 0, 1)
-    return jnp.stack([jnp.where(first, total, sibling), jnp.where(first, sibling, total)])
+    here = jnp.arange(2)[:, None, None] == core
+    return jnp.where(here, total[None], sibling[None])
 
 
 def local(out_grad, saved_input, saved_hidden, expert_ids, down_weight, router_weight):
@@ -281,9 +282,9 @@
     own = out_grad.reshape(rows, depth)
     weight = down_weight.reshape(2, hid, depth)
 
-    across = send(own, 0, 1, 0)
     sibling_weight = send(weight, 0, 0, 1)
     first, second = out_grad[0, 0], out_grad[0, 1]
+    across = send(after(own, first, second), 0, 1, 0)
     low, high = [send(first, 1, 0, 0)], [send(second, -1, 0, 0)]
     far = send(low[0], 1, 0, 0), send(high[0], -1, 0, 0)
     low, high = (low[0], send(second, 1, 0, 0)), (send(first, -1, 0, 0), high[0])

time: 153 us -> 153 us (level)
  no operation moved by 1% of the time
where the time goes in v4:
time: 153 us
  waiting for transfers between devices  69.7 us (46%)
  starting transfers between devices  43.3 us (28%)
  Pallas kernels  34 us (22%)
  local copies, waits for them, and re-layouts  4.01 us (3%)
    ppermute x25, waiting for transfers between devices, send(): return lax.ppermute(block, 'expert', shift(dx, dy, dc))  63.6 us
    ppermute x25, starting transfers between devices, send(): return lax.ppermute(block, 'expert', shift(dx, dy, dc))  35.8 us
    pallas_call x2, Pallas kernels, project(): pl.pallas_call(functools.partial(project_kernel, layout, depth_of), in_sp...  29.7 us
    ppermute x2, starting transfers between devices, send_mirror(): return lax.ppermute(block, ('pipe', 'expert'), route)  7.43 us
    ppermute x2, waiting for transfers between devices, send_mirror(): return lax.ppermute(block, ('pipe', 'expert'), route)  6.1 us
    pallas_call x1, Pallas kernels, token_math(): pl.pallas_call(functools.partial(token_kernel, n), in_specs=[inside] * (6...  4.27 us
  transfers between devices with their start and end apart: 27, of which 15 were waited for; matrix products, arithmetic and copies ran while one was open for 3% of the time, Pallas kernels for 19%

profile of v4, /device:TPU:1, one launch (start us, length us, event | category | flops | bytes accessed | tf_op | source)
XLA Modules:
  0.0 153.2 jit_solution(8280315607417469028)
XLA Ops:
  0.6 1.5 collective-permute-start.7
  2.1 1.2 slice_bitcast_fusion.2
  3.4 3.1 %collective-permute-start = (bf16[128,3584]{1,0:T(8,128)(2,1)}, bf16[128,3584]{1,0:T(8,128)(2,1)S(1)}, u32[]{:S(2)}, u32[]{:S(2)}) collective-permute-start(bf16[128,3584]{1,0:T(8,128)(2,1)} %bitcast.32), channel_id=1, source_target_pairs={{0,2},{1,3},{2,0},{3,1},{4,6},{5,7},{6,4},{7,5},{8,10},{9,11},{10,... | collective-permute-start | bytes 2752520 | tf_op jit(solution)/shard_map/ppermute | solution.py:33
  6.4 1.2 collective-permute-start.1
  7.7 1.5 collective-permute-start.4
  9.1 10.3 %collective-permute-done.1.refs_2_ = bf16[64,3584]{1,0:T(8,128)(2,1)S(1)} collective-permute-done((bf16[64,3584]{1,0:T(8,128)(2,1)S(1)}, bf16[64,3584]{1,0:T(8,128)(2,1)S(1)}, u32[]{:S(2)}, u32[]{:S(2)}) %collective-permute-start.1) | collective-permute-done | bytes 458784 | tf_op jit(solution)/shard_map/ppermute | solution.py:33
  19.5 1.3 collective-permute-start.3
  20.9 8.4 %collective-permute-done.2.refs_3_ = bf16[64,3584]{1,0:T(8,128)(2,1)S(1)} collective-permute-done((bf16[64,3584]{1,0:T(8,128)(2,1)S(1)}, bf16[64,3584]{1,0:T(8,128)(2,1)S(1)}, u32[]{:S(2)}, u32[]{:S(2)}) %collective-permute-start.2) | collective-permute-done | bytes 458784 | tf_op jit(solution)/shard_map/ppermute | solution.py:33
  29.3 1.3 collective-permute-start.6
  30.8 2.5 %collective-permute-start.13 = (bf16[128,3584]{1,0:T(8,128)(2,1)S(1)}, bf16[128,3584]{1,0:T(8,128)(2,1)S(1)}, u32[]{:S(2)}, u32[]{:S(2)}) collective-permute-start(bf16[128,3584]{1,0:T(8,128)(2,1)S(1)} %collective-permute-done.refs_1_), channel_id=1, source_target_pairs={{0,12},{1,13},{2,14},{3,15},{4,0},{5,1},{6,2},{7,3},{8,4},{9,5},{1... | collective-permute-start | bytes 2752520 | tf_op jit(solution)/shard_map/ppermute | solution.py:33
  33.3 5.9 %collective-permute-done.5.refs_6_ = bf16[64,3584]{1,0:T(8,128)(2,1)S(1)} collective-permute-done((bf16[64,3584]{1,0:T(8,128)(2,1)S(1)}, bf16[64,3584]{1,0:T(8,128)(2,1)S(1)}, u32[]{:S(2)}, u32[]{:S(2)}) %collective-permute-start.5) | collective-permute-done | bytes 458784 | tf_op jit(solution)/shard_map/ppermute | solution.py:33
  39.5 2.6 %collective-permute-start.15 = (bf16[64,3584]{1,0:T(8,128)(2,1)S(1)}, bf16[64,3584]{1,0:T(8,128)(2,1)S(1)}, u32[]{:S(2)}, u32[]{:S(2)}) collective-permute-start(bf16[64,3584]{1,0:T(8,128)(2,1)S(1)} %collective-permute-done.6.refs_7_), channel_id=1, source_target_pairs={{0,2},{1,3},{2,0},{3,1},{4,6},{5,7},{6,4},{7,5},{8,10},{9,11},{10,... | collective-permute-start | bytes 1376264 | tf_op jit(solution)/shard_map/ppermute | solution.py:33
  42.1 15.1 %shard_map.86 = (bf16[2,128,1024]{2,1,0:T(8,128)(2,1)S(1)}, bf16[2,128,1024]{2,1,0:T(8,128)(2,1)S(1)}, bf16[2,128,1024]{2,1,0:T(8,128)(2,1)}, bf16[2,128,1024]{2,1,0:T(8,128)(2,1)S(1)}, bf16[2,128,1024]{2,1,0:T(8,128)(2,1)}) custom-call(bf16[128,3584]{1,0:T(8,128)(2,1)} %bitcast.33, bf16[128,3584]{1,0:T(8,128)(2,1)} %copy-done.3, ...), custom_call_target="tpu_custom_call" | custom-call | flops 9395240960 | bytes 36569088 | tf_op jit(solution)/shard_map/pallas_call | solution.py:141
  57.3 1.5 %collective-permute-done.12.refs_0_ = bf16[128,3584]{1,0:T(8,128)(2,1)S(1)} collective-permute-done((bf16[128,3584]{1,0:T(8,128)(2,1)S(1)}, bf16[128,3584]{1,0:T(8,128)(2,1)S(1)}, u32[]{:S(2)}, u32[]{:S(2)}) %collective-permute-start.12) | collective-permute-done | bytes 917536 | tf_op jit(solution)/shard_map/ppermute | solution.py:33
  59.0 2.4 %collective-permute-start.11 = (bf16[2,128,1024]{2,1,0:T(8,128)(2,1)}, bf16[2,128,1024]{2,1,0:T(8,128)(2,1)}, u32[]{:S(2)}, u32[]{:S(2)}) collective-permute-start(bf16[2,128,1024]{2,1,0:T(8,128)(2,1)} %get-tuple-element.22), channel_id=1, source_target_pairs={{0,8},{1,9},{2,10},{3,11},{4,12},{5,13},{6,14},{7,15},{8,0},{9,1},... | collective-permute-start | bytes 1572872 | tf_op jit(solution)/shard_map/ppermute | solution.py:33
  62.5 14.6 %shard_map.87 = (bf16[2,128,1024]{2,1,0:T(8,128)(2,1)}, bf16[2,128,1024]{2,1,0:T(8,128)(2,1)}, bf16[2,128,1024]{2,1,0:T(8,128)(2,1)}) custom-call(bf16[128,3584]{1,0:T(8,128)(2,1)S(1)} %collective-permute-done.12.refs_0_, bf16[128,3584]{1,0:T(8,128)(2,1)S(1)} %collective-permute-done.13.refs_1_, bf16[64,3584]{1,0:T(8,128)(2,1)S(1)} %collective-permute-done.14.refs_2_, ...), custom_call_target="tpu_custom_call" | custom-call | flops 5637144576 | bytes 33685504 | tf_op jit(solution)/shard_map/pallas_call | solution.py:141
  77.2 4.1 %collective-permute-start.18 = (bf16[2,128,1024]{2,1,0:T(8,128)(2,1)}, bf16[2,128,1024]{2,1,0:T(8,128)(2,1)}, u32[]{:S(2)}, u32[]{:S(2)}) collective-permute-start(bf16[2,128,1024]{2,1,0:T(8,128)(2,1)} %get-tuple-element.29), channel_id=1, source_target_pairs={{0,10},{1,11},{2,8},{3,9},{4,14},{5,15},{6,12},{7,13},{8,2},{9,3},... | collective-permute-start | bytes 1572872 | tf_op jit(solution)/shard_map/ppermute | solution.py:33
  81.3 5.1 %collective-permute-start.16 = (bf16[2,128,1024]{2,1,0:T(8,128)(2,1)}, bf16[2,128,1024]{2,1,0:T(8,128)(2,1)}, u32[]{:S(2)}, u32[]{:S(2)}) collective-permute-start(bf16[2,128,1024]{2,1,0:T(8,128)(2,1)} %get-tuple-element.25), channel_id=1, source_target_pairs={{0,14},{1,15},{2,12},{3,13},{4,2},{5,3},{6,0},{7,1},{8,6},{9,7},{1... | collective-permute-start | bytes 1572872 | tf_op jit(solution)/shard_map/ppermute | solution.py:33
  87.8 1.7 %slice_bitcast_fusion = (bf16[512,1024]{1,0:T(8,128)(2,1)S(1)}, bf16[512,1024]{1,0:T(8,128)(2,1)S(1)}) fusion(bf16[1,2,64,8,1024]{4,3,2,1,0:T(8,128)(2,1)} %param.9), kind=kLoop, calls=%fused_computation.4 | loop fusion | bytes 4194304 | tf_op jit(solution)/shard_map/reshape;squeeze | solution.py:316
  89.5 6.1 %collective-permute-done.18.refs_9_ = bf16[2,128,1024]{2,1,0:T(8,128)(2,1)} collective-permute-done((bf16[2,128,1024]{2,1,0:T(8,128)(2,1)}, bf16[2,128,1024]{2,1,0:T(8,128)(2,1)}, u32[]{:S(2)}, u32[]{:S(2)}) %collective-permute-start.18) | collective-permute-done | bytes 524320 | tf_op jit(solution)/shard_map/ppermute | solution.py:33
  95.6 22.2 %collective-permute-done.17.refs_8_ = bf16[2,128,1024]{2,1,0:T(8,128)(2,1)} collective-permute-done((bf16[2,128,1024]{2,1,0:T(8,128)(2,1)}, bf16[2,128,1024]{2,1,0:T(8,128)(2,1)}, u32[]{:S(2)}, u32[]{:S(2)}) %collective-permute-start.17) | collective-permute-done | bytes 524320 | tf_op jit(solution)/shard_map/ppermute | solution.py:33
  117.8 1.4 collective-permute-done.16.refs_7_
  119.3 4.3 %shard_map.88 = (bf16[1024,1024]{1,0:T(8,128)(2,1)}, f32[2,16,3584]{2,1,0:T(8,128)S(1)}) custom-call(s32[1,256]{1,0:T(1,128)S(1)} %constant_dynamic-slice_fusion.source, s32[1024,1]{1,0:T(8,128)S(1)} %reshape.42.ids, f32[128,16]{1,0:T(8,128)S(1)} %bitcast.28, bf16[128,3584]{1,0:T(8,128)(2,1)S(1)} %bitcast.27, ...), custom_call_target="tpu_custom_call" | custom-call | flops 536870912 | bytes 8388608 | tf_op jit(solution)/shard_map/pallas_call | solution.py:227
  123.6 2.9 %collective-permute-start.19 = (f32[16,3584]{1,0:T(8,128)S(1)}, f32[16,3584]{1,0:T(8,128)S(1)}, u32[]{:S(2)}, u32[]{:S(2)}) collective-permute-start(f32[16,3584]{1,0:T(8,128)S(1)} %select_bitcast_fusion), channel_id=1, source_target_pairs={{0,1},{1,0},{2,3},{3,2},{4,5},{5,4},{6,7},{7,6},{8,9},{9,8},{10,11... | collective-permute-start | bytes 688136 | tf_op jit(solution)/shard_map/ppermute | solution.py:33
  128.0 3.4 %collective-permute-start.21 = (bf16[16,3584]{1,0:T(8,128)(2,1)S(1)}, bf16[16,3584]{1,0:T(8,128)(2,1)S(1)}, u32[]{:S(2)}, u32[]{:S(2)}) collective-permute-start(bf16[16,3584]{1,0:T(8,128)(2,1)S(1)} %fusion.4), channel_id=1, source_target_pairs={{0,4},{1,5},{2,6},{3,7},{4,8},{5,9},{6,10},{7,11},{8,12},{9,13},{1... | collective-permute-start | bytes 344072 | tf_op jit(solution)/shard_map/ppermute | solution.py:33
  131.8 1.7 %collective-permute-done.20 = bf16[16,3584]{1,0:T(8,128)(2,1)S(1)} collective-permute-done((bf16[16,3584]{1,0:T(8,128)(2,1)S(1)}, bf16[16,3584]{1,0:T(8,128)(2,1)S(1)}, u32[]{:S(2)}, u32[]{:S(2)}) %collective-permute-start.20) | collective-permute-done | bytes 114720 | tf_op jit(solution)/shard_map/ppermute | solution.py:33
  133.6 3.2 %collective-permute-done.21 = bf16[16,3584]{1,0:T(8,128)(2,1)S(1)} collective-permute-done((bf16[16,3584]{1,0:T(8,128)(2,1)S(1)}, bf16[16,3584]{1,0:T(8,128)(2,1)S(1)}, u32[]{:S(2)}, u32[]{:S(2)}) %collective-permute-start.21) | collective-permute-done | bytes 114720 | tf_op jit(solution)/shard_map/ppermute | solution.py:33
  137.2 6.0 %collective-permute-start.24 = (bf16[16,3584]{1,0:T(8,128)(2,1)S(1)}, bf16[16,3584]{1,0:T(8,128)(2,1)S(1)}, u32[]{:S(2)}, u32[]{:S(2)}) collective-permute-start(bf16[16,3584]{1,0:T(8,128)(2,1)S(1)} %add_convert_fusion), channel_id=1, source_target_pairs={{0,113},{1,112},{2,115},{3,114},{4,117},{5,116},{6,119},{7,118},{8... | collective-permute-start | bytes 344072 | tf_op jit(solution)/shard_map/ppermute | solution.py:46
  143.2 1.4 collective-permute-start.25
  144.6 3.1 %collective-permute-done.24 = bf16[16,3584]{1,0:T(8,128)(2,1)S(1)} collective-permute-done((bf16[16,3584]{1,0:T(8,128)(2,1)S(1)}, bf16[16,3584]{1,0:T(8,128)(2,1)S(1)}, u32[]{:S(2)}, u32[]{:S(2)}) %collective-permute-start.24) | collective-permute-done | bytes 114720 | tf_op jit(solution)/shard_map/ppermute | solution.py:46
  147.7 3.0 %collective-permute-done.25 = bf16[16,3584]{1,0:T(8,128)(2,1)S(1)} collective-permute-done((bf16[16,3584]{1,0:T(8,128)(2,1)S(1)}, bf16[16,3584]{1,0:T(8,128)(2,1)S(1)}, u32[]{:S(2)}, u32[]{:S(2)}) %collective-permute-start.25) | collective-permute-done | bytes 114720 | tf_op jit(solution)/shard_map/ppermute | solution.py:46
  150.9 1.5 collective-permute-done.26
  (46 shorter events, 6.9 us)
Async XLA Ops:
  0.6 85.7 %copy-start = (bf16[1,2,16,3584]{3,2,1,0:T(8,128)(2,1)S(1)}, bf16[1,2,16,3584]{3,2,1,0:T(8,128)(2,1)}, u32[]{:S(2)}) copy-start(bf16[1,2,16,3584]{3,2,1,0:T(8,128)(2,1)} %param.12) | copy-start | bytes 688132
  0.6 41.5 %collective-permute-start.7 = (bf16[2,1024,3584]{2,1,0:T(8,128)(2,1)}, bf16[2,1024,3584]{2,1,0:T(8,128)(2,1)}, u32[]{:S(2)}, u32[]{:S(2)}) collective-permute-start(bf16[2,1024,3584]{2,1,0:T(8,128)(2,1)} %bitcast.29), channel_id=1, source_target_pairs={{0,1},{1,0},{2,3},{3,2},{4,5},{5,4},{6,7},{7,6},{8,9},{9,8},{10,11... | collective-permute-start | bytes 44040200 | tf_op jit(solution)/shard_map/ppermute | solution.py:33
  3.4 27.2 %collective-permute-start = (bf16[128,3584]{1,0:T(8,128)(2,1)}, bf16[128,3584]{1,0:T(8,128)(2,1)S(1)}, u32[]{:S(2)}, u32[]{:S(2)}) collective-permute-start(bf16[128,3584]{1,0:T(8,128)(2,1)} %bitcast.32), channel_id=1, source_target_pairs={{0,2},{1,3},{2,0},{3,1},{4,6},{5,7},{6,4},{7,5},{8,10},{9,11},{10,... | collective-permute-start | bytes 2752520 | tf_op jit(solution)/shard_map/ppermute | solution.py:33
  6.4 13.0 %collective-permute-start.1 = (bf16[64,3584]{1,0:T(8,128)(2,1)S(1)}, bf16[64,3584]{1,0:T(8,128)(2,1)S(1)}, u32[]{:S(2)}, u32[]{:S(2)}) collective-permute-start(bf16[64,3584]{1,0:T(8,128)(2,1)S(1)} %get-tuple-element.35), channel_id=1, source_target_pairs={{0,4},{1,5},{2,6},{3,7},{4,8},{5,9},{6,10},{7,11},{8,12},{9,13},{1... | collective-permute-start | bytes 1376264 | tf_op jit(solution)/shard_map/ppermute | solution.py:33
  7.7 13.1 %collective-permute-start.4 = (bf16[64,3584]{1,0:T(8,128)(2,1)S(1)}, bf16[64,3584]{1,0:T(8,128)(2,1)S(1)}, u32[]{:S(2)}, u32[]{:S(2)}) collective-permute-start(bf16[64,3584]{1,0:T(8,128)(2,1)S(1)} %get-tuple-element.34), channel_id=1, source_target_pairs={{0,12},{1,13},{2,14},{3,15},{4,0},{5,1},{6,2},{7,3},{8,4},{9,5},{1... | collective-permute-start | bytes 1376264 | tf_op jit(solution)/shard_map/ppermute | solution.py:33
  9.1 20.2 %collective-permute-start.2 = (bf16[64,3584]{1,0:T(8,128)(2,1)S(1)}, bf16[64,3584]{1,0:T(8,128)(2,1)S(1)}, u32[]{:S(2)}, u32[]{:S(2)}) collective-permute-start(bf16[64,3584]{1,0:T(8,128)(2,1)S(1)} %get-tuple-element.34), channel_id=1, source_target_pairs={{0,4},{1,5},{2,6},{3,7},{4,8},{5,9},{6,10},{7,11},{8,12},{9,13},{1... | collective-permute-start | bytes 1376264 | tf_op jit(solution)/shard_map/ppermute | solution.py:33
  19.5 11.3 %collective-permute-start.3 = (bf16[64,3584]{1,0:T(8,128)(2,1)S(1)}, bf16[64,3584]{1,0:T(8,128)(2,1)S(1)}, u32[]{:S(2)}, u32[]{:S(2)}) collective-permute-start(bf16[64,3584]{1,0:T(8,128)(2,1)S(1)} %get-tuple-element.35), channel_id=1, source_target_pairs={{0,12},{1,13},{2,14},{3,15},{4,0},{5,1},{6,2},{7,3},{8,4},{9,5},{1... | collective-permute-start | bytes 1376264 | tf_op jit(solution)/shard_map/ppermute | solution.py:33
  20.7 18.4 %collective-permute-start.5 = (bf16[64,3584]{1,0:T(8,128)(2,1)S(1)}, bf16[64,3584]{1,0:T(8,128)(2,1)S(1)}, u32[]{:S(2)}, u32[]{:S(2)}) collective-permute-start(bf16[64,3584]{1,0:T(8,128)(2,1)S(1)} %collective-permute-done.1.refs_2_), channel_id=1, source_target_pairs={{0,4},{1,5},{2,6},{3,7},{4,8},{5,9},{6,10},{7,11},{8,12},{9,13},{1... | collective-permute-start | bytes 1376264 | tf_op jit(solution)/shard_map/ppermute | solution.py:33
  29.3 10.2 %collective-permute-start.6 = (bf16[64,3584]{1,0:T(8,128)(2,1)S(1)}, bf16[64,3584]{1,0:T(8,128)(2,1)S(1)}, u32[]{:S(2)}, u32[]{:S(2)}) collective-permute-start(bf16[64,3584]{1,0:T(8,128)(2,1)S(1)} %collective-permute-done.4.refs_5_), channel_id=1, source_target_pairs={{0,12},{1,13},{2,14},{3,15},{4,0},{5,1},{6,2},{7,3},{8,4},{9,5},{1... | collective-permute-start | bytes 1376264 | tf_op jit(solution)/shard_map/ppermute | solution.py:33
  30.6 11.5 %copy-start.3 = (bf16[128,3584]{1,0:T(8,128)(2,1)}, bf16[128,3584]{1,0:T(8,128)(2,1)S(1)}, u32[]{:S(2)}) copy-start(bf16[128,3584]{1,0:T(8,128)(2,1)S(1)} %collective-permute-done.refs_1_) | copy-start | bytes 2752516
  30.6 28.2 %collective-permute-start.12 = (bf16[128,3584]{1,0:T(8,128)(2,1)S(1)}, bf16[128,3584]{1,0:T(8,128)(2,1)S(1)}, u32[]{:S(2)}, u32[]{:S(2)}) collective-permute-start(bf16[128,3584]{1,0:T(8,128)(2,1)S(1)} %collective-permute-done.refs_1_), channel_id=1, source_target_pairs={{0,4},{1,5},{2,6},{3,7},{4,8},{5,9},{6,10},{7,11},{8,12},{9,13},{1... | collective-permute-start | bytes 2752520 | tf_op jit(solution)/shard_map/ppermute | solution.py:33
  30.8 31.7 %collective-permute-start.13 = (bf16[128,3584]{1,0:T(8,128)(2,1)S(1)}, bf16[128,3584]{1,0:T(8,128)(2,1)S(1)}, u32[]{:S(2)}, u32[]{:S(2)}) collective-permute-start(bf16[128,3584]{1,0:T(8,128)(2,1)S(1)} %collective-permute-done.refs_1_), channel_id=1, source_target_pairs={{0,12},{1,13},{2,14},{3,15},{4,0},{5,1},{6,2},{7,3},{8,4},{9,5},{1... | collective-permute-start | bytes 2752520 | tf_op jit(solution)/shard_map/ppermute | solution.py:33
  39.1 19.9 %collective-permute-start.14 = (bf16[64,3584]{1,0:T(8,128)(2,1)S(1)}, bf16[64,3584]{1,0:T(8,128)(2,1)S(1)}, u32[]{:S(2)}, u32[]{:S(2)}) collective-permute-start(bf16[64,3584]{1,0:T(8,128)(2,1)S(1)} %collective-permute-done.5.refs_6_), channel_id=1, source_target_pairs={{0,2},{1,3},{2,0},{3,1},{4,6},{5,7},{6,4},{7,5},{8,10},{9,11},{10,... | collective-permute-start | bytes 1376264 | tf_op jit(solution)/shard_map/ppermute | solution.py:33
  39.5 21.9 %collective-permute-start.15 = (bf16[64,3584]{1,0:T(8,128)(2,1)S(1)}, bf16[64,3584]{1,0:T(8,128)(2,1)S(1)}, u32[]{:S(2)}, u32[]{:S(2)}) collective-permute-start(bf16[64,3584]{1,0:T(8,128)(2,1)S(1)} %collective-permute-done.6.refs_7_), channel_id=1, source_target_pairs={{0,2},{1,3},{2,0},{3,1},{4,6},{5,7},{6,4},{7,5},{8,10},{9,11},{10,... | collective-permute-start | bytes 1376264 | tf_op jit(solution)/shard_map/ppermute | solution.py:33
  58.8 18.4 %collective-permute-start.8 = (bf16[2,128,1024]{2,1,0:T(8,128)(2,1)S(1)}, bf16[2,128,1024]{2,1,0:T(8,128)(2,1)S(1)}, u32[]{:S(2)}, u32[]{:S(2)}) collective-permute-start(bf16[2,128,1024]{2,1,0:T(8,128)(2,1)S(1)} %get-tuple-element.19), channel_id=1, source_target_pairs={{0,2},{1,3},{2,0},{3,1},{4,6},{5,7},{6,4},{7,5},{8,10},{9,11},{10,... | collective-permute-start | bytes 1572872 | tf_op jit(solution)/shard_map/ppermute | solution.py:33
  59.0 22.3 %collective-permute-start.10 = (bf16[2,128,1024]{2,1,0:T(8,128)(2,1)S(1)}, bf16[2,128,1024]{2,1,0:T(8,128)(2,1)S(1)}, u32[]{:S(2)}, u32[]{:S(2)}) collective-permute-start(bf16[2,128,1024]{2,1,0:T(8,128)(2,1)S(1)} %get-tuple-element.21), channel_id=1, source_target_pairs={{0,4},{1,5},{2,6},{3,7},{4,8},{5,9},{6,10},{7,11},{8,12},{9,13},{1... | collective-permute-start | bytes 1572872 | tf_op jit(solution)/shard_map/ppermute | solution.py:33
  59.0 30.5 %collective-permute-start.11 = (bf16[2,128,1024]{2,1,0:T(8,128)(2,1)}, bf16[2,128,1024]{2,1,0:T(8,128)(2,1)}, u32[]{:S(2)}, u32[]{:S(2)}) collective-permute-start(bf16[2,128,1024]{2,1,0:T(8,128)(2,1)} %get-tuple-element.22), channel_id=1, source_target_pairs={{0,8},{1,9},{2,10},{3,11},{4,12},{5,13},{6,14},{7,15},{8,0},{9,1},... | collective-permute-start | bytes 1572872 | tf_op jit(solution)/shard_map/ppermute | solution.py:33
  61.4 25.0 %copy-start.1 = (bf16[1,2,64,3584]{3,2,1,0:T(8,128)(2,1)S(1)}, bf16[1,2,64,3584]{3,2,1,0:T(8,128)(2,1)}, u32[]{:S(2)}) copy-start(bf16[1,2,64,3584]{3,2,1,0:T(8,128)(2,1)} %param.8) | copy-start | bytes 2752516
  61.4 25.3 %copy-start.2 = (s32[1,2,64,8]{2,3,1,0:T(8,128)S(1)}, s32[1,2,64,8]{2,3,1,0:T(8,128)}, u32[]{:S(2)}) copy-start(s32[1,2,64,8]{2,3,1,0:T(8,128)} %param.10) | copy-start | bytes 12292
  61.4 28.2 %collective-permute-start.9 = (bf16[2,128,1024]{2,1,0:T(8,128)(2,1)}, bf16[2,128,1024]{2,1,0:T(8,128)(2,1)}, u32[]{:S(2)}, u32[]{:S(2)}) collective-permute-start(bf16[2,128,1024]{2,1,0:T(8,128)(2,1)} %get-tuple-element.20), channel_id=1, source_target_pairs={{0,12},{1,13},{2,14},{3,15},{4,0},{5,1},{6,2},{7,3},{8,4},{9,5},{1... | collective-permute-start | bytes 1572872 | tf_op jit(solution)/shard_map/ppermute | solution.py:33
  77.2 18.5 %collective-permute-start.18 = (bf16[2,128,1024]{2,1,0:T(8,128)(2,1)}, bf16[2,128,1024]{2,1,0:T(8,128)(2,1)}, u32[]{:S(2)}, u32[]{:S(2)}) collective-permute-start(bf16[2,128,1024]{2,1,0:T(8,128)(2,1)} %get-tuple-element.29), channel_id=1, source_target_pairs={{0,10},{1,11},{2,8},{3,9},{4,14},{5,15},{6,12},{7,13},{8,2},{9,3},... | collective-permute-start | bytes 1572872 | tf_op jit(solution)/shard_map/ppermute | solution.py:33
  81.2 36.6 %collective-permute-start.17 = (bf16[2,128,1024]{2,1,0:T(8,128)(2,1)}, bf16[2,128,1024]{2,1,0:T(8,128)(2,1)}, u32[]{:S(2)}, u32[]{:S(2)}) collective-permute-start(bf16[2,128,1024]{2,1,0:T(8,128)(2,1)} %get-tuple-element.27), channel_id=1, source_target_pairs={{0,6},{1,7},{2,4},{3,5},{4,10},{5,11},{6,8},{7,9},{8,14},{9,15},{1... | collective-permute-start | bytes 1572872 | tf_op jit(solution)/shard_map/ppermute | solution.py:33
  81.3 38.0 %collective-permute-start.16 = (bf16[2,128,1024]{2,1,0:T(8,128)(2,1)}, bf16[2,128,1024]{2,1,0:T(8,128)(2,1)}, u32[]{:S(2)}, u32[]{:S(2)}) collective-permute-start(bf16[2,128,1024]{2,1,0:T(8,128)(2,1)} %get-tuple-element.25), channel_id=1, source_target_pairs={{0,14},{1,15},{2,12},{3,13},{4,2},{5,3},{6,0},{7,1},{8,6},{9,7},{1... | collective-permute-start | bytes 1572872 | tf_op jit(solution)/shard_map/ppermute | solution.py:33
  123.6 4.0 %collective-permute-start.19 = (f32[16,3584]{1,0:T(8,128)S(1)}, f32[16,3584]{1,0:T(8,128)S(1)}, u32[]{:S(2)}, u32[]{:S(2)}) collective-permute-start(f32[16,3584]{1,0:T(8,128)S(1)} %select_bitcast_fusion), channel_id=1, source_target_pairs={{0,1},{1,0},{2,3},{3,2},{4,5},{5,4},{6,7},{7,6},{8,9},{9,8},{10,11... | collective-permute-start | bytes 688136 | tf_op jit(solution)/shard_map/ppermute | solution.py:33
  127.6 5.9 %collective-permute-start.20 = (bf16[16,3584]{1,0:T(8,128)(2,1)S(1)}, bf16[16,3584]{1,0:T(8,128)(2,1)S(1)}, u32[]{:S(2)}, u32[]{:S(2)}) collective-permute-start(bf16[16,3584]{1,0:T(8,128)(2,1)S(1)} %fusion.4), channel_id=1, source_target_pairs={{0,8},{1,9},{2,10},{3,11},{4,12},{5,13},{6,14},{7,15},{8,0},{9,1},... | collective-permute-start | bytes 344072 | tf_op jit(solution)/shard_map/ppermute | solution.py:33
  128.0 8.7 %collective-permute-start.21 = (bf16[16,3584]{1,0:T(8,128)(2,1)S(1)}, bf16[16,3584]{1,0:T(8,128)(2,1)S(1)}, u32[]{:S(2)}, u32[]{:S(2)}) collective-permute-start(bf16[16,3584]{1,0:T(8,128)(2,1)S(1)} %fusion.4), channel_id=1, source_target_pairs={{0,4},{1,5},{2,6},{3,7},{4,8},{5,9},{6,10},{7,11},{8,12},{9,13},{1... | collective-permute-start | bytes 344072 | tf_op jit(solution)/shard_map/ppermute | solution.py:33
  131.5 5.4 %collective-permute-start.22 = (bf16[16,3584]{1,0:T(8,128)(2,1)S(1)}, bf16[16,3584]{1,0:T(8,128)(2,1)S(1)}, u32[]{:S(2)}, u32[]{:S(2)}) collective-permute-start(bf16[16,3584]{1,0:T(8,128)(2,1)S(1)} %fusion.4), channel_id=1, source_target_pairs={{0,12},{1,13},{2,14},{3,15},{4,0},{5,1},{6,2},{7,3},{8,4},{9,5},{1... | collective-permute-start | bytes 344072 | tf_op jit(solution)/shard_map/ppermute | solution.py:33
  136.9 7.7 %collective-permute-start.23 = (bf16[16,3584]{1,0:T(8,128)(2,1)S(1)}, bf16[16,3584]{1,0:T(8,128)(2,1)S(1)}, u32[]{:S(2)}, u32[]{:S(2)}) collective-permute-start(bf16[16,3584]{1,0:T(8,128)(2,1)S(1)} %add_convert_fusion), channel_id=1, source_target_pairs={{0,2},{1,3},{2,0},{3,1},{4,6},{5,7},{6,4},{7,5},{8,10},{9,11},{10,... | collective-permute-start | bytes 344072 | tf_op jit(solution)/shard_map/ppermute | solution.py:33
  137.2 10.5 %collective-permute-start.24 = (bf16[16,3584]{1,0:T(8,128)(2,1)S(1)}, bf16[16,3584]{1,0:T(8,128)(2,1)S(1)}, u32[]{:S(2)}, u32[]{:S(2)}) collective-permute-start(bf16[16,3584]{1,0:T(8,128)(2,1)S(1)} %add_convert_fusion), channel_id=1, source_target_pairs={{0,113},{1,112},{2,115},{3,114},{4,117},{5,116},{6,119},{7,118},{8... | collective-permute-start | bytes 344072 | tf_op jit(solution)/shard_map/ppermute | solution.py:46
  143.2 7.5 %collective-permute-start.25 = (bf16[16,3584]{1,0:T(8,128)(2,1)S(1)}, bf16[16,3584]{1,0:T(8,128)(2,1)S(1)}, u32[]{:S(2)}, u32[]{:S(2)}) collective-permute-start(bf16[16,3584]{1,0:T(8,128)(2,1)S(1)} %add_convert_fusion), channel_id=1, source_target_pairs={{0,115},{1,114},{2,113},{3,112},{4,119},{5,118},{6,117},{7,116},{8... | collective-permute-start | bytes 344072 | tf_op jit(solution)/shard_map/ppermute | solution.py:46
  150.8 1.6 %collective-permute-start.26 = (f32[16,3584]{1,0:T(8,128)S(1)}, f32[16,3584]{1,0:T(8,128)S(1)}, u32[]{:S(2)}, u32[]{:S(2)}) collective-permute-start(f32[16,3584]{1,0:T(8,128)S(1)} %add_add_fusion), channel_id=1, source_target_pairs={{0,1},{1,0},{2,3},{3,2},{4,5},{5,4},{6,7},{7,6},{8,9},{9,8},{10,11... | collective-permute-start | bytes 688136 | tf_op jit(solution)/shard_map/ppermute | solution.py:33

commit v5 on v4

--- a/solution.py
+++ b/solution.py
@@ -135,7 +135,7 @@
         blocks += shard
     n = len(shards)
     _, hid, depth = own.shape
-    tok = blocks[0].shape[0] // 2
+    tok = max(b.shape[0] for b in blocks) // 2
     wide, depth_of = 512, 2
     anywhere = pl.BlockSpec(memory_space=pl.ANY)
     return pl.pallas_call(
@@ -151,7 +151,7 @@
             pltpu.SemaphoreType.DMA((depth_of, NC)),
             pltpu.SemaphoreType.DMA((2, n)),
         ],
-        compiler_params=pltpu.CompilerParams(vmem_limit_bytes=48 * MIB),
+        compiler_params=pltpu.CompilerParams(vmem_limit_bytes=40 * MIB),
         cost_estimate=pl.CostEstimate(
             flops=8 * n * tok * depth * hid,
             bytes_accessed=8 * hid * depth + 4 * n * tok * (depth + 2 * hid),
@@ -282,15 +282,15 @@
     own = out_grad.reshape(rows, depth)
     weight = down_weight.reshape(2, hid, depth)
 
+    across = send(own, 0, 1, 0)
     sibling_weight = send(weight, 0, 0, 1)
     first, second = out_grad[0, 0], out_grad[0, 1]
-    across = send(after(own, first, second), 0, 1, 0)
     low, high = [send(first, 1, 0, 0)], [send(second, -1, 0, 0)]
     far = send(low[0], 1, 0, 0), send(high[0], -1, 0, 0)
     low, high = (low[0], send(second, 1, 0, 0)), (send(first, -1, 0, 0), high[0])
     far_across = send(far[0], 0, 1, 0), send(far[1], 0, 1, 0)
     low_across, high_across = send(across, 1, 0, 0), send(across, -1, 0, 0)
-    early = project([own, across, low, high, far], weight, sibling_weight)
+    early = project([(first, second), across, low, high, far], weight, sibling_weight)
     low_across = after(low_across, early[0])
     late = project([low_across, high_across, far_across], weight, sibling_weight)
     places = [(0, 0), (0, 1), (-1, 0), (1, 0), (2, 0), (-1, 1), (1, 1), (2, 1)]

time: 153 us -> 153 us (level)
  transfers between devices with their start and end apart: 27 -> 27, of which waited for: 15 -> 14; matrix products, arithmetic and copies ran while one was open for 3% -> 3% of each run, Pallas kernels for 19% -> 20%
where the time goes in v5:
time: 153 us
  waiting for transfers between devices  68.3 us (45%)
  starting transfers between devices  44.1 us (29%)
  Pallas kernels  34.5 us (23%)
  local copies, waits for them, and re-layouts  4.01 us (3%)
    ppermute x25, waiting for transfers between devices, send(): return lax.ppermute(block, 'expert', shift(dx, dy, dc))  62.2 us
    ppermute x25, starting transfers between devices, send(): return lax.ppermute(block, 'expert', shift(dx, dy, dc))  36.6 us
    pallas_call x2, Pallas kernels, project(): pl.pallas_call(functools.partial(project_kernel, layout, depth_of), in_sp...  30.3 us
    ppermute x2, starting transfers between devices, send_mirror(): return lax.ppermute(block, ('pipe', 'expert'), route)  7.51 us
    ppermute x2, waiting for transfers between devices, send_mirror(): return lax.ppermute(block, ('pipe', 'expert'), route)  6.1 us
    pallas_call x1, Pallas kernels, token_math(): pl.pallas_call(functools.partial(token_kernel, n), in_specs=[inside] * (6...  4.27 us
  transfers between devices with their start and end apart: 27, of which 14 were waited for; matrix products, arithmetic and copies ran while one was open for 3% of the time, Pallas kernels for 20%

profile of v5, /device:TPU:1, one launch (start us, length us, event | category | flops | bytes accessed | tf_op | source)
XLA Modules:
  0.0 153.1 jit_solution(8913627482402479091)
XLA Ops:
  0.6 1.5 collective-permute-start.7
  2.1 3.0 %collective-permute-start = (bf16[128,3584]{1,0:T(8,128)(2,1)}, bf16[128,3584]{1,0:T(8,128)(2,1)S(1)}, u32[]{:S(2)}, u32[]{:S(2)}) collective-permute-start(bf16[128,3584]{1,0:T(8,128)(2,1)} %bitcast.32), channel_id=1, source_target_pairs={{0,2},{1,3},{2,0},{3,1},{4,6},{5,7},{6,4},{7,5},{8,10},{9,11},{10,... | collective-permute-start | bytes 2752520 | tf_op jit(solution)/shard_map/ppermute | solution.py:33
  5.2 1.2 slice_bitcast_fusion.2
  6.4 1.3 collective-permute-start.1
  7.7 1.5 collective-permute-start.4
  9.1 10.3 %collective-permute-done.1.refs_3_ = bf16[64,3584]{1,0:T(8,128)(2,1)S(1)} collective-permute-done((bf16[64,3584]{1,0:T(8,128)(2,1)S(1)}, bf16[64,3584]{1,0:T(8,128)(2,1)S(1)}, u32[]{:S(2)}, u32[]{:S(2)}) %collective-permute-start.1) | collective-permute-done | bytes 458784 | tf_op jit(solution)/shard_map/ppermute | solution.py:33
  19.4 1.3 collective-permute-start.3
  20.9 8.4 %collective-permute-done.2.refs_4_ = bf16[64,3584]{1,0:T(8,128)(2,1)S(1)} collective-permute-done((bf16[64,3584]{1,0:T(8,128)(2,1)S(1)}, bf16[64,3584]{1,0:T(8,128)(2,1)S(1)}, u32[]{:S(2)}, u32[]{:S(2)}) %collective-permute-start.2) | collective-permute-done | bytes 458784 | tf_op jit(solution)/shard_map/ppermute | solution.py:33
  29.2 1.3 collective-permute-start.6
  30.7 2.5 %collective-permute-start.13 = (bf16[128,3584]{1,0:T(8,128)(2,1)S(1)}, bf16[128,3584]{1,0:T(8,128)(2,1)S(1)}, u32[]{:S(2)}, u32[]{:S(2)}) collective-permute-start(bf16[128,3584]{1,0:T(8,128)(2,1)S(1)} %collective-permute-done.refs_2_), channel_id=1, source_target_pairs={{0,12},{1,13},{2,14},{3,15},{4,0},{5,1},{6,2},{7,3},{8,4},{9,5},{1... | collective-permute-start | bytes 2752520 | tf_op jit(solution)/shard_map/ppermute | solution.py:33
  33.2 5.9 %collective-permute-done.5.refs_7_ = bf16[64,3584]{1,0:T(8,128)(2,1)S(1)} collective-permute-done((bf16[64,3584]{1,0:T(8,128)(2,1)S(1)}, bf16[64,3584]{1,0:T(8,128)(2,1)S(1)}, u32[]{:S(2)}, u32[]{:S(2)}) %collective-permute-start.5) | collective-permute-done | bytes 458784 | tf_op jit(solution)/shard_map/ppermute | solution.py:33
  39.3 2.8 %collective-permute-start.15 = (bf16[64,3584]{1,0:T(8,128)(2,1)S(1)}, bf16[64,3584]{1,0:T(8,128)(2,1)S(1)}, u32[]{:S(2)}, u32[]{:S(2)}) collective-permute-start(bf16[64,3584]{1,0:T(8,128)(2,1)S(1)} %collective-permute-done.6.refs_8_), channel_id=1, source_target_pairs={{0,2},{1,3},{2,0},{3,1},{4,6},{5,7},{6,4},{7,5},{8,10},{9,11},{10,... | collective-permute-start | bytes 1376264 | tf_op jit(solution)/shard_map/ppermute | solution.py:33
  42.0 15.6 %shard_map.86 = (bf16[2,128,1024]{2,1,0:T(8,128)(2,1)S(1)}, bf16[2,128,1024]{2,1,0:T(8,128)(2,1)S(1)}, bf16[2,128,1024]{2,1,0:T(8,128)(2,1)}, bf16[2,128,1024]{2,1,0:T(8,128)(2,1)S(1)}, bf16[2,128,1024]{2,1,0:T(8,128)(2,1)}) custom-call(bf16[64,3584]{1,0:T(8,128)(2,1)S(1)} %get-tuple-element.33.refs_0_, bf16[64,3584]{1,0:T(8,128)(2,1)S(1)} %get-tuple-element.32.refs_1_, ...), custom_call_target="tpu_custom_call" | custom-call | flops 9395240960 | bytes 36569088 | tf_op jit(solution)/shard_map/pallas_call | solution.py:141
  57.7 1.1 collective-permute-done.12.refs_0_
  58.8 2.8 %collective-permute-start.11 = (bf16[2,128,1024]{2,1,0:T(8,128)(2,1)}, bf16[2,128,1024]{2,1,0:T(8,128)(2,1)}, u32[]{:S(2)}, u32[]{:S(2)}) collective-permute-start(bf16[2,128,1024]{2,1,0:T(8,128)(2,1)} %get-tuple-element.20), channel_id=1, source_target_pairs={{0,8},{1,9},{2,10},{3,11},{4,12},{5,13},{6,14},{7,15},{8,0},{9,1},... | collective-permute-start | bytes 1572872 | tf_op jit(solution)/shard_map/ppermute | solution.py:33
  62.4 14.6 %shard_map.87 = (bf16[2,128,1024]{2,1,0:T(8,128)(2,1)}, bf16[2,128,1024]{2,1,0:T(8,128)(2,1)}, bf16[2,128,1024]{2,1,0:T(8,128)(2,1)}) custom-call(bf16[128,3584]{1,0:T(8,128)(2,1)S(1)} %collective-permute-done.12.refs_0_, bf16[128,3584]{1,0:T(8,128)(2,1)S(1)} %collective-permute-done.13.refs_1_, bf16[64,3584]{1,0:T(8,128)(2,1)S(1)} %collective-permute-done.14.refs_2_, ...), custom_call_target="tpu_custom_call" | custom-call | flops 5637144576 | bytes 33685504 | tf_op jit(solution)/shard_map/pallas_call | solution.py:141
  77.1 4.1 %collective-permute-start.18 = (bf16[2,128,1024]{2,1,0:T(8,128)(2,1)}, bf16[2,128,1024]{2,1,0:T(8,128)(2,1)}, u32[]{:S(2)}, u32[]{:S(2)}) collective-permute-start(bf16[2,128,1024]{2,1,0:T(8,128)(2,1)} %get-tuple-element.27), channel_id=1, source_target_pairs={{0,10},{1,11},{2,8},{3,9},{4,14},{5,15},{6,12},{7,13},{8,2},{9,3},... | collective-permute-start | bytes 1572872 | tf_op jit(solution)/shard_map/ppermute | solution.py:33
  81.2 5.1 %collective-permute-start.16 = (bf16[2,128,1024]{2,1,0:T(8,128)(2,1)}, bf16[2,128,1024]{2,1,0:T(8,128)(2,1)}, u32[]{:S(2)}, u32[]{:S(2)}) collective-permute-start(bf16[2,128,1024]{2,1,0:T(8,128)(2,1)} %get-tuple-element.23), channel_id=1, source_target_pairs={{0,14},{1,15},{2,12},{3,13},{4,2},{5,3},{6,0},{7,1},{8,6},{9,7},{1... | collective-permute-start | bytes 1572872 | tf_op jit(solution)/shard_map/ppermute | solution.py:33
  87.8 1.7 %slice_bitcast_fusion = (bf16[512,1024]{1,0:T(8,128)(2,1)S(1)}, bf16[512,1024]{1,0:T(8,128)(2,1)S(1)}) fusion(bf16[1,2,64,8,1024]{4,3,2,1,0:T(8,128)(2,1)} %param.9), kind=kLoop, calls=%fused_computation.4 | loop fusion | bytes 4194304 | tf_op jit(solution)/shard_map/reshape;squeeze | solution.py:316
  89.5 5.9 %collective-permute-done.18.refs_9_ = bf16[2,128,1024]{2,1,0:T(8,128)(2,1)} collective-permute-done((bf16[2,128,1024]{2,1,0:T(8,128)(2,1)}, bf16[2,128,1024]{2,1,0:T(8,128)(2,1)}, u32[]{:S(2)}, u32[]{:S(2)}) %collective-permute-start.18) | collective-permute-done | bytes 524320 | tf_op jit(solution)/shard_map/ppermute | solution.py:33
  95.4 22.9 %collective-permute-done.17.refs_8_ = bf16[2,128,1024]{2,1,0:T(8,128)(2,1)} collective-permute-done((bf16[2,128,1024]{2,1,0:T(8,128)(2,1)}, bf16[2,128,1024]{2,1,0:T(8,128)(2,1)}, u32[]{:S(2)}, u32[]{:S(2)}) %collective-permute-start.17) | collective-permute-done | bytes 524320 | tf_op jit(solution)/shard_map/ppermute | solution.py:33
  118.3 4.3 %shard_map.88 = (bf16[1024,1024]{1,0:T(8,128)(2,1)}, f32[2,16,3584]{2,1,0:T(8,128)S(1)}) custom-call(s32[1,256]{1,0:T(1,128)S(1)} %constant_dynamic-slice_fusion.source, s32[1024,1]{1,0:T(8,128)S(1)} %reshape.42.ids, f32[128,16]{1,0:T(8,128)S(1)} %bitcast.28, bf16[128,3584]{1,0:T(8,128)(2,1)S(1)} %bitcast.27, ...), custom_call_target="tpu_custom_call" | custom-call | flops 536870912 | bytes 8388608 | tf_op jit(solution)/shard_map/pallas_call | solution.py:227
  122.6 3.8 %collective-permute-start.19 = (f32[16,3584]{1,0:T(8,128)S(1)}, f32[16,3584]{1,0:T(8,128)S(1)}, u32[]{:S(2)}, u32[]{:S(2)}) collective-permute-start(f32[16,3584]{1,0:T(8,128)S(1)} %select_bitcast_fusion), channel_id=1, source_target_pairs={{0,1},{1,0},{2,3},{3,2},{4,5},{5,4},{6,7},{7,6},{8,9},{9,8},{10,11... | collective-permute-start | bytes 688136 | tf_op jit(solution)/shard_map/ppermute | solution.py:33
  126.4 1.1 collective-permute-done.19
  128.0 3.4 %collective-permute-start.21 = (bf16[16,3584]{1,0:T(8,128)(2,1)S(1)}, bf16[16,3584]{1,0:T(8,128)(2,1)S(1)}, u32[]{:S(2)}, u32[]{:S(2)}) collective-permute-start(bf16[16,3584]{1,0:T(8,128)(2,1)S(1)} %fusion.4), channel_id=1, source_target_pairs={{0,4},{1,5},{2,6},{3,7},{4,8},{5,9},{6,10},{7,11},{8,12},{9,13},{1... | collective-permute-start | bytes 344072 | tf_op jit(solution)/shard_map/ppermute | solution.py:33
  131.8 1.7 %collective-permute-done.20 = bf16[16,3584]{1,0:T(8,128)(2,1)S(1)} collective-permute-done((bf16[16,3584]{1,0:T(8,128)(2,1)S(1)}, bf16[16,3584]{1,0:T(8,128)(2,1)S(1)}, u32[]{:S(2)}, u32[]{:S(2)}) %collective-permute-start.20) | collective-permute-done | bytes 114720 | tf_op jit(solution)/shard_map/ppermute | solution.py:33
  133.5 3.2 %collective-permute-done.21 = bf16[16,3584]{1,0:T(8,128)(2,1)S(1)} collective-permute-done((bf16[16,3584]{1,0:T(8,128)(2,1)S(1)}, bf16[16,3584]{1,0:T(8,128)(2,1)S(1)}, u32[]{:S(2)}, u32[]{:S(2)}) %collective-permute-start.21) | collective-permute-done | bytes 114720 | tf_op jit(solution)/shard_map/ppermute | solution.py:33
  137.0 6.1 %collective-permute-start.24 = (bf16[16,3584]{1,0:T(8,128)(2,1)S(1)}, bf16[16,3584]{1,0:T(8,128)(2,1)S(1)}, u32[]{:S(2)}, u32[]{:S(2)}) collective-permute-start(bf16[16,3584]{1,0:T(8,128)(2,1)S(1)} %add_convert_fusion), channel_id=1, source_target_pairs={{0,113},{1,112},{2,115},{3,114},{4,117},{5,116},{6,119},{7,118},{8... | collective-permute-start | bytes 344072 | tf_op jit(solution)/shard_map/ppermute | solution.py:46
  143.1 1.4 collective-permute-start.25
  144.5 3.1 %collective-permute-done.24 = bf16[16,3584]{1,0:T(8,128)(2,1)S(1)} collective-permute-done((bf16[16,3584]{1,0:T(8,128)(2,1)S(1)}, bf16[16,3584]{1,0:T(8,128)(2,1)S(1)}, u32[]{:S(2)}, u32[]{:S(2)}) %collective-permute-start.24) | collective-permute-done | bytes 114720 | tf_op jit(solution)/shard_map/ppermute | solution.py:46
  147.6 3.0 %collective-permute-done.25 = bf16[16,3584]{1,0:T(8,128)(2,1)S(1)} collective-permute-done((bf16[16,3584]{1,0:T(8,128)(2,1)S(1)}, bf16[16,3584]{1,0:T(8,128)(2,1)S(1)}, u32[]{:S(2)}, u32[]{:S(2)}) %collective-permute-start.25) | collective-permute-done | bytes 114720 | tf_op jit(solution)/shard_map/ppermute | solution.py:46
  150.8 1.5 collective-permute-done.26
  (44 shorter events, 5.1 us)
Async XLA Ops:
  0.6 85.7 %copy-start = (bf16[1,2,16,3584]{3,2,1,0:T(8,128)(2,1)S(1)}, bf16[1,2,16,3584]{3,2,1,0:T(8,128)(2,1)}, u32[]{:S(2)}) copy-start(bf16[1,2,16,3584]{3,2,1,0:T(8,128)(2,1)} %param.12) | copy-start | bytes 688132
  0.6 41.4 %collective-permute-start.7 = (bf16[2,1024,3584]{2,1,0:T(8,128)(2,1)}, bf16[2,1024,3584]{2,1,0:T(8,128)(2,1)}, u32[]{:S(2)}, u32[]{:S(2)}) collective-permute-start(bf16[2,1024,3584]{2,1,0:T(8,128)(2,1)} %bitcast.29), channel_id=1, source_target_pairs={{0,1},{1,0},{2,3},{3,2},{4,5},{5,4},{6,7},{7,6},{8,9},{9,8},{10,11... | collective-permute-start | bytes 44040200 | tf_op jit(solution)/shard_map/ppermute | solution.py:33
  2.1 28.4 %collective-permute-start = (bf16[128,3584]{1,0:T(8,128)(2,1)}, bf16[128,3584]{1,0:T(8,128)(2,1)S(1)}, u32[]{:S(2)}, u32[]{:S(2)}) collective-permute-start(bf16[128,3584]{1,0:T(8,128)(2,1)} %bitcast.32), channel_id=1, source_target_pairs={{0,2},{1,3},{2,0},{3,1},{4,6},{5,7},{6,4},{7,5},{8,10},{9,11},{10,... | collective-permute-start | bytes 2752520 | tf_op jit(solution)/shard_map/ppermute | solution.py:33
  6.4 13.0 %collective-permute-start.1 = (bf16[64,3584]{1,0:T(8,128)(2,1)S(1)}, bf16[64,3584]{1,0:T(8,128)(2,1)S(1)}, u32[]{:S(2)}, u32[]{:S(2)}) collective-permute-start(bf16[64,3584]{1,0:T(8,128)(2,1)S(1)} %get-tuple-element.33.refs_0_), channel_id=1, source_target_pairs={{0,4},{1,5},{2,6},{3,7},{4,8},{5,9},{6,10},{7,11},{8,12},{9,13},{1... | collective-permute-start | bytes 1376264 | tf_op jit(solution)/shard_map/ppermute | solution.py:33
  7.7 13.0 %collective-permute-start.4 = (bf16[64,3584]{1,0:T(8,128)(2,1)S(1)}, bf16[64,3584]{1,0:T(8,128)(2,1)S(1)}, u32[]{:S(2)}, u32[]{:S(2)}) collective-permute-start(bf16[64,3584]{1,0:T(8,128)(2,1)S(1)} %get-tuple-element.32.refs_1_), channel_id=1, source_target_pairs={{0,12},{1,13},{2,14},{3,15},{4,0},{5,1},{6,2},{7,3},{8,4},{9,5},{1... | collective-permute-start | bytes 1376264 | tf_op jit(solution)/shard_map/ppermute | solution.py:33
  9.1 20.1 %collective-permute-start.2 = (bf16[64,3584]{1,0:T(8,128)(2,1)S(1)}, bf16[64,3584]{1,0:T(8,128)(2,1)S(1)}, u32[]{:S(2)}, u32[]{:S(2)}) collective-permute-start(bf16[64,3584]{1,0:T(8,128)(2,1)S(1)} %get-tuple-element.32.refs_1_), channel_id=1, source_target_pairs={{0,4},{1,5},{2,6},{3,7},{4,8},{5,9},{6,10},{7,11},{8,12},{9,13},{1... | collective-permute-start | bytes 1376264 | tf_op jit(solution)/shard_map/ppermute | solution.py:33
  19.4 11.3 %collective-permute-start.3 = (bf16[64,3584]{1,0:T(8,128)(2,1)S(1)}, bf16[64,3584]{1,0:T(8,128)(2,1)S(1)}, u32[]{:S(2)}, u32[]{:S(2)}) collective-permute-start(bf16[64,3584]{1,0:T(8,128)(2,1)S(1)} %get-tuple-element.33.refs_0_), channel_id=1, source_target_pairs={{0,12},{1,13},{2,14},{3,15},{4,0},{5,1},{6,2},{7,3},{8,4},{9,5},{1... | collective-permute-start | bytes 1376264 | tf_op jit(solution)/shard_map/ppermute | solution.py:33
  20.7 18.4 %collective-permute-start.5 = (bf16[64,3584]{1,0:T(8,128)(2,1)S(1)}, bf16[64,3584]{1,0:T(8,128)(2,1)S(1)}, u32[]{:S(2)}, u32[]{:S(2)}) collective-permute-start(bf16[64,3584]{1,0:T(8,128)(2,1)S(1)} %collective-permute-done.1.refs_3_), channel_id=1, source_target_pairs={{0,4},{1,5},{2,6},{3,7},{4,8},{5,9},{6,10},{7,11},{8,12},{9,13},{1... | collective-permute-start | bytes 1376264 | tf_op jit(solution)/shard_map/ppermute | solution.py:33
  29.2 10.0 %collective-permute-start.6 = (bf16[64,3584]{1,0:T(8,128)(2,1)S(1)}, bf16[64,3584]{1,0:T(8,128)(2,1)S(1)}, u32[]{:S(2)}, u32[]{:S(2)}) collective-permute-start(bf16[64,3584]{1,0:T(8,128)(2,1)S(1)} %collective-permute-done.4.refs_6_), channel_id=1, source_target_pairs={{0,12},{1,13},{2,14},{3,15},{4,0},{5,1},{6,2},{7,3},{8,4},{9,5},{1... | collective-permute-start | bytes 1376264 | tf_op jit(solution)/shard_map/ppermute | solution.py:33
  30.5 28.2 %collective-permute-start.12 = (bf16[128,3584]{1,0:T(8,128)(2,1)S(1)}, bf16[128,3584]{1,0:T(8,128)(2,1)S(1)}, u32[]{:S(2)}, u32[]{:S(2)}) collective-permute-start(bf16[128,3584]{1,0:T(8,128)(2,1)S(1)} %collective-permute-done.refs_2_), channel_id=1, source_target_pairs={{0,4},{1,5},{2,6},{3,7},{4,8},{5,9},{6,10},{7,11},{8,12},{9,13},{1... | collective-permute-start | bytes 2752520 | tf_op jit(solution)/shard_map/ppermute | solution.py:33
  30.7 31.7 %collective-permute-start.13 = (bf16[128,3584]{1,0:T(8,128)(2,1)S(1)}, bf16[128,3584]{1,0:T(8,128)(2,1)S(1)}, u32[]{:S(2)}, u32[]{:S(2)}) collective-permute-start(bf16[128,3584]{1,0:T(8,128)(2,1)S(1)} %collective-permute-done.refs_2_), channel_id=1, source_target_pairs={{0,12},{1,13},{2,14},{3,15},{4,0},{5,1},{6,2},{7,3},{8,4},{9,5},{1... | collective-permute-start | bytes 2752520 | tf_op jit(solution)/shard_map/ppermute | solution.py:33
  39.1 19.7 %collective-permute-start.14 = (bf16[64,3584]{1,0:T(8,128)(2,1)S(1)}, bf16[64,3584]{1,0:T(8,128)(2,1)S(1)}, u32[]{:S(2)}, u32[]{:S(2)}) collective-permute-start(bf16[64,3584]{1,0:T(8,128)(2,1)S(1)} %collective-permute-done.5.refs_7_), channel_id=1, source_target_pairs={{0,2},{1,3},{2,0},{3,1},{4,6},{5,7},{6,4},{7,5},{8,10},{9,11},{10,... | collective-permute-start | bytes 1376264 | tf_op jit(solution)/shard_map/ppermute | solution.py:33
  39.3 22.4 %collective-permute-start.15 = (bf16[64,3584]{1,0:T(8,128)(2,1)S(1)}, bf16[64,3584]{1,0:T(8,128)(2,1)S(1)}, u32[]{:S(2)}, u32[]{:S(2)}) collective-permute-start(bf16[64,3584]{1,0:T(8,128)(2,1)S(1)} %collective-permute-done.6.refs_8_), channel_id=1, source_target_pairs={{0,2},{1,3},{2,0},{3,1},{4,6},{5,7},{6,4},{7,5},{8,10},{9,11},{10,... | collective-permute-start | bytes 1376264 | tf_op jit(solution)/shard_map/ppermute | solution.py:33
  58.7 18.3 %collective-permute-start.8 = (bf16[2,128,1024]{2,1,0:T(8,128)(2,1)S(1)}, bf16[2,128,1024]{2,1,0:T(8,128)(2,1)S(1)}, u32[]{:S(2)}, u32[]{:S(2)}) collective-permute-start(bf16[2,128,1024]{2,1,0:T(8,128)(2,1)S(1)} %get-tuple-element.17), channel_id=1, source_target_pairs={{0,2},{1,3},{2,0},{3,1},{4,6},{5,7},{6,4},{7,5},{8,10},{9,11},{10,... | collective-permute-start | bytes 1572872 | tf_op jit(solution)/shard_map/ppermute | solution.py:33
  58.7 22.5 %collective-permute-start.10 = (bf16[2,128,1024]{2,1,0:T(8,128)(2,1)S(1)}, bf16[2,128,1024]{2,1,0:T(8,128)(2,1)S(1)}, u32[]{:S(2)}, u32[]{:S(2)}) collective-permute-start(bf16[2,128,1024]{2,1,0:T(8,128)(2,1)S(1)} %get-tuple-element.19), channel_id=1, source_target_pairs={{0,4},{1,5},{2,6},{3,7},{4,8},{5,9},{6,10},{7,11},{8,12},{9,13},{1... | collective-permute-start | bytes 1572872 | tf_op jit(solution)/shard_map/ppermute | solution.py:33
  58.8 30.7 %collective-permute-start.11 = (bf16[2,128,1024]{2,1,0:T(8,128)(2,1)}, bf16[2,128,1024]{2,1,0:T(8,128)(2,1)}, u32[]{:S(2)}, u32[]{:S(2)}) collective-permute-start(bf16[2,128,1024]{2,1,0:T(8,128)(2,1)} %get-tuple-element.20), channel_id=1, source_target_pairs={{0,8},{1,9},{2,10},{3,11},{4,12},{5,13},{6,14},{7,15},{8,0},{9,1},... | collective-permute-start | bytes 1572872 | tf_op jit(solution)/shard_map/ppermute | solution.py:33
  61.6 24.7 %copy-start.1 = (bf16[1,2,64,3584]{3,2,1,0:T(8,128)(2,1)S(1)}, bf16[1,2,64,3584]{3,2,1,0:T(8,128)(2,1)}, u32[]{:S(2)}) copy-start(bf16[1,2,64,3584]{3,2,1,0:T(8,128)(2,1)} %param.8) | copy-start | bytes 2752516
  61.6 25.0 %copy-start.2 = (s32[1,2,64,8]{2,3,1,0:T(8,128)S(1)}, s32[1,2,64,8]{2,3,1,0:T(8,128)}, u32[]{:S(2)}) copy-start(s32[1,2,64,8]{2,3,1,0:T(8,128)} %param.10) | copy-start | bytes 12292
  61.6 27.9 %collective-permute-start.9 = (bf16[2,128,1024]{2,1,0:T(8,128)(2,1)}, bf16[2,128,1024]{2,1,0:T(8,128)(2,1)}, u32[]{:S(2)}, u32[]{:S(2)}) collective-permute-start(bf16[2,128,1024]{2,1,0:T(8,128)(2,1)} %get-tuple-element.18), channel_id=1, source_target_pairs={{0,12},{1,13},{2,14},{3,15},{4,0},{5,1},{6,2},{7,3},{8,4},{9,5},{1... | collective-permute-start | bytes 1572872 | tf_op jit(solution)/shard_map/ppermute | solution.py:33
  77.1 18.3 %collective-permute-start.18 = (bf16[2,128,1024]{2,1,0:T(8,128)(2,1)}, bf16[2,128,1024]{2,1,0:T(8,128)(2,1)}, u32[]{:S(2)}, u32[]{:S(2)}) collective-permute-start(bf16[2,128,1024]{2,1,0:T(8,128)(2,1)} %get-tuple-element.27), channel_id=1, source_target_pairs={{0,10},{1,11},{2,8},{3,9},{4,14},{5,15},{6,12},{7,13},{8,2},{9,3},... | collective-permute-start | bytes 1572872 | tf_op jit(solution)/shard_map/ppermute | solution.py:33
  81.2 37.1 %collective-permute-start.17 = (bf16[2,128,1024]{2,1,0:T(8,128)(2,1)}, bf16[2,128,1024]{2,1,0:T(8,128)(2,1)}, u32[]{:S(2)}, u32[]{:S(2)}) collective-permute-start(bf16[2,128,1024]{2,1,0:T(8,128)(2,1)} %get-tuple-element.25), channel_id=1, source_target_pairs={{0,6},{1,7},{2,4},{3,5},{4,10},{5,11},{6,8},{7,9},{8,14},{9,15},{1... | collective-permute-start | bytes 1572872 | tf_op jit(solution)/shard_map/ppermute | solution.py:33
  81.2 37.1 %collective-permute-start.16 = (bf16[2,128,1024]{2,1,0:T(8,128)(2,1)}, bf16[2,128,1024]{2,1,0:T(8,128)(2,1)}, u32[]{:S(2)}, u32[]{:S(2)}) collective-permute-start(bf16[2,128,1024]{2,1,0:T(8,128)(2,1)} %get-tuple-element.23), channel_id=1, source_target_pairs={{0,14},{1,15},{2,12},{3,13},{4,2},{5,3},{6,0},{7,1},{8,6},{9,7},{1... | collective-permute-start | bytes 1572872 | tf_op jit(solution)/shard_map/ppermute | solution.py:33
  122.6 4.9 %collective-permute-start.19 = (f32[16,3584]{1,0:T(8,128)S(1)}, f32[16,3584]{1,0:T(8,128)S(1)}, u32[]{:S(2)}, u32[]{:S(2)}) collective-permute-start(f32[16,3584]{1,0:T(8,128)S(1)} %select_bitcast_fusion), channel_id=1, source_target_pairs={{0,1},{1,0},{2,3},{3,2},{4,5},{5,4},{6,7},{7,6},{8,9},{9,8},{10,11... | collective-permute-start | bytes 688136 | tf_op jit(solution)/shard_map/ppermute | solution.py:33
  127.6 5.9 %collective-permute-start.20 = (bf16[16,3584]{1,0:T(8,128)(2,1)S(1)}, bf16[16,3584]{1,0:T(8,128)(2,1)S(1)}, u32[]{:S(2)}, u32[]{:S(2)}) collective-permute-start(bf16[16,3584]{1,0:T(8,128)(2,1)S(1)} %fusion.4), channel_id=1, source_target_pairs={{0,8},{1,9},{2,10},{3,11},{4,12},{5,13},{6,14},{7,15},{8,0},{9,1},... | collective-permute-start | bytes 344072 | tf_op jit(solution)/shard_map/ppermute | solution.py:33
  128.0 8.7 %collective-permute-start.21 = (bf16[16,3584]{1,0:T(8,128)(2,1)S(1)}, bf16[16,3584]{1,0:T(8,128)(2,1)S(1)}, u32[]{:S(2)}, u32[]{:S(2)}) collective-permute-start(bf16[16,3584]{1,0:T(8,128)(2,1)S(1)} %fusion.4), channel_id=1, source_target_pairs={{0,4},{1,5},{2,6},{3,7},{4,8},{5,9},{6,10},{7,11},{8,12},{9,13},{1... | collective-permute-start | bytes 344072 | tf_op jit(solution)/shard_map/ppermute | solution.py:33
  131.4 5.4 %collective-permute-start.22 = (bf16[16,3584]{1,0:T(8,128)(2,1)S(1)}, bf16[16,3584]{1,0:T(8,128)(2,1)S(1)}, u32[]{:S(2)}, u32[]{:S(2)}) collective-permute-start(bf16[16,3584]{1,0:T(8,128)(2,1)S(1)} %fusion.4), channel_id=1, source_target_pairs={{0,12},{1,13},{2,14},{3,15},{4,0},{5,1},{6,2},{7,3},{8,4},{9,5},{1... | collective-permute-start | bytes 344072 | tf_op jit(solution)/shard_map/ppermute | solution.py:33
  136.8 7.7 %collective-permute-start.23 = (bf16[16,3584]{1,0:T(8,128)(2,1)S(1)}, bf16[16,3584]{1,0:T(8,128)(2,1)S(1)}, u32[]{:S(2)}, u32[]{:S(2)}) collective-permute-start(bf16[16,3584]{1,0:T(8,128)(2,1)S(1)} %add_convert_fusion), channel_id=1, source_target_pairs={{0,2},{1,3},{2,0},{3,1},{4,6},{5,7},{6,4},{7,5},{8,10},{9,11},{10,... | collective-permute-start | bytes 344072 | tf_op jit(solution)/shard_map/ppermute | solution.py:33
  137.0 10.6 %collective-permute-start.24 = (bf16[16,3584]{1,0:T(8,128)(2,1)S(1)}, bf16[16,3584]{1,0:T(8,128)(2,1)S(1)}, u32[]{:S(2)}, u32[]{:S(2)}) collective-permute-start(bf16[16,3584]{1,0:T(8,128)(2,1)S(1)} %add_convert_fusion), channel_id=1, source_target_pairs={{0,113},{1,112},{2,115},{3,114},{4,117},{5,116},{6,119},{7,118},{8... | collective-permute-start | bytes 344072 | tf_op jit(solution)/shard_map/ppermute | solution.py:46
  143.1 7.5 %collective-permute-start.25 = (bf16[16,3584]{1,0:T(8,128)(2,1)S(1)}, bf16[16,3584]{1,0:T(8,128)(2,1)S(1)}, u32[]{:S(2)}, u32[]{:S(2)}) collective-permute-start(bf16[16,3584]{1,0:T(8,128)(2,1)S(1)} %add_convert_fusion), channel_id=1, source_target_pairs={{0,115},{1,114},{2,113},{3,112},{4,119},{5,118},{6,117},{7,116},{8... | collective-permute-start | bytes 344072 | tf_op jit(solution)/shard_map/ppermute | solution.py:46
  150.7 1.6 %collective-permute-start.26 = (f32[16,3584]{1,0:T(8,128)S(1)}, f32[16,3584]{1,0:T(8,128)S(1)}, u32[]{:S(2)}, u32[]{:S(2)}) collective-permute-start(f32[16,3584]{1,0:T(8,128)S(1)} %add_add_fusion), channel_id=1, source_target_pairs={{0,1},{1,0},{2,3},{3,2},{4,5},{5,4},{6,7},{7,6},{8,9},{9,8},{10,11... | collective-permute-start | bytes 688136 | tf_op jit(solution)/shard_map/ppermute | solution.py:33

commit v6 on v3

--- a/solution.py
+++ b/solution.py
@@ -211,8 +211,9 @@
         low = (logit - high.astype(jnp.float32)).astype(jnp.bfloat16)
         over = (((0,), (0,)), ((), ()))
         values = inputs[s * half : (s + 1) * half, :]
-        made = lax.dot_general(high, values, over, preferred_element_type=jnp.float32)
-        part[s] = made + lax.dot_general(low, values, over, preferred_element_type=jnp.float32)
+        both = jnp.concatenate([high, low], axis=1)
+        made = lax.dot_general(both, values, over, preferred_element_type=jnp.float32)
+        part[s] = made[:EXPERTS] + made[EXPERTS:]
     for q in range(chunks):
         out_copy(q).wait()
 

time: 153 us -> 153 us (level)
  no operation moved by 1% of the time
where the time goes in v6:
time: 153 us
  waiting for transfers between devices  69.4 us (45%)
  starting transfers between devices  43.5 us (28%)
  Pallas kernels  34 us (22%)
  local copies, waits for them, and re-layouts  4.01 us (3%)
    ppermute x25, waiting for transfers between devices, send(): return lax.ppermute(block, 'expert', shift(dx, dy, dc))  63.3 us
    ppermute x25, starting transfers between devices, send(): return lax.ppermute(block, 'expert', shift(dx, dy, dc))  35.9 us
    pallas_call x2, Pallas kernels, project(): pl.pallas_call(functools.partial(project_kernel, layout, depth_of), in_sp...  29.8 us
    ppermute x2, starting transfers between devices, send_mirror(): return lax.ppermute(block, ('pipe', 'expert'), route)  7.62 us
    ppermute x2, waiting for transfers between devices, send_mirror(): return lax.ppermute(block, ('pipe', 'expert'), route)  6.1 us
    pallas_call x1, Pallas kernels, token_math(): pl.pallas_call(functools.partial(token_kernel, n), in_specs=[inside] * (6...  4.26 us
  transfers between devices with their start and end apart: 27, of which 15 were waited for; matrix products, arithmetic and copies ran while one was open for 3% of the time, Pallas kernels for 19%

profile of v6, /device:TPU:1, one launch (start us, length us, event | category | flops | bytes accessed | tf_op | source)
XLA Modules:
  0.0 153.1 jit_solution(12821186093501529953)
XLA Ops:
  0.6 1.5 collective-permute-start.7
  2.1 3.0 %collective-permute-start = (bf16[128,3584]{1,0:T(8,128)(2,1)}, bf16[128,3584]{1,0:T(8,128)(2,1)S(1)}, u32[]{:S(2)}, u32[]{:S(2)}) collective-permute-start(bf16[128,3584]{1,0:T(8,128)(2,1)} %bitcast.38), channel_id=1, source_target_pairs={{0,2},{1,3},{2,0},{3,1},{4,6},{5,7},{6,4},{7,5},{8,10},{9,11},{10,... | collective-permute-start | bytes 2752520 | tf_op jit(solution)/shard_map/ppermute | solution.py:33
  5.2 1.2 slice_bitcast_fusion.2
  6.4 1.3 collective-permute-start.1
  7.7 1.5 collective-permute-start.4
  9.1 10.3 %collective-permute-done.1.refs_2_ = bf16[64,3584]{1,0:T(8,128)(2,1)S(1)} collective-permute-done((bf16[64,3584]{1,0:T(8,128)(2,1)S(1)}, bf16[64,3584]{1,0:T(8,128)(2,1)S(1)}, u32[]{:S(2)}, u32[]{:S(2)}) %collective-permute-start.1) | collective-permute-done | bytes 458784 | tf_op jit(solution)/shard_map/ppermute | solution.py:33
  19.4 1.3 collective-permute-start.3
  20.9 8.4 %collective-permute-done.2.refs_3_ = bf16[64,3584]{1,0:T(8,128)(2,1)S(1)} collective-permute-done((bf16[64,3584]{1,0:T(8,128)(2,1)S(1)}, bf16[64,3584]{1,0:T(8,128)(2,1)S(1)}, u32[]{:S(2)}, u32[]{:S(2)}) %collective-permute-start.2) | collective-permute-done | bytes 458784 | tf_op jit(solution)/shard_map/ppermute | solution.py:33
  29.2 1.3 collective-permute-start.6
  30.7 2.5 %collective-permute-start.13 = (bf16[128,3584]{1,0:T(8,128)(2,1)S(1)}, bf16[128,3584]{1,0:T(8,128)(2,1)S(1)}, u32[]{:S(2)}, u32[]{:S(2)}) collective-permute-start(bf16[128,3584]{1,0:T(8,128)(2,1)S(1)} %collective-permute-done.refs_1_), channel_id=1, source_target_pairs={{0,12},{1,13},{2,14},{3,15},{4,0},{5,1},{6,2},{7,3},{8,4},{9,5},{1... | collective-permute-start | bytes 2752520 | tf_op jit(solution)/shard_map/ppermute | solution.py:33
  33.2 5.9 %collective-permute-done.5.refs_6_ = bf16[64,3584]{1,0:T(8,128)(2,1)S(1)} collective-permute-done((bf16[64,3584]{1,0:T(8,128)(2,1)S(1)}, bf16[64,3584]{1,0:T(8,128)(2,1)S(1)}, u32[]{:S(2)}, u32[]{:S(2)}) %collective-permute-start.5) | collective-permute-done | bytes 458784 | tf_op jit(solution)/shard_map/ppermute | solution.py:33
  39.3 2.8 %collective-permute-start.15 = (bf16[64,3584]{1,0:T(8,128)(2,1)S(1)}, bf16[64,3584]{1,0:T(8,128)(2,1)S(1)}, u32[]{:S(2)}, u32[]{:S(2)}) collective-permute-start(bf16[64,3584]{1,0:T(8,128)(2,1)S(1)} %collective-permute-done.6.refs_7_), channel_id=1, source_target_pairs={{0,2},{1,3},{2,0},{3,1},{4,6},{5,7},{6,4},{7,5},{8,10},{9,11},{10,... | collective-permute-start | bytes 1376264 | tf_op jit(solution)/shard_map/ppermute | solution.py:33
  42.0 15.1 %shard_map.86 = (bf16[2,128,1024]{2,1,0:T(8,128)(2,1)S(1)}, bf16[2,128,1024]{2,1,0:T(8,128)(2,1)S(1)}, bf16[2,128,1024]{2,1,0:T(8,128)(2,1)}, bf16[2,128,1024]{2,1,0:T(8,128)(2,1)S(1)}, bf16[2,128,1024]{2,1,0:T(8,128)(2,1)}) custom-call(bf16[128,3584]{1,0:T(8,128)(2,1)} %bitcast.39, bf16[128,3584]{1,0:T(8,128)(2,1)} %copy-done.3, ...), custom_call_target="tpu_custom_call" | custom-call | flops 9395240960 | bytes 36569088 | tf_op jit(solution)/shard_map/pallas_call | solution.py:141
  57.2 1.5 %collective-permute-done.12.refs_0_ = bf16[128,3584]{1,0:T(8,128)(2,1)S(1)} collective-permute-done((bf16[128,3584]{1,0:T(8,128)(2,1)S(1)}, bf16[128,3584]{1,0:T(8,128)(2,1)S(1)}, u32[]{:S(2)}, u32[]{:S(2)}) %collective-permute-start.12) | collective-permute-done | bytes 917536 | tf_op jit(solution)/shard_map/ppermute | solution.py:33
  58.8 2.5 %collective-permute-start.11 = (bf16[2,128,1024]{2,1,0:T(8,128)(2,1)}, bf16[2,128,1024]{2,1,0:T(8,128)(2,1)}, u32[]{:S(2)}, u32[]{:S(2)}) collective-permute-start(bf16[2,128,1024]{2,1,0:T(8,128)(2,1)} %get-tuple-element.20), channel_id=1, source_target_pairs={{0,8},{1,9},{2,10},{3,11},{4,12},{5,13},{6,14},{7,15},{8,0},{9,1},... | collective-permute-start | bytes 1572872 | tf_op jit(solution)/shard_map/ppermute | solution.py:33
  61.2 1.2 collective-permute-start.9
  62.4 14.6 %shard_map.87 = (bf16[2,128,1024]{2,1,0:T(8,128)(2,1)}, bf16[2,128,1024]{2,1,0:T(8,128)(2,1)}, bf16[2,128,1024]{2,1,0:T(8,128)(2,1)}) custom-call(bf16[128,3584]{1,0:T(8,128)(2,1)S(1)} %collective-permute-done.12.refs_0_, bf16[128,3584]{1,0:T(8,128)(2,1)S(1)} %collective-permute-done.13.refs_1_, bf16[64,3584]{1,0:T(8,128)(2,1)S(1)} %collective-permute-done.14.refs_2_, ...), custom_call_target="tpu_custom_call" | custom-call | flops 5637144576 | bytes 33685504 | tf_op jit(solution)/shard_map/pallas_call | solution.py:141
  77.0 4.1 %collective-permute-start.18 = (bf16[2,128,1024]{2,1,0:T(8,128)(2,1)}, bf16[2,128,1024]{2,1,0:T(8,128)(2,1)}, u32[]{:S(2)}, u32[]{:S(2)}) collective-permute-start(bf16[2,128,1024]{2,1,0:T(8,128)(2,1)} %get-tuple-element.27), channel_id=1, source_target_pairs={{0,10},{1,11},{2,8},{3,9},{4,14},{5,15},{6,12},{7,13},{8,2},{9,3},... | collective-permute-start | bytes 1572872 | tf_op jit(solution)/shard_map/ppermute | solution.py:33
  81.2 5.1 %collective-permute-start.16 = (bf16[2,128,1024]{2,1,0:T(8,128)(2,1)}, bf16[2,128,1024]{2,1,0:T(8,128)(2,1)}, u32[]{:S(2)}, u32[]{:S(2)}) collective-permute-start(bf16[2,128,1024]{2,1,0:T(8,128)(2,1)} %get-tuple-element.23), channel_id=1, source_target_pairs={{0,14},{1,15},{2,12},{3,13},{4,2},{5,3},{6,0},{7,1},{8,6},{9,7},{1... | collective-permute-start | bytes 1572872 | tf_op jit(solution)/shard_map/ppermute | solution.py:33
  87.7 1.7 %slice_bitcast_fusion = (bf16[512,1024]{1,0:T(8,128)(2,1)S(1)}, bf16[512,1024]{1,0:T(8,128)(2,1)S(1)}) fusion(bf16[1,2,64,8,1024]{4,3,2,1,0:T(8,128)(2,1)} %param.9), kind=kLoop, calls=%fused_computation.4 | loop fusion | bytes 4194304 | tf_op jit(solution)/shard_map/reshape;squeeze | solution.py:316
  89.5 6.0 %collective-permute-done.18.refs_9_ = bf16[2,128,1024]{2,1,0:T(8,128)(2,1)} collective-permute-done((bf16[2,128,1024]{2,1,0:T(8,128)(2,1)}, bf16[2,128,1024]{2,1,0:T(8,128)(2,1)}, u32[]{:S(2)}, u32[]{:S(2)}) %collective-permute-start.18) | collective-permute-done | bytes 524320 | tf_op jit(solution)/shard_map/ppermute | solution.py:33
  95.4 22.4 %collective-permute-done.17.refs_8_ = bf16[2,128,1024]{2,1,0:T(8,128)(2,1)} collective-permute-done((bf16[2,128,1024]{2,1,0:T(8,128)(2,1)}, bf16[2,128,1024]{2,1,0:T(8,128)(2,1)}, u32[]{:S(2)}, u32[]{:S(2)}) %collective-permute-start.17) | collective-permute-done | bytes 524320 | tf_op jit(solution)/shard_map/ppermute | solution.py:33
  118.9 4.3 %shard_map.88 = (bf16[1024,1024]{1,0:T(8,128)(2,1)}, f32[2,16,3584]{2,1,0:T(8,128)S(1)}) custom-call(s32[1,256]{1,0:T(1,128)S(1)} %constant_dynamic-slice_fusion.source, s32[1024,1]{1,0:T(8,128)S(1)} %reshape.32.ids, f32[128,16]{1,0:T(8,128)S(1)} %bitcast.34, bf16[128,3584]{1,0:T(8,128)(2,1)S(1)} %bitcast.33, ...), custom_call_target="tpu_custom_call" | custom-call | flops 536870912 | bytes 8388608 | tf_op jit(solution)/shard_map/pallas_call | solution.py:228
  123.2 3.2 %collective-permute-start.19 = (f32[16,3584]{1,0:T(8,128)S(1)}, f32[16,3584]{1,0:T(8,128)S(1)}, u32[]{:S(2)}, u32[]{:S(2)}) collective-permute-start(f32[16,3584]{1,0:T(8,128)S(1)} %select_bitcast_fusion.2), channel_id=1, source_target_pairs={{0,1},{1,0},{2,3},{3,2},{4,5},{5,4},{6,7},{7,6},{8,9},{9,8},{10,11... | collective-permute-start | bytes 688136 | tf_op jit(solution)/shard_map/ppermute | solution.py:33
  128.0 3.4 %collective-permute-start.21 = (bf16[16,3584]{1,0:T(8,128)(2,1)S(1)}, bf16[16,3584]{1,0:T(8,128)(2,1)S(1)}, u32[]{:S(2)}, u32[]{:S(2)}) collective-permute-start(bf16[16,3584]{1,0:T(8,128)(2,1)S(1)} %fusion.4), channel_id=1, source_target_pairs={{0,4},{1,5},{2,6},{3,7},{4,8},{5,9},{6,10},{7,11},{8,12},{9,13},{1... | collective-permute-start | bytes 344072 | tf_op jit(solution)/shard_map/ppermute | solution.py:33
  131.7 1.8 %collective-permute-done.20 = bf16[16,3584]{1,0:T(8,128)(2,1)S(1)} collective-permute-done((bf16[16,3584]{1,0:T(8,128)(2,1)S(1)}, bf16[16,3584]{1,0:T(8,128)(2,1)S(1)}, u32[]{:S(2)}, u32[]{:S(2)}) %collective-permute-start.20) | collective-permute-done | bytes 114720 | tf_op jit(solution)/shard_map/ppermute | solution.py:33
  133.5 3.2 %collective-permute-done.21 = bf16[16,3584]{1,0:T(8,128)(2,1)S(1)} collective-permute-done((bf16[16,3584]{1,0:T(8,128)(2,1)S(1)}, bf16[16,3584]{1,0:T(8,128)(2,1)S(1)}, u32[]{:S(2)}, u32[]{:S(2)}) %collective-permute-start.21) | collective-permute-done | bytes 114720 | tf_op jit(solution)/shard_map/ppermute | solution.py:33
  136.9 6.2 %collective-permute-start.24 = (bf16[16,3584]{1,0:T(8,128)(2,1)S(1)}, bf16[16,3584]{1,0:T(8,128)(2,1)S(1)}, u32[]{:S(2)}, u32[]{:S(2)}) collective-permute-start(bf16[16,3584]{1,0:T(8,128)(2,1)S(1)} %add_convert_fusion), channel_id=1, source_target_pairs={{0,113},{1,112},{2,115},{3,114},{4,117},{5,116},{6,119},{7,118},{8... | collective-permute-start | bytes 344072 | tf_op jit(solution)/shard_map/ppermute | solution.py:46
  143.1 1.4 collective-permute-start.25
  144.5 3.1 %collective-permute-done.24 = bf16[16,3584]{1,0:T(8,128)(2,1)S(1)} collective-permute-done((bf16[16,3584]{1,0:T(8,128)(2,1)S(1)}, bf16[16,3584]{1,0:T(8,128)(2,1)S(1)}, u32[]{:S(2)}, u32[]{:S(2)}) %collective-permute-start.24) | collective-permute-done | bytes 114720 | tf_op jit(solution)/shard_map/ppermute | solution.py:46
  147.6 3.0 %collective-permute-done.25 = bf16[16,3584]{1,0:T(8,128)(2,1)S(1)} collective-permute-done((bf16[16,3584]{1,0:T(8,128)(2,1)S(1)}, bf16[16,3584]{1,0:T(8,128)(2,1)S(1)}, u32[]{:S(2)}, u32[]{:S(2)}) %collective-permute-start.25) | collective-permute-done | bytes 114720 | tf_op jit(solution)/shard_map/ppermute | solution.py:46
  150.8 1.5 collective-permute-done.26
  (46 shorter events, 6.3 us)
Async XLA Ops:
  0.6 85.6 %copy-start = (bf16[1,2,16,3584]{3,2,1,0:T(8,128)(2,1)S(1)}, bf16[1,2,16,3584]{3,2,1,0:T(8,128)(2,1)}, u32[]{:S(2)}) copy-start(bf16[1,2,16,3584]{3,2,1,0:T(8,128)(2,1)} %param.12) | copy-start | bytes 688132
  0.6 41.4 %collective-permute-start.7 = (bf16[2,1024,3584]{2,1,0:T(8,128)(2,1)}, bf16[2,1024,3584]{2,1,0:T(8,128)(2,1)}, u32[]{:S(2)}, u32[]{:S(2)}) collective-permute-start(bf16[2,1024,3584]{2,1,0:T(8,128)(2,1)} %bitcast.35), channel_id=1, source_target_pairs={{0,1},{1,0},{2,3},{3,2},{4,5},{5,4},{6,7},{7,6},{8,9},{9,8},{10,11... | collective-permute-start | bytes 44040200 | tf_op jit(solution)/shard_map/ppermute | solution.py:33
  2.1 28.4 %collective-permute-start = (bf16[128,3584]{1,0:T(8,128)(2,1)}, bf16[128,3584]{1,0:T(8,128)(2,1)S(1)}, u32[]{:S(2)}, u32[]{:S(2)}) collective-permute-start(bf16[128,3584]{1,0:T(8,128)(2,1)} %bitcast.38), channel_id=1, source_target_pairs={{0,2},{1,3},{2,0},{3,1},{4,6},{5,7},{6,4},{7,5},{8,10},{9,11},{10,... | collective-permute-start | bytes 2752520 | tf_op jit(solution)/shard_map/ppermute | solution.py:33
  6.4 13.0 %collective-permute-start.1 = (bf16[64,3584]{1,0:T(8,128)(2,1)S(1)}, bf16[64,3584]{1,0:T(8,128)(2,1)S(1)}, u32[]{:S(2)}, u32[]{:S(2)}) collective-permute-start(bf16[64,3584]{1,0:T(8,128)(2,1)S(1)} %get-tuple-element.33), channel_id=1, source_target_pairs={{0,4},{1,5},{2,6},{3,7},{4,8},{5,9},{6,10},{7,11},{8,12},{9,13},{1... | collective-permute-start | bytes 1376264 | tf_op jit(solution)/shard_map/ppermute | solution.py:33
  7.7 13.0 %collective-permute-start.4 = (bf16[64,3584]{1,0:T(8,128)(2,1)S(1)}, bf16[64,3584]{1,0:T(8,128)(2,1)S(1)}, u32[]{:S(2)}, u32[]{:S(2)}) collective-permute-start(bf16[64,3584]{1,0:T(8,128)(2,1)S(1)} %get-tuple-element.32), channel_id=1, source_target_pairs={{0,12},{1,13},{2,14},{3,15},{4,0},{5,1},{6,2},{7,3},{8,4},{9,5},{1... | collective-permute-start | bytes 1376264 | tf_op jit(solution)/shard_map/ppermute | solution.py:33
  9.1 20.1 %collective-permute-start.2 = (bf16[64,3584]{1,0:T(8,128)(2,1)S(1)}, bf16[64,3584]{1,0:T(8,128)(2,1)S(1)}, u32[]{:S(2)}, u32[]{:S(2)}) collective-permute-start(bf16[64,3584]{1,0:T(8,128)(2,1)S(1)} %get-tuple-element.32), channel_id=1, source_target_pairs={{0,4},{1,5},{2,6},{3,7},{4,8},{5,9},{6,10},{7,11},{8,12},{9,13},{1... | collective-permute-start | bytes 1376264 | tf_op jit(solution)/shard_map/ppermute | solution.py:33
  19.4 11.3 %collective-permute-start.3 = (bf16[64,3584]{1,0:T(8,128)(2,1)S(1)}, bf16[64,3584]{1,0:T(8,128)(2,1)S(1)}, u32[]{:S(2)}, u32[]{:S(2)}) collective-permute-start(bf16[64,3584]{1,0:T(8,128)(2,1)S(1)} %get-tuple-element.33), channel_id=1, source_target_pairs={{0,12},{1,13},{2,14},{3,15},{4,0},{5,1},{6,2},{7,3},{8,4},{9,5},{1... | collective-permute-start | bytes 1376264 | tf_op jit(solution)/shard_map/ppermute | solution.py:33
  20.7 18.4 %collective-permute-start.5 = (bf16[64,3584]{1,0:T(8,128)(2,1)S(1)}, bf16[64,3584]{1,0:T(8,128)(2,1)S(1)}, u32[]{:S(2)}, u32[]{:S(2)}) collective-permute-start(bf16[64,3584]{1,0:T(8,128)(2,1)S(1)} %collective-permute-done.1.refs_2_), channel_id=1, source_target_pairs={{0,4},{1,5},{2,6},{3,7},{4,8},{5,9},{6,10},{7,11},{8,12},{9,13},{1... | collective-permute-start | bytes 1376264 | tf_op jit(solution)/shard_map/ppermute | solution.py:33
  29.2 10.0 %collective-permute-start.6 = (bf16[64,3584]{1,0:T(8,128)(2,1)S(1)}, bf16[64,3584]{1,0:T(8,128)(2,1)S(1)}, u32[]{:S(2)}, u32[]{:S(2)}) collective-permute-start(bf16[64,3584]{1,0:T(8,128)(2,1)S(1)} %collective-permute-done.4.refs_5_), channel_id=1, source_target_pairs={{0,12},{1,13},{2,14},{3,15},{4,0},{5,1},{6,2},{7,3},{8,4},{9,5},{1... | collective-permute-start | bytes 1376264 | tf_op jit(solution)/shard_map/ppermute | solution.py:33
  30.5 11.5 %copy-start.3 = (bf16[128,3584]{1,0:T(8,128)(2,1)}, bf16[128,3584]{1,0:T(8,128)(2,1)S(1)}, u32[]{:S(2)}) copy-start(bf16[128,3584]{1,0:T(8,128)(2,1)S(1)} %collective-permute-done.refs_1_) | copy-start | bytes 2752516
  30.5 28.2 %collective-permute-start.12 = (bf16[128,3584]{1,0:T(8,128)(2,1)S(1)}, bf16[128,3584]{1,0:T(8,128)(2,1)S(1)}, u32[]{:S(2)}, u32[]{:S(2)}) collective-permute-start(bf16[128,3584]{1,0:T(8,128)(2,1)S(1)} %collective-permute-done.refs_1_), channel_id=1, source_target_pairs={{0,4},{1,5},{2,6},{3,7},{4,8},{5,9},{6,10},{7,11},{8,12},{9,13},{1... | collective-permute-start | bytes 2752520 | tf_op jit(solution)/shard_map/ppermute | solution.py:33
  30.7 31.7 %collective-permute-start.13 = (bf16[128,3584]{1,0:T(8,128)(2,1)S(1)}, bf16[128,3584]{1,0:T(8,128)(2,1)S(1)}, u32[]{:S(2)}, u32[]{:S(2)}) collective-permute-start(bf16[128,3584]{1,0:T(8,128)(2,1)S(1)} %collective-permute-done.refs_1_), channel_id=1, source_target_pairs={{0,12},{1,13},{2,14},{3,15},{4,0},{5,1},{6,2},{7,3},{8,4},{9,5},{1... | collective-permute-start | bytes 2752520 | tf_op jit(solution)/shard_map/ppermute | solution.py:33
  39.1 19.7 %collective-permute-start.14 = (bf16[64,3584]{1,0:T(8,128)(2,1)S(1)}, bf16[64,3584]{1,0:T(8,128)(2,1)S(1)}, u32[]{:S(2)}, u32[]{:S(2)}) collective-permute-start(bf16[64,3584]{1,0:T(8,128)(2,1)S(1)} %collective-permute-done.5.refs_6_), channel_id=1, source_target_pairs={{0,2},{1,3},{2,0},{3,1},{4,6},{5,7},{6,4},{7,5},{8,10},{9,11},{10,... | collective-permute-start | bytes 1376264 | tf_op jit(solution)/shard_map/ppermute | solution.py:33
  39.3 22.0 %collective-permute-start.15 = (bf16[64,3584]{1,0:T(8,128)(2,1)S(1)}, bf16[64,3584]{1,0:T(8,128)(2,1)S(1)}, u32[]{:S(2)}, u32[]{:S(2)}) collective-permute-start(bf16[64,3584]{1,0:T(8,128)(2,1)S(1)} %collective-permute-done.6.refs_7_), channel_id=1, source_target_pairs={{0,2},{1,3},{2,0},{3,1},{4,6},{5,7},{6,4},{7,5},{8,10},{9,11},{10,... | collective-permute-start | bytes 1376264 | tf_op jit(solution)/shard_map/ppermute | solution.py:33
  58.7 18.3 %collective-permute-start.8 = (bf16[2,128,1024]{2,1,0:T(8,128)(2,1)S(1)}, bf16[2,128,1024]{2,1,0:T(8,128)(2,1)S(1)}, u32[]{:S(2)}, u32[]{:S(2)}) collective-permute-start(bf16[2,128,1024]{2,1,0:T(8,128)(2,1)S(1)} %get-tuple-element.17), channel_id=1, source_target_pairs={{0,2},{1,3},{2,0},{3,1},{4,6},{5,7},{6,4},{7,5},{8,10},{9,11},{10,... | collective-permute-start | bytes 1572872 | tf_op jit(solution)/shard_map/ppermute | solution.py:33
  58.7 22.5 %collective-permute-start.10 = (bf16[2,128,1024]{2,1,0:T(8,128)(2,1)S(1)}, bf16[2,128,1024]{2,1,0:T(8,128)(2,1)S(1)}, u32[]{:S(2)}, u32[]{:S(2)}) collective-permute-start(bf16[2,128,1024]{2,1,0:T(8,128)(2,1)S(1)} %get-tuple-element.19), channel_id=1, source_target_pairs={{0,4},{1,5},{2,6},{3,7},{4,8},{5,9},{6,10},{7,11},{8,12},{9,13},{1... | collective-permute-start | bytes 1572872 | tf_op jit(solution)/shard_map/ppermute | solution.py:33
  58.8 30.7 %collective-permute-start.11 = (bf16[2,128,1024]{2,1,0:T(8,128)(2,1)}, bf16[2,128,1024]{2,1,0:T(8,128)(2,1)}, u32[]{:S(2)}, u32[]{:S(2)}) collective-permute-start(bf16[2,128,1024]{2,1,0:T(8,128)(2,1)} %get-tuple-element.20), channel_id=1, source_target_pairs={{0,8},{1,9},{2,10},{3,11},{4,12},{5,13},{6,14},{7,15},{8,0},{9,1},... | collective-permute-start | bytes 1572872 | tf_op jit(solution)/shard_map/ppermute | solution.py:33
  61.2 25.0 %copy-start.1 = (bf16[1,2,64,3584]{3,2,1,0:T(8,128)(2,1)S(1)}, bf16[1,2,64,3584]{3,2,1,0:T(8,128)(2,1)}, u32[]{:S(2)}) copy-start(bf16[1,2,64,3584]{3,2,1,0:T(8,128)(2,1)} %param.8) | copy-start | bytes 2752516
  61.2 25.4 %copy-start.2 = (s32[1,2,64,8]{2,3,1,0:T(8,128)S(1)}, s32[1,2,64,8]{2,3,1,0:T(8,128)}, u32[]{:S(2)}) copy-start(s32[1,2,64,8]{2,3,1,0:T(8,128)} %param.10) | copy-start | bytes 12292
  61.2 28.2 %collective-permute-start.9 = (bf16[2,128,1024]{2,1,0:T(8,128)(2,1)}, bf16[2,128,1024]{2,1,0:T(8,128)(2,1)}, u32[]{:S(2)}, u32[]{:S(2)}) collective-permute-start(bf16[2,128,1024]{2,1,0:T(8,128)(2,1)} %get-tuple-element.18), channel_id=1, source_target_pairs={{0,12},{1,13},{2,14},{3,15},{4,0},{5,1},{6,2},{7,3},{8,4},{9,5},{1... | collective-permute-start | bytes 1572872 | tf_op jit(solution)/shard_map/ppermute | solution.py:33
  77.0 18.4 %collective-permute-start.18 = (bf16[2,128,1024]{2,1,0:T(8,128)(2,1)}, bf16[2,128,1024]{2,1,0:T(8,128)(2,1)}, u32[]{:S(2)}, u32[]{:S(2)}) collective-permute-start(bf16[2,128,1024]{2,1,0:T(8,128)(2,1)} %get-tuple-element.27), channel_id=1, source_target_pairs={{0,10},{1,11},{2,8},{3,9},{4,14},{5,15},{6,12},{7,13},{8,2},{9,3},... | collective-permute-start | bytes 1572872 | tf_op jit(solution)/shard_map/ppermute | solution.py:33
  81.2 36.7 %collective-permute-start.17 = (bf16[2,128,1024]{2,1,0:T(8,128)(2,1)}, bf16[2,128,1024]{2,1,0:T(8,128)(2,1)}, u32[]{:S(2)}, u32[]{:S(2)}) collective-permute-start(bf16[2,128,1024]{2,1,0:T(8,128)(2,1)} %get-tuple-element.25), channel_id=1, source_target_pairs={{0,6},{1,7},{2,4},{3,5},{4,10},{5,11},{6,8},{7,9},{8,14},{9,15},{1... | collective-permute-start | bytes 1572872 | tf_op jit(solution)/shard_map/ppermute | solution.py:33
  81.2 37.7 %collective-permute-start.16 = (bf16[2,128,1024]{2,1,0:T(8,128)(2,1)}, bf16[2,128,1024]{2,1,0:T(8,128)(2,1)}, u32[]{:S(2)}, u32[]{:S(2)}) collective-permute-start(bf16[2,128,1024]{2,1,0:T(8,128)(2,1)} %get-tuple-element.23), channel_id=1, source_target_pairs={{0,14},{1,15},{2,12},{3,13},{4,2},{5,3},{6,0},{7,1},{8,6},{9,7},{1... | collective-permute-start | bytes 1572872 | tf_op jit(solution)/shard_map/ppermute | solution.py:33
  123.2 4.3 %collective-permute-start.19 = (f32[16,3584]{1,0:T(8,128)S(1)}, f32[16,3584]{1,0:T(8,128)S(1)}, u32[]{:S(2)}, u32[]{:S(2)}) collective-permute-start(f32[16,3584]{1,0:T(8,128)S(1)} %select_bitcast_fusion.2), channel_id=1, source_target_pairs={{0,1},{1,0},{2,3},{3,2},{4,5},{5,4},{6,7},{7,6},{8,9},{9,8},{10,11... | collective-permute-start | bytes 688136 | tf_op jit(solution)/shard_map/ppermute | solution.py:33
  127.6 5.9 %collective-permute-start.20 = (bf16[16,3584]{1,0:T(8,128)(2,1)S(1)}, bf16[16,3584]{1,0:T(8,128)(2,1)S(1)}, u32[]{:S(2)}, u32[]{:S(2)}) collective-permute-start(bf16[16,3584]{1,0:T(8,128)(2,1)S(1)} %fusion.4), channel_id=1, source_target_pairs={{0,8},{1,9},{2,10},{3,11},{4,12},{5,13},{6,14},{7,15},{8,0},{9,1},... | collective-permute-start | bytes 344072 | tf_op jit(solution)/shard_map/ppermute | solution.py:33
  128.0 8.7 %collective-permute-start.21 = (bf16[16,3584]{1,0:T(8,128)(2,1)S(1)}, bf16[16,3584]{1,0:T(8,128)(2,1)S(1)}, u32[]{:S(2)}, u32[]{:S(2)}) collective-permute-start(bf16[16,3584]{1,0:T(8,128)(2,1)S(1)} %fusion.4), channel_id=1, source_target_pairs={{0,4},{1,5},{2,6},{3,7},{4,8},{5,9},{6,10},{7,11},{8,12},{9,13},{1... | collective-permute-start | bytes 344072 | tf_op jit(solution)/shard_map/ppermute | solution.py:33
  131.4 5.4 %collective-permute-start.22 = (bf16[16,3584]{1,0:T(8,128)(2,1)S(1)}, bf16[16,3584]{1,0:T(8,128)(2,1)S(1)}, u32[]{:S(2)}, u32[]{:S(2)}) collective-permute-start(bf16[16,3584]{1,0:T(8,128)(2,1)S(1)} %fusion.4), channel_id=1, source_target_pairs={{0,12},{1,13},{2,14},{3,15},{4,0},{5,1},{6,2},{7,3},{8,4},{9,5},{1... | collective-permute-start | bytes 344072 | tf_op jit(solution)/shard_map/ppermute | solution.py:33
  136.8 7.7 %collective-permute-start.23 = (bf16[16,3584]{1,0:T(8,128)(2,1)S(1)}, bf16[16,3584]{1,0:T(8,128)(2,1)S(1)}, u32[]{:S(2)}, u32[]{:S(2)}) collective-permute-start(bf16[16,3584]{1,0:T(8,128)(2,1)S(1)} %add_convert_fusion), channel_id=1, source_target_pairs={{0,2},{1,3},{2,0},{3,1},{4,6},{5,7},{6,4},{7,5},{8,10},{9,11},{10,... | collective-permute-start | bytes 344072 | tf_op jit(solution)/shard_map/ppermute | solution.py:33
  136.9 10.7 %collective-permute-start.24 = (bf16[16,3584]{1,0:T(8,128)(2,1)S(1)}, bf16[16,3584]{1,0:T(8,128)(2,1)S(1)}, u32[]{:S(2)}, u32[]{:S(2)}) collective-permute-start(bf16[16,3584]{1,0:T(8,128)(2,1)S(1)} %add_convert_fusion), channel_id=1, source_target_pairs={{0,113},{1,112},{2,115},{3,114},{4,117},{5,116},{6,119},{7,118},{8... | collective-permute-start | bytes 344072 | tf_op jit(solution)/shard_map/ppermute | solution.py:46
  143.1 7.5 %collective-permute-start.25 = (bf16[16,3584]{1,0:T(8,128)(2,1)S(1)}, bf16[16,3584]{1,0:T(8,128)(2,1)S(1)}, u32[]{:S(2)}, u32[]{:S(2)}) collective-permute-start(bf16[16,3584]{1,0:T(8,128)(2,1)S(1)} %add_convert_fusion), channel_id=1, source_target_pairs={{0,115},{1,114},{2,113},{3,112},{4,119},{5,118},{6,117},{7,116},{8... | collective-permute-start | bytes 344072 | tf_op jit(solution)/shard_map/ppermute | solution.py:46
  150.7 1.6 %collective-permute-start.26 = (f32[16,3584]{1,0:T(8,128)S(1)}, f32[16,3584]{1,0:T(8,128)S(1)}, u32[]{:S(2)}, u32[]{:S(2)}) collective-permute-start(f32[16,3584]{1,0:T(8,128)S(1)} %add_add_fusion), channel_id=1, source_target_pairs={{0,1},{1,0},{2,3},{3,2},{4,5},{5,4},{6,7},{7,6},{8,9},{9,8},{10,11... | collective-permute-start | bytes 688136 | tf_op jit(solution)/shard_map/ppermute | solution.py:33
